TPU v7x, 128 devices: a whole 4x4x4 slice. The times are simulated.
128 devices in a mesh: grp: 8 (over x, core), sp: 16 (over z, y).
Axes of the slice: x: 4, y: 4, z: 4, core: 2. Of those that a mesh axis runs over, the one named last changes fastest.
Arguments:
- qkv: bfloat16 [64, 1024, 3, 2048], P('grp', 'sp'), may hold values from -6 to 6
- tokens: bfloat16 [64, 1024, 3072], P('grp', 'sp'), may hold values from -3 to 3
- lengths: int32 [64], replicated, may hold values from 1 to 1024, as said below
- t_index: int32 [64], replicated, may hold values from 0 to 49
- slot_target: int32 [64], replicated, may hold values from 0 to 63, as said below
- gate_table: float32 [50, 3072], replicated, may hold values from -12 to 12
- q_gain: float32 [128], replicated, may hold values from 0.1 to 1.9
- k_gain: float32 [128], replicated, may hold values from 0.1 to 1.9
- out_weight: bfloat16 [2048, 3072], replicated, may hold values from -0.5 to 0.5
Outputs:
- mixed: bfloat16 [64, 1024, 3072], P('grp', 'sp')
Inputs may be any that keep to these rules, and one draw needn't show every extreme that they name: Token positions from lengths[c] on are padding of clip c; some clip has exactly 1024 live tokens. `slot_target`: A permutation of the 64 clip slots; slots g * 8 to (g + 1) * 8 - 1 belong to group g, and clips g * 8 to (g + 1) * 8 - 1 start in group g. Every group sends exactly 1 of its clips to each group, itself included.
All inputs are finite; a program needn't handle non-finite values.
Results may differ from a plain program's by a relative error of at most 0.0065.
Values may be sent and summed in bfloat16 or wider, within the bound.
No kernel may reach another device: no remote copies, remote signals or barrier semaphores. Data moves between devices by JAX's collectives and lax.ppermute only.
A program may use at most 128 MiB of HBM per device.

v0:
```python
import jax
import jax.numpy as jnp
from jax import lax
from jax.sharding import PartitionSpec as P

HEADS = 16
HD = 128


def as_sent(array):
    return jax.tree.map(lambda a: a.astype(jnp.bfloat16) if a.dtype == jnp.float32 else a, array)


def rms_scale(part, gain):
    wide = part.astype(jnp.float32)
    normed = wide * lax.rsqrt(jnp.mean(wide * wide, axis=-1, keepdims=True) + 1e-06) * gain
    return normed.astype(jnp.bfloat16)


def normalize(block, q_gain, k_gain):
    return jnp.stack(
        [
            rms_scale(block[..., 0, :, :], q_gain),
            rms_scale(block[..., 1, :, :], k_gain),
            block[..., 2, :, :],
        ],
        axis=-3,
    )


def clip_attention(item):
    block, length = item
    seq_total, local_heads, head_size = (block.shape[0], block.shape[2], block.shape[3])
    tile = min(512, seq_total)
    count = seq_total // tile
    queries = block[:, 0]
    key_rows = block[:, 1]
    value_rows = block[:, 2]
    scale = head_size ** (-0.5)
    outputs = []
    for query_block in range(count):
        query_part = queries[query_block * tile : (query_block + 1) * tile]

        def live_query(unused, query_part=query_part):
            raised_parts = []
            for key_block in range(count):
                key_part = key_rows[key_block * tile : (key_block + 1) * tile]

                def live_key(inner, key_part=key_part, key_block=key_block):
                    scores = (
                        jnp.einsum(
                            "qhd,khd->hqk", query_part, key_part, preferred_element_type=jnp.float32
                        )
                        * scale
                    )
                    key_live = key_block * tile + jnp.arange(tile, dtype=jnp.int32) < length
                    return jnp.where(key_live[None, None, :], jnp.exp(scores), jnp.float32(0.0))

                def dead_key(inner):
                    return jnp.zeros((local_heads, tile, tile), jnp.float32)

                raised_parts.append(lax.cond(key_block * tile < length, live_key, dead_key, None))
            raised = jnp.concatenate(raised_parts, axis=2)
            weights = (raised / jnp.sum(raised, axis=-1, keepdims=True)).astype(jnp.bfloat16)
            total = jnp.zeros((tile, local_heads, head_size), jnp.float32)
            for key_block in range(count):
                value_part = value_rows[key_block * tile : (key_block + 1) * tile]
                weight_part = weights[:, :, key_block * tile : (key_block + 1) * tile]

                def live_value(inner, value_part=value_part, weight_part=weight_part):
                    return jnp.einsum(
                        "hqk,khd->qhd", weight_part, value_part, preferred_element_type=jnp.float32
                    )

                def dead_value(inner):
                    return jnp.zeros((tile, local_heads, head_size), jnp.float32)

                total = total + lax.cond(key_block * tile < length, live_value, dead_value, None)
            return total

        def dead_query(unused):
            return jnp.zeros((tile, local_heads, head_size), jnp.float32)

        summed = lax.cond(query_block * tile < length, live_query, dead_query, None)
        query_live = query_block * tile + jnp.arange(tile, dtype=jnp.int32) < length
        outputs.append(
            jnp.where(query_live[:, None, None], summed, jnp.float32(0.0)).astype(jnp.bfloat16)
        )
    return jnp.concatenate(outputs, axis=0)


def attend(block, clip_len):
    head_block = lax.all_to_all(block, "sp", split_axis=3, concat_axis=1, tiled=True)
    attended = lax.map(clip_attention, (head_block, clip_len))
    return jax.tree.map(
        lambda part, own: part.astype(own.dtype),
        lax.all_to_all(as_sent(attended), "sp", split_axis=1, concat_axis=2, tiled=True),
        attended,
    )


def finish(block, resid, clip_ids, lengths, t_index, gate_table, out_weight):
    clip_count, slot_rows = (block.shape[0], block.shape[1])
    clip_len = jnp.take(lengths, clip_ids)
    step_of = jnp.take(t_index, clip_ids)
    attended = attend(block, clip_len)
    projected = jnp.dot(
        attended.reshape(clip_count * slot_rows, HEADS * HD),
        out_weight,
        preferred_element_type=jnp.float32,
    )
    projected = projected.reshape(clip_count, slot_rows, out_weight.shape[1])
    onehot = (step_of[:, None] == jnp.arange(gate_table.shape[0], dtype=jnp.int32)[None, :]).astype(
        jnp.float32
    )
    gate_rows = jnp.dot(onehot, gate_table, precision=lax.Precision.HIGHEST)
    return (resid.astype(jnp.float32) + gate_rows[:, None, :] * projected).astype(jnp.bfloat16)


def per_device(qkv, tokens, lengths, t_index, slot_target, gate_table, q_gain, k_gain, out_weight):
    clip_count, slot_rows = (qkv.shape[0], qkv.shape[1])
    group_count = lax.axis_size("grp")
    per_peer = clip_count // group_count
    group_index = lax.axis_index("grp")
    all_clips = slot_target.shape[0]
    shaped = qkv.reshape(clip_count, slot_rows, 3, HEADS, HD)
    shaped = normalize(shaped, q_gain, k_gain)
    destination = (slot_target // clip_count).reshape(group_count, clip_count)
    same_dest = destination[:, :, None] == destination[:, None, :]
    positions = jnp.arange(clip_count, dtype=jnp.int32)
    earlier = positions[None, :] < positions[:, None]
    order_rank = jnp.sum(jnp.where(same_dest & earlier[None], 1, 0), axis=2).astype(jnp.int32)
    send_slot = jnp.take(destination, group_index, axis=0) * per_peer + jnp.take(
        order_rank, group_index, axis=0
    )
    send_order = jnp.sum(
        jnp.where(send_slot[None, :] == positions[:, None], positions[None, :], 0), axis=1
    )
    incoming = group_index * clip_count + positions
    clip_numbers = jnp.arange(all_clips, dtype=jnp.int32)
    clip_of = jnp.sum(
        jnp.where(slot_target[None, :] == incoming[:, None], clip_numbers[None, :], 0), axis=1
    )
    recv_pos = clip_of // clip_count * per_peer + jnp.take(order_rank.reshape(-1), clip_of)
    arrived_qkv, arrived_rows = (
        lax.all_to_all(
            jnp.take(shaped, send_order, axis=0), "grp", split_axis=0, concat_axis=0, tiled=True
        ),
        lax.all_to_all(
            jnp.take(tokens, send_order, axis=0), "grp", split_axis=0, concat_axis=0, tiled=True
        ),
    )
    local_qkv = jnp.take(arrived_qkv, recv_pos, axis=0)
    local_rows = jnp.take(arrived_rows, recv_pos, axis=0)
    return finish(local_qkv, local_rows, clip_of, lengths, t_index, gate_table, out_weight)


def solution(mesh):
    return jax.shard_map(
        per_device,
        mesh=mesh,
        in_specs=(
            P("grp", "sp", None, None),
            P("grp", "sp", None),
            P(),
            P(),
            P(),
            P(),
            P(),
            P(),
            P(),
        ),
        out_specs=P("grp", "sp", None),
        check_vma=False,
    )
```

profile of v0, /device:TPU:0, one launch (start us, length us, event | category | flops | bytes accessed | tf_op | source)
XLA Modules:
  0.0 481.1 jit_solution(11375418378671152968)
XLA Ops:
  0.0 7.9 %copy.55 = bf16[192,8,16,128]{3,2,1,0:T(8,128)(2,1)} copy(bf16[192,8,16,128]{3,1,2,0:T(8,128)(2,1)} %bitcast.147) | data formatting | bytes 12582912
  7.9 5.2 %fusion.47 = (f32[8,64,16]{2,1,0:T(8,128)S(1)}, f32[8,64,16]{2,1,0:T(8,128)}) fusion(bf16[8,64,3,16,128]{4,3,1,2,0:T(8,128)(2,1)} %bitcast.61), kind=kLoop, calls=%fused_computation.84 | loop fusion | flops 6275072 | bytes 4259840 | tf_op jit(solution)/shard_map/reduce_sum | solution.py:16
  13.2 3.3 slice_bitcast_fusion.4
  18.3 4.5 fusion.49
  22.8 3.2 pad_maximum_fusion
  26.0 6.8 %gather_fusion.5 = bf16[8,64,3,16,128]{4,3,2,1,0:T(8,128)(2,1)} fusion(bf16[8,64,3,16,128]{4,3,2,1,0:T(8,128)(2,1)} %pad_maximum_fusion, s32[1024]{0:T(1024)S(1)} %pad_clamp_fusion.1), kind=kCustom, calls=%fused_computation.2.clone | custom fusion | bytes 12582944 | tf_op jit(solution)/shard_map/jit(_take)/gather | solution.py:147
  32.8 6.1 %broadcast_select_fusion.1 = bf16[8,64,3,16,128]{4,3,2,1,0:T(8,128)(2,1)} fusion(bf16[8,64,3,16,128]{4,3,2,1,0:T(8,128)(2,1)} %gather_fusion.5, pred[8]{0:T(512)(128)(4,1)S(1)} %compare_and_fusion.2), kind=kLoop, calls=%fused_computation.79 | loop fusion | flops 3145728 | bytes 12582920 | tf_op jit(solution)/shard_map/jit(_take)/select_n | solution.py:147
  38.9 4.8 all-to-all-start.1
  44.4 71.4 %all-to-all-done.1 = bf16[8,64,3,16,128]{4,3,2,1,0:T(8,128)(2,1)} async-done(((bf16[8,64,3,16,128]{4,3,2,1,0:T(8,128)(2,1)}), bf16[8,64,3,16,128]{4,3,2,1,0:T(8,128)(2,1)}, u32[]{:S(2)}, u32[]{:S(2)}) %all-to-all-start.1) | async-done | bytes 6291488 | tf_op jit(solution)/shard_map/all_to_all | solution.py:146
  115.8 6.8 %gather_fusion.6 = bf16[8,64,3,16,128]{4,3,2,1,0:T(8,128)(2,1)} fusion(bf16[8,64,3,16,128]{4,3,2,1,0:T(8,128)(2,1)} %all-to-all-done.1, s32[1024]{0:T(1024)S(1)} %pad_clamp_fusion), kind=kCustom, calls=%fused_computation.6.clone | custom fusion | bytes 12582944 | tf_op jit(solution)/shard_map/jit(_take)/gather | solution.py:153
  122.6 3.5 broadcast_select_fusion
  126.0 4.4 copy.46
  130.4 8.3 %all-to-all-start.2 = ((bf16[8,64,3,16,128]{4,1,2,0,3:T(8,128)(2,1)}), bf16[8,64,3,16,128]{4,1,2,0,3:T(8,128)(2,1)}, u32[]{:S(2)}, u32[]{:S(2)}) async-start(bf16[8,64,3,16,128]{4,1,2,0,3:T(8,128)(2,1)} %copy.46), calls=%async_computation.2 | async-start | bytes 12582912 | tf_op jit(solution)/shard_map/all_to_all | solution.py:93
  140.0 2.4 gather_fusion
  143.0 3.9 broadcast_select_fusion.2
  146.9 84.8 %all-to-all-done.2 = bf16[8,64,3,16,128]{4,1,2,0,3:T(8,128)(2,1)} async-done(((bf16[8,64,3,16,128]{4,1,2,0,3:T(8,128)(2,1)}), bf16[8,64,3,16,128]{4,1,2,0,3:T(8,128)(2,1)}, u32[]{:S(2)}, u32[]{:S(2)}) %all-to-all-start.2) | async-done | bytes 6291488 | tf_op jit(solution)/shard_map/all_to_all | solution.py:93
  231.7 4.7 all-to-all-start
  236.3 7.6 %copy.47 = bf16[8,64,3,16,128]{4,1,3,2,0:T(8,128)(2,1)} copy(bf16[8,64,3,16,128]{4,1,2,0,3:T(8,128)(2,1)} %all-to-all-done.2) | data formatting | bytes 12582912 | tf_op jit(solution)/shard_map/all_to_all | solution.py:93
  244.0 175.9 %while.11 = (s32[]{:T(128)}, bf16[8,1024,1,128]{1,3,2,0:T(8,128)(2,1)}, s32[8]{0:T(128)}, bf16[8,1024,3,1,128]{4,1,2,3,0:T(8,128)(2,1)}, s32[]{:T(128)}, /*index=5*/s32[]{:T(128)}, s32[]{:T(128)}) while((s32[]{:T(128)}, bf16[8,1024,1,128]{1,3,2,0:T(8,128)(2,1)}, s32[8]{0:T(128)}, bf16[8,1024,3,1,128]{4,1,2,3,0:T(8,128)(2,1)}, s32[]{:T(128)}, ...), condition=%wide.region_30.35_spmd, body=%wide.region_5.34_spmd.sunk | while | flops 543952384 | bytes 25459632 | solution.py:94
  245.2 2.1 dynamic-slice_bitcast_fusion.2
  249.8 7.6 %conditional.13 = (bf16[512,1,128]{0,2,1:T(8,128)(2,1)S(1)}) conditional(s32[]{:T(128)} %convert_element_type.108, () %tuple.109, (s32[]{:T(128)}, bf16[1024,3,1,128]{3,0,2,1:T(8,128)(2,1)}, bf16[1024,1,128]{2,0,1:T(8,128)(2,1)}, bf16[1024,1,128]{2,0,1:T(8,128)(2,1)S(1)}) %tuple.108), branch_computations={%region_6.10_spmd, %region_7.21_spmd} | conditional | flops 271647744 | bytes 10631292 | solution.py:84
  251.4 2.0 conditional
  254.2 2.0 conditional.1
  259.7 8.2 %conditional.12 = (bf16[512,1,128]{0,2,1:T(8,128)(2,1)}) conditional(s32[]{:T(128)} %convert_element_type.107, () %tuple.107, (s32[]{:T(128)}, bf16[1024,3,1,128]{3,0,2,1:T(8,128)(2,1)}, bf16[1024,1,128]{2,0,1:T(8,128)(2,1)}, bf16[1024,1,128]{2,0,1:T(8,128)(2,1)S(1)}) %tuple.108), branch_computations={%region_18.22_spmd, %region_19.0_spmd} | conditional | flops 271647744 | bytes 10631292 | solution.py:84
  264.2 2.0 conditional.5
  270.9 2.1 dynamic-slice_bitcast_fusion.2
  275.4 7.6 %conditional.13 = (bf16[512,1,128]{0,2,1:T(8,128)(2,1)S(1)}) conditional(s32[]{:T(128)} %convert_element_type.108, () %tuple.109, (s32[]{:T(128)}, bf16[1024,3,1,128]{3,0,2,1:T(8,128)(2,1)}, bf16[1024,1,128]{2,0,1:T(8,128)(2,1)}, bf16[1024,1,128]{2,0,1:T(8,128)(2,1)S(1)}) %tuple.108), branch_computations={%region_6.10_spmd, %region_7.21_spmd} | conditional | flops 271647744 | bytes 10631292 | solution.py:84
  277.0 2.0 conditional
  279.8 2.0 conditional.1
  285.3 8.2 %conditional.12 = (bf16[512,1,128]{0,2,1:T(8,128)(2,1)}) conditional(s32[]{:T(128)} %convert_element_type.107, () %tuple.107, (s32[]{:T(128)}, bf16[1024,3,1,128]{3,0,2,1:T(8,128)(2,1)}, bf16[1024,1,128]{2,0,1:T(8,128)(2,1)}, bf16[1024,1,128]{2,0,1:T(8,128)(2,1)S(1)}) %tuple.108), branch_computations={%region_18.22_spmd, %region_19.0_spmd} | conditional | flops 271647744 | bytes 10631292 | solution.py:84
  289.8 2.0 conditional.5
  296.5 2.1 dynamic-slice_bitcast_fusion.2
  301.0 7.6 %conditional.13 = (bf16[512,1,128]{0,2,1:T(8,128)(2,1)S(1)}) conditional(s32[]{:T(128)} %convert_element_type.108, () %tuple.109, (s32[]{:T(128)}, bf16[1024,3,1,128]{3,0,2,1:T(8,128)(2,1)}, bf16[1024,1,128]{2,0,1:T(8,128)(2,1)}, bf16[1024,1,128]{2,0,1:T(8,128)(2,1)S(1)}) %tuple.108), branch_computations={%region_6.10_spmd, %region_7.21_spmd} | conditional | flops 271647744 | bytes 10631292 | solution.py:84
  302.6 2.0 conditional
  305.5 2.0 conditional.1
  310.9 8.2 %conditional.12 = (bf16[512,1,128]{0,2,1:T(8,128)(2,1)}) conditional(s32[]{:T(128)} %convert_element_type.107, () %tuple.107, (s32[]{:T(128)}, bf16[1024,3,1,128]{3,0,2,1:T(8,128)(2,1)}, bf16[1024,1,128]{2,0,1:T(8,128)(2,1)}, bf16[1024,1,128]{2,0,1:T(8,128)(2,1)S(1)}) %tuple.108), branch_computations={%region_18.22_spmd, %region_19.0_spmd} | conditional | flops 271647744 | bytes 10631292 | solution.py:84
  315.4 2.0 conditional.5
  322.1 2.1 dynamic-slice_bitcast_fusion.2
  326.6 7.6 %conditional.13 = (bf16[512,1,128]{0,2,1:T(8,128)(2,1)S(1)}) conditional(s32[]{:T(128)} %convert_element_type.108, () %tuple.109, (s32[]{:T(128)}, bf16[1024,3,1,128]{3,0,2,1:T(8,128)(2,1)}, bf16[1024,1,128]{2,0,1:T(8,128)(2,1)}, bf16[1024,1,128]{2,0,1:T(8,128)(2,1)S(1)}) %tuple.108), branch_computations={%region_6.10_spmd, %region_7.21_spmd} | conditional | flops 271647744 | bytes 10631292 | solution.py:84
  328.3 2.0 conditional
  331.1 2.0 conditional.1
  336.5 8.2 %conditional.12 = (bf16[512,1,128]{0,2,1:T(8,128)(2,1)}) conditional(s32[]{:T(128)} %convert_element_type.107, () %tuple.107, (s32[]{:T(128)}, bf16[1024,3,1,128]{3,0,2,1:T(8,128)(2,1)}, bf16[1024,1,128]{2,0,1:T(8,128)(2,1)}, bf16[1024,1,128]{2,0,1:T(8,128)(2,1)S(1)}) %tuple.108), branch_computations={%region_18.22_spmd, %region_19.0_spmd} | conditional | flops 271647744 | bytes 10631292 | solution.py:84
  341.0 2.0 conditional.5
  347.7 2.1 dynamic-slice_bitcast_fusion.2
  352.2 7.6 %conditional.13 = (bf16[512,1,128]{0,2,1:T(8,128)(2,1)S(1)}) conditional(s32[]{:T(128)} %convert_element_type.108, () %tuple.109, (s32[]{:T(128)}, bf16[1024,3,1,128]{3,0,2,1:T(8,128)(2,1)}, bf16[1024,1,128]{2,0,1:T(8,128)(2,1)}, bf16[1024,1,128]{2,0,1:T(8,128)(2,1)S(1)}) %tuple.108), branch_computations={%region_6.10_spmd, %region_7.21_spmd} | conditional | flops 271647744 | bytes 10631292 | solution.py:84
  353.8 1.9 conditional
  356.7 2.0 conditional.1
  362.1 8.2 %conditional.12 = (bf16[512,1,128]{0,2,1:T(8,128)(2,1)}) conditional(s32[]{:T(128)} %convert_element_type.107, () %tuple.107, (s32[]{:T(128)}, bf16[1024,3,1,128]{3,0,2,1:T(8,128)(2,1)}, bf16[1024,1,128]{2,0,1:T(8,128)(2,1)}, bf16[1024,1,128]{2,0,1:T(8,128)(2,1)S(1)}) %tuple.108), branch_computations={%region_18.22_spmd, %region_19.0_spmd} | conditional | flops 271647744 | bytes 10631292 | solution.py:84
  363.8 2.0 conditional.4
  366.6 2.0 conditional.5
  373.3 2.1 dynamic-slice_bitcast_fusion.2
  377.8 5.5 %conditional.13 = (bf16[512,1,128]{0,2,1:T(8,128)(2,1)S(1)}) conditional(s32[]{:T(128)} %convert_element_type.108, () %tuple.109, (s32[]{:T(128)}, bf16[1024,3,1,128]{3,0,2,1:T(8,128)(2,1)}, bf16[1024,1,128]{2,0,1:T(8,128)(2,1)}, bf16[1024,1,128]{2,0,1:T(8,128)(2,1)S(1)}) %tuple.108), branch_computations={%region_6.10_spmd, %region_7.21_spmd} | conditional | flops 271647744 | bytes 10631292 | solution.py:84
  379.4 2.0 conditional
  389.2 2.1 dynamic-slice_bitcast_fusion.2
  393.8 5.4 %conditional.13 = (bf16[512,1,128]{0,2,1:T(8,128)(2,1)S(1)}) conditional(s32[]{:T(128)} %convert_element_type.108, () %tuple.109, (s32[]{:T(128)}, bf16[1024,3,1,128]{3,0,2,1:T(8,128)(2,1)}, bf16[1024,1,128]{2,0,1:T(8,128)(2,1)}, bf16[1024,1,128]{2,0,1:T(8,128)(2,1)S(1)}) %tuple.108), branch_computations={%region_6.10_spmd, %region_7.21_spmd} | conditional | flops 271647744 | bytes 10631292 | solution.py:84
  405.2 2.1 dynamic-slice_bitcast_fusion.2
  409.8 5.4 %conditional.13 = (bf16[512,1,128]{0,2,1:T(8,128)(2,1)S(1)}) conditional(s32[]{:T(128)} %convert_element_type.108, () %tuple.109, (s32[]{:T(128)}, bf16[1024,3,1,128]{3,0,2,1:T(8,128)(2,1)}, bf16[1024,1,128]{2,0,1:T(8,128)(2,1)}, bf16[1024,1,128]{2,0,1:T(8,128)(2,1)S(1)}) %tuple.108), branch_computations={%region_6.10_spmd, %region_7.21_spmd} | conditional | flops 271647744 | bytes 10631292 | solution.py:84
  411.4 1.9 conditional
  419.9 4.2 copy.49
  424.1 5.6 %all-to-all-start.3 = ((bf16[8,1024,1,128]{3,0,2,1:T(8,128)(2,1)}), bf16[8,1024,1,128]{3,0,2,1:T(8,128)(2,1)S(1)}, u32[]{:S(2)}, u32[]{:S(2)}) async-start(bf16[8,1024,1,128]{3,0,2,1:T(8,128)(2,1)} %copy.49), calls=%async_computation.3 | async-start | bytes 4194304 | tf_op jit(solution)/shard_map/all_to_all | solution.py:97
  430.1 4.3 gather_fusion.2
  434.4 29.1 %all-to-all-done.3 = bf16[8,1024,1,128]{3,0,2,1:T(8,128)(2,1)S(1)} async-done(((bf16[8,1024,1,128]{3,0,2,1:T(8,128)(2,1)}), bf16[8,1024,1,128]{3,0,2,1:T(8,128)(2,1)S(1)}, u32[]{:S(2)}, u32[]{:S(2)}) %all-to-all-start.3) | async-done | bytes 2097184 | tf_op jit(solution)/shard_map/all_to_all | solution.py:97
  465.1 2.3 dot_general.41
  467.4 13.6 %add_convert_fusion = bf16[8,64,3072]{2,1,0:T(8,128)(2,1)} fusion(bf16[8,64,2048]{2,1,0:T(8,128)(2,1)} %dot_general.41, bf16[2048,3072]{1,0:T(8,128)(2,1)} %param.47, bf16[8,64,3072]{2,1,0:T(8,128)(2,1)} %gather_fusion.2, f32[8,3072]{1,0:T(8,128)S(1)} %fusion.53, pred[8]{0:T(512)(128)(4,1)S(1)} %get-tuple-element.203), kind=kOutput, calls=%fused_computation.77 | convolution fusion | flops 6450315264 | bytes 21069832 | tf_op jit(solution)/shard_map/dot_general | solution.py:107
  (300 shorter events, 153.6 us)
Async XLA Ops:
  0.0 140.0 %copy-start = (bf16[8,64,3072]{2,1,0:T(8,128)(2,1)S(1)}, bf16[8,64,3072]{2,1,0:T(8,128)(2,1)}, u32[]{:S(2)}) copy-start(bf16[8,64,3072]{2,1,0:T(8,128)(2,1)} %param.40) | copy-start | bytes 9437188
  13.1 3.3 copy-start.9
  13.1 5.1 %copy-start.7 = (f32[128]{0:T(128)S(1)}, f32[128]{0:T(128)}, u32[]{:S(2)}) copy-start(f32[128]{0:T(128)} %param.45) | copy-start | bytes 1540
  13.1 5.1 %copy-start.8 = (f32[128]{0:T(128)S(1)}, f32[128]{0:T(128)}, u32[]{:S(2)}) copy-start(f32[128]{0:T(128)} %param.46) | copy-start | bytes 1540
  18.3 4.6 copy-start.5
  38.9 76.9 %all-to-all-start.1 = ((bf16[8,64,3,16,128]{4,3,2,1,0:T(8,128)(2,1)}), bf16[8,64,3,16,128]{4,3,2,1,0:T(8,128)(2,1)}, u32[]{:S(2)}, u32[]{:S(2)}) async-start(bf16[8,64,3,16,128]{4,3,2,1,0:T(8,128)(2,1)} %broadcast_select_fusion.1), calls=%async_computation.1 | async-start | bytes 12582912 | tf_op jit(solution)/shard_map/all_to_all | solution.py:146
  130.4 8.3 %copy-start.2 = (s32[64]{0:T(128)S(1)}, s32[64]{0:T(128)}, u32[]{:S(2)}) copy-start(s32[64]{0:T(128)} %param.42) | copy-start | bytes 772
  130.4 9.0 %copy-start.3 = (s32[64]{0:T(128)S(1)}, s32[64]{0:T(128)}, u32[]{:S(2)}) copy-start(s32[64]{0:T(128)} %param.41) | copy-start | bytes 772
  130.4 101.3 %all-to-all-start.2 = ((bf16[8,64,3,16,128]{4,1,2,0,3:T(8,128)(2,1)}), bf16[8,64,3,16,128]{4,1,2,0,3:T(8,128)(2,1)}, u32[]{:S(2)}, u32[]{:S(2)}) async-start(bf16[8,64,3,16,128]{4,1,2,0,3:T(8,128)(2,1)} %copy.46), calls=%async_computation.2 | async-start | bytes 12582912 | tf_op jit(solution)/shard_map/all_to_all | solution.py:93
  231.7 192.4 %all-to-all-start = ((bf16[8,64,3072]{2,1,0:T(8,128)(2,1)}), bf16[8,64,3072]{2,1,0:T(8,128)(2,1)}, u32[]{:S(2)}, u32[]{:S(2)}) async-start(bf16[8,64,3072]{2,1,0:T(8,128)(2,1)} %broadcast_select_fusion.2), calls=%async_computation | async-start | bytes 6291456 | tf_op jit(solution)/shard_map/all_to_all | solution.py:149
  257.4 0.7 copy-start.4
  283.0 0.7 copy-start.4
  308.6 0.7 copy-start.4
  334.2 0.7 copy-start.4
  359.8 0.7 copy-start.4
  383.3 0.7 copy-start.4
  399.2 0.7 copy-start.4
  415.2 0.7 copy-start.4
  424.1 5.7 %copy-start.6 = (f32[50,3072]{1,0:T(8,128)S(1)}, f32[50,3072]{1,0:T(8,128)}, u32[]{:S(2)}) copy-start(f32[50,3072]{1,0:T(8,128)} %param.44) | copy-start | bytes 1843204
  424.1 39.4 %all-to-all-start.3 = ((bf16[8,1024,1,128]{3,0,2,1:T(8,128)(2,1)}), bf16[8,1024,1,128]{3,0,2,1:T(8,128)(2,1)S(1)}, u32[]{:S(2)}, u32[]{:S(2)}) async-start(bf16[8,1024,1,128]{3,0,2,1:T(8,128)(2,1)} %copy.49), calls=%async_computation.3 | async-start | bytes 4194304 | tf_op jit(solution)/shard_map/all_to_all | solution.py:97
  467.4 13.6 %copy-start.1 = (bf16[8,64,3072]{2,1,0:T(8,128)(2,1)S(1)}, bf16[8,64,3072]{2,1,0:T(8,128)(2,1)}, u32[]{:S(2)}) copy-start(bf16[8,64,3072]{2,1,0:T(8,128)(2,1)} %param.40) | copy-start | bytes 9437188
where the time goes:
time: 484 us; the launch traced here: 481 us
  waiting for transfers between devices  185 us (38%)
  local copies, waits for them, and re-layouts  109 us (23%)
  other arithmetic  82.1 us (17%)
  matrix products  49.4 us (10%)
  loops' own time  31.8 us (7%)
  starting transfers between devices  23.4 us (5%)
    all_to_all x1, waiting for transfers between devices, attend(): lax.all_to_all(block, 'sp', split_axis=3, concat_axis=1, tiled=True)  84.8 us
    all_to_all x1, waiting for transfers between devices, per_device(): lax.all_to_all(jnp.take(shaped, send_order, axis=0), 'grp', split_axis=0,...  71.4 us
    all_to_all x1, waiting for transfers between devices, attend(): lax.all_to_all(as_sent(attended), 'sp', split_axis=1, concat_axis=2, tile...  29.1 us
    dot_general x23, matrix products, live_key(): jnp.einsum('qhd,khd->hqk', query_part, key_part, preferred_element_type=j...  28.3 us
    another operation x16, loops' own time, clip_attention(): summed = lax.cond(query_block * tile < length, live_query, dead_query, None)  19.1 us
    squeeze x8, local copies, waits for them, and re-layouts, attend(): attended = lax.map(clip_attention, (head_block, clip_len))  16.7 us
    lt x23, other arithmetic, live_key(): key_live = key_block * tile + jnp.arange(tile, dtype=jnp.int32) < length  16 us
    convert_element_type x16, other arithmetic, clip_attention(): jnp.where(query_live[:, None, None], summed, jnp.float32(0.0))  14.9 us
  transfers between devices with their start and end apart: 4, of which 3 were waited for; matrix products, arithmetic and copies ran while one was open for 35% of the time, Pallas kernels for 0%

commit v1 on v0

v1 whole, which is shorter than its diff:
```python
import functools
import math

import jax
import jax.numpy as jnp
from jax import lax
from jax.experimental import pallas as pl
from jax.experimental.pallas import tpu as pltpu
from jax.sharding import PartitionSpec as P

HEADS = 16
HD = 128
CG = 8
TILE = 256
CHUNKS = ((4, 2), (6, 2), (2, 2), (0, 2))
SCALE = math.log2(math.e) / math.sqrt(HD)
VMEM_LIMIT = 24 * 2**20


def params(limit=VMEM_LIMIT):
    return pltpu.CompilerParams(vmem_limit_bytes=limit)


def in_vmem(array):
    return pltpu.with_memory_space_constraint(array, pltpu.VMEM)


def meta_kernel(group_ref, length_ref, step_ref, slot_ref, meta_ref):
    group = group_ref[0]
    for i in range(CG):
        clip = group * CG + i
        k = lax.shift_right_logical(slot_ref[clip], 3) ^ group
        meta_ref[k] = i
        meta_ref[CG + k] = length_ref[clip]
        meta_ref[2 * CG + k] = step_ref[clip]
    for clip in range(slot_ref.shape[0]):
        slot = slot_ref[clip]

        @pl.when(lax.shift_right_logical(slot, 3) == group)
        def _(slot=slot, clip=clip):
            meta_ref[3 * CG + ((clip // CG) ^ group)] = slot & 7


def make_meta(group, lengths, t_index, slot_target):
    smem = pl.BlockSpec(memory_space=pltpu.SMEM)
    return pl.pallas_call(
        meta_kernel,
        out_shape=jax.ShapeDtypeStruct((4 * CG,), jnp.int32),
        in_specs=[smem] * 4,
        out_specs=smem,
        name="meta",
    )(group, lengths, t_index, slot_target)


def prep_kernel(meta_ref, x_ref, o_ref):
    j = pl.program_id(0)
    for h in range(HEADS):
        o_ref[h, j] = x_ref[0, :, :, h * HD : (h + 1) * HD]


def prep(meta, x, first, count):
    rows = x.shape[2]
    return pl.pallas_call(
        prep_kernel,
        grid_spec=pltpu.PrefetchScalarGridSpec(
            num_scalar_prefetch=1,
            grid=(count,),
            in_specs=[
                pl.BlockSpec((1, 3, rows, HEADS * HD), lambda j, m: (m[first + j], 0, 0, 0))
            ],
            out_specs=pl.BlockSpec(memory_space=pltpu.VMEM),
        ),
        out_shape=pltpu.VMEM((HEADS, count, 3, rows, HD), jnp.bfloat16),
        compiler_params=params(),
        name="prep",
    )(meta, x)


def rms(part, gain):
    wide = part.astype(jnp.float32)
    mean = jnp.mean(wide * wide, axis=-1, keepdims=True)
    return (wide * lax.rsqrt(mean + 1e-06) * gain).astype(jnp.bfloat16)


def attention_kernel(first, count, meta_ref, y_ref, qg_ref, kg_ref, o_ref, q_ref, k_ref, v_ref):
    blocks, rows = y_ref.shape[0], y_ref.shape[3]
    total = blocks * rows
    tiles = total // TILE
    per_tile = TILE // rows
    q_gain, k_gain = qg_ref[...], kg_ref[...]

    for c in range(count):
        length = meta_ref[CG + first + c]
        live_tiles = lax.div(length + (TILE - 1), TILE)
        for t in range(tiles):
            at = slice(t * per_tile, (t + 1) * per_tile)
            to = slice(t * TILE, (t + 1) * TILE)

            @pl.when(t < live_tiles)
            def _(at=at, to=to, t=t):
                q_ref[to] = rms(y_ref[at, c, 0].reshape(TILE, HD), q_gain)
                k_ref[to] = rms(y_ref[at, c, 1].reshape(TILE, HD), k_gain)
                row = t * TILE + lax.broadcasted_iota(jnp.int32, (TILE, HD), 0)
                live = row < length
                value = y_ref[at, c, 2].reshape(TILE, HD)
                v_ref[to, :HD] = jnp.where(live, value, jnp.zeros_like(value))
                v_ref[to, HD:] = jnp.where(live, 1.0, 0.0).astype(jnp.bfloat16)

            @pl.when(t >= live_tiles)
            def _(at=at):
                o_ref[at, c] = jnp.zeros((per_tile, rows, HD), jnp.bfloat16)

        for n in range(1, tiles + 1):

            @pl.when(live_tiles == n)
            def _(n=n):
                keys = k_ref[: n * TILE]
                values = v_ref[: n * TILE]
                for t in range(n):
                    scores = lax.dot_general(
                        q_ref[t * TILE : (t + 1) * TILE],
                        keys,
                        (((1,), (1,)), ((), ())),
                        preferred_element_type=jnp.float32,
                    )
                    raised = jnp.exp2(scores * SCALE).astype(jnp.bfloat16)
                    summed = jnp.dot(raised, values, preferred_element_type=jnp.float32)
                    result = summed[:, :HD] / summed[:, HD:]
                    if t == n - 1:
                        row = t * TILE + lax.broadcasted_iota(jnp.int32, (TILE, HD), 0)
                        result = jnp.where(row < length, result, 0.0)
                    o_ref[t * per_tile : (t + 1) * per_tile, c] = result.astype(
                        jnp.bfloat16
                    ).reshape(per_tile, rows, HD)


def attention(meta, y, q_gain, k_gain, first, count):
    blocks, rows = y.shape[0], y.shape[3]
    total = blocks * rows
    vmem = pl.BlockSpec(memory_space=pltpu.VMEM)
    return pl.pallas_call(
        functools.partial(attention_kernel, first, count),
        in_specs=[pl.BlockSpec(memory_space=pltpu.SMEM), vmem, vmem, vmem],
        out_specs=vmem,
        out_shape=pltpu.VMEM((blocks, count, rows, HD), jnp.bfloat16),
        scratch_shapes=[
            pltpu.VMEM((total, HD), jnp.bfloat16),
            pltpu.VMEM((total, HD), jnp.bfloat16),
            pltpu.VMEM((total, 2 * HD), jnp.bfloat16),
        ],
        compiler_params=params(),
        cost_estimate=pl.CostEstimate(
            flops=count * 4 * total * total * HD,
            bytes_accessed=count * total * HD * 8,
            transcendentals=count * total * total,
        ),
        name="attention",
    )(meta, in_vmem(y), q_gain, k_gain)


def project_kernel(first, count, meta_ref, z_ref, w_ref, gate_ref, *refs):
    token_refs, out_refs, a_ref = refs[:count], refs[count : 2 * count], refs[2 * count]
    rows = z_ref.shape[2]

    @pl.when(pl.program_id(0) == 0)
    def _():
        for c in range(count):
            for h in range(HEADS):
                a_ref[c * rows : (c + 1) * rows, h * HD : (h + 1) * HD] = z_ref[h, c]

    projected = jnp.dot(a_ref[...], w_ref[...], preferred_element_type=jnp.float32)
    for c in range(count):
        gate = gate_ref[pl.ds(meta_ref[2 * CG + first + c], 1), :]
        part = projected[c * rows : (c + 1) * rows]
        out_refs[c][...] = (token_refs[c][0].astype(jnp.float32) + gate * part).astype(
            jnp.bfloat16
        )


def project(meta, z, out_weight, gate_table, tokens, first, count):
    rows, width = tokens.shape[1], tokens.shape[2]
    block = 512

    def token_block(c):
        return pl.BlockSpec((1, rows, block), lambda n, m: (m[first + c], 0, n))

    return pl.pallas_call(
        functools.partial(project_kernel, first, count),
        grid_spec=pltpu.PrefetchScalarGridSpec(
            num_scalar_prefetch=1,
            grid=(width // block,),
            in_specs=[
                pl.BlockSpec(memory_space=pltpu.VMEM),
                pl.BlockSpec((HEADS * HD, block), lambda n, m: (0, n)),
                pl.BlockSpec((gate_table.shape[0], block), lambda n, m: (0, n)),
            ]
            + [token_block(c) for c in range(count)],
            out_specs=[pl.BlockSpec((rows, block), lambda n, m: (0, n))] * count,
            scratch_shapes=[pltpu.VMEM((count * rows, HEADS * HD), jnp.bfloat16)],
        ),
        out_shape=[jax.ShapeDtypeStruct((rows, width), jnp.bfloat16)] * count,
        compiler_params=params(),
        cost_estimate=pl.CostEstimate(
            flops=2 * count * rows * HEADS * HD * width,
            bytes_accessed=2 * HEADS * HD * width + 4 * count * rows * width,
            transcendentals=0,
        ),
        name="project",
    )(meta, in_vmem(z), out_weight, gate_table, *[tokens] * count)


def per_device(qkv, tokens, lengths, t_index, slot_target, gate_table, q_gain, k_gain, out_weight):
    groups = lax.axis_size("grp")
    x = jnp.swapaxes(qkv, 1, 2)
    q_gain, k_gain = q_gain.reshape(1, HD), k_gain.reshape(1, HD)
    meta = make_meta(lax.axis_index("grp").reshape(1), lengths, t_index, slot_target)

    last = None

    def exchange(array):
        nonlocal last
        if last is not None:
            array, _ = lax.optimization_barrier((array, last))
        last = lax.all_to_all(array, "sp", split_axis=0, concat_axis=0, tiled=True)
        return last

    out = jnp.zeros_like(tokens)

    def finish(chunk, attended):
        nonlocal out
        z = exchange(attended)
        results = project(meta, z, out_weight, gate_table, tokens, *chunk)
        for c, result in enumerate(results):
            k = chunk[0] + c
            if k:
                result = lax.ppermute(result, "grp", [(g, g ^ k) for g in range(groups)])
            out = lax.dynamic_update_slice(out, result[None], (meta[3 * CG + k], 0, 0))

    waiting = None
    for chunk in CHUNKS:
        y = exchange(prep(meta, x, *chunk))
        if waiting is not None:
            finish(*waiting)
        waiting = (chunk, attention(meta, y, q_gain, k_gain, *chunk))
    finish(*waiting)
    return out


def solution(mesh):
    return jax.shard_map(
        per_device,
        mesh=mesh,
        in_specs=(
            P("grp", "sp", None, None),
            P("grp", "sp", None),
            P(),
            P(),
            P(),
            P(),
            P(),
            P(),
            P(),
        ),
        out_specs=P("grp", "sp", None),
        check_vma=False,
    )
```

time: 484 us -> 246 us (0.51)
  waiting for transfers between devices: 185 us -> 73.2 us
  other arithmetic: 82.1 us -> 8.61 us
  local copies, waits for them, and re-layouts: 109 us -> 46.3 us
  matrix products: 49.4 us -> 0 us
  Pallas kernels: 0 us -> 49.4 us
  loops' own time: 31.8 us -> 0 us
  starting transfers between devices: 23.4 us -> 49.4 us
  between operations: 0.19 us -> 15.5 us
    all_to_all x4 -> x8, waiting for transfers between devices: 185 us -> 65.9 us  [exchange(): last = lax.all_to_all(array, 'sp', split_axis=0, concat_axis=0, tiled=True)]
    dot_general x48 -> x0, matrix products: 49.4 us -> none  [the longest x23 28.3 us: live_key(): jnp.einsum('qhd,khd->hqk', query_part, key_part, preferred_element_type=j...]
    pallas_call x0 -> x12, Pallas kernels: none -> 49.4 us  [the longest x4 23.7 us: attention(): pl.pallas_call(functools.partial(attention_kernel, first, count), in_spec...]
    another operation x69 -> x0, loops' own time: 31.8 us -> none  [the longest x16 19.1 us: clip_attention(): summed = lax.cond(query_block * tile < length, live_query, dead_query, None)]
    squeeze x16 -> x0, local copies, waits for them, and re-layouts: 30.8 us -> none  [the longest x8 16.7 us: attend(): attended = lax.map(clip_attention, (head_block, clip_len))]
    convert_element_type x30 -> x0, other arithmetic: 22.9 us -> none  [the longest x16 14.9 us: clip_attention(): jnp.where(query_live[:, None, None], summed, jnp.float32(0.0))]
    gather x7 -> x0, local copies, waits for them, and re-layouts: 22.2 us -> none  [the longest x1 6.78 us: per_device(): local_qkv = jnp.take(arrived_qkv, recv_pos, axis=0)]
    unnamed x20 -> x42, local copies, waits for them, and re-layouts: 11.3 us -> 33.2 us
  transfers between devices with their start and end apart: 4 -> 15, of which waited for: 3 -> 8; matrix products, arithmetic and copies ran while one was open for 35% -> 5% of each run, Pallas kernels for 0% -> 19%
where the time goes in v1:
time: 246 us; the launch traced here: 242 us
  waiting for transfers between devices  73.2 us (30%)
  Pallas kernels  49.4 us (20%)
  starting transfers between devices  49.4 us (20%)
  local copies, waits for them, and re-layouts  46.3 us (19%)
  between operations  15.5 us (6%)
  other arithmetic  8.61 us (4%)
    all_to_all x8, waiting for transfers between devices, exchange(): last = lax.all_to_all(array, 'sp', split_axis=0, concat_axis=0, tiled=True)  65.9 us
    all_to_all x8, starting transfers between devices, exchange(): last = lax.all_to_all(array, 'sp', split_axis=0, concat_axis=0, tiled=True)  41.8 us
    unnamed x42, local copies, waits for them, and re-layouts  33.2 us
    pallas_call x4, Pallas kernels, attention(): pl.pallas_call(functools.partial(attention_kernel, first, count), in_spec...  23.7 us
    pallas_call x3, Pallas kernels, project(): pl.pallas_call(functools.partial(project_kernel, first, count), grid_spec...  17.5 us
    dynamic_update_slice x7, local copies, waits for them, and re-layouts, finish(): out = lax.dynamic_update_slice(out, result[None], (meta[3 * CG + k], 0, 0))  10.4 us
    pallas_call x1, other arithmetic, project(): pl.pallas_call(functools.partial(project_kernel, first, count), grid_spec...  8.61 us
    ppermute x7, starting transfers between devices, finish(): result = lax.ppermute(result, 'grp', [(g, g ^ k) for g in range(groups)])  7.63 us
  transfers between devices with their start and end apart: 15, of which 8 were waited for; matrix products, arithmetic and copies ran while one was open for 5% of the time, Pallas kernels for 19%

profile of v1, /device:TPU:0, one launch (start us, length us, event | category | flops | bytes accessed | tf_op | source)
XLA Modules:
  0.0 242.4 jit_solution(13210603150756157797)
XLA Ops:
  0.0 1.3 meta.1.meta_ref
  1.3 0.0 copy-start.4
  1.3 2.8 %copy-done.4 = bf16[8,64,3,2048]{3,1,2,0:T(8,128)(2,1)S(1)} copy-done((bf16[8,64,3,2048]{3,1,2,0:T(8,128)(2,1)S(1)}, bf16[8,64,3,2048]{3,1,2,0:T(8,128)(2,1)}, u32[]{:S(2)}) %copy-start.4) | copy-done | bytes 6291480
  4.1 0.7 copy-done.17
  4.8 2.0 prep.4
  6.8 8.2 %all-to-all-start = ((bf16[16,2,3,64,128]{4,3,2,1,0:T(8,128)(2,1)}), bf16[16,2,3,64,128]{4,3,2,1,0:T(8,128)(2,1)}, u32[]{:S(2)}, u32[]{:S(2)}) async-start(bf16[16,2,3,64,128]{4,3,2,1,0:T(8,128)(2,1)} %prep.4), calls=%async_computation | async-start | bytes 3145728 | tf_op jit(solution)/shard_map/all_to_all | solution.py:224
  15.0 0.0 copy-start.5
  15.0 2.8 %copy-done.5 = bf16[8,64,3,2048]{3,1,2,0:T(8,128)(2,1)S(1)} copy-done((bf16[8,64,3,2048]{3,1,2,0:T(8,128)(2,1)S(1)}, bf16[8,64,3,2048]{3,1,2,0:T(8,128)(2,1)}, u32[]{:S(2)}) %copy-start.5) | copy-done | bytes 6291480
  17.7 2.0 prep.5
  19.8 19.7 %all-to-all-done.y_ref = bf16[16,2,3,64,128]{4,3,2,1,0:T(8,128)(2,1)} async-done(((bf16[16,2,3,64,128]{4,3,2,1,0:T(8,128)(2,1)}), bf16[16,2,3,64,128]{4,3,2,1,0:T(8,128)(2,1)}, u32[]{:S(2)}, u32[]{:S(2)}) %all-to-all-start) | async-done | bytes 1572896 | tf_op jit(solution)/shard_map/all_to_all | solution.py:224
  39.5 4.4 %all-to-all-start.1 = ((bf16[16,2,3,64,128]{4,3,2,1,0:T(8,128)(2,1)}), bf16[16,2,3,64,128]{4,3,2,1,0:T(8,128)(2,1)}, u32[]{:S(2)}, u32[]{:S(2)}) async-start(bf16[16,2,3,64,128]{4,3,2,1,0:T(8,128)(2,1)} %prep.5), calls=%async_computation.1 | async-start | bytes 3145728 | tf_op jit(solution)/shard_map/all_to_all | solution.py:224
  43.9 6.4 %attention.4 = bf16[16,2,64,128]{3,2,1,0:T(8,128)(2,1)} custom-call(s32[32]{0:T(128)S(1)} %copy-done.18, bf16[16,2,3,64,128]{4,3,2,1,0:T(8,128)(2,1)} %all-to-all-done.y_ref, f32[1,128]{1,0:T(1,128)S(1)} %bitcast.32, f32[1,128]{1,0:T(1,128)S(1)} %bitcast.36), custom_call_target="tpu_custom_call" | custom-call | flops 1073741824 | bytes 2097152 | tf_op jit(solution)/shard_map/attention/pallas_call | solution.py:141
  50.3 15.7 %all-to-all-done.1.y_ref = bf16[16,2,3,64,128]{4,3,2,1,0:T(8,128)(2,1)} async-done(((bf16[16,2,3,64,128]{4,3,2,1,0:T(8,128)(2,1)}), bf16[16,2,3,64,128]{4,3,2,1,0:T(8,128)(2,1)}, u32[]{:S(2)}, u32[]{:S(2)}) %all-to-all-start.1) | async-done | bytes 1572896 | tf_op jit(solution)/shard_map/all_to_all | solution.py:224
  66.1 3.6 %all-to-all-start.2 = ((bf16[16,2,64,128]{3,2,1,0:T(8,128)(2,1)}), bf16[16,2,64,128]{3,2,1,0:T(8,128)(2,1)S(1)}, u32[]{:S(2)}, u32[]{:S(2)}) async-start(bf16[16,2,64,128]{3,2,1,0:T(8,128)(2,1)} %attention.4), calls=%async_computation.2 | async-start | bytes 1048576 | tf_op jit(solution)/shard_map/all_to_all | solution.py:224
  69.6 2.8 %copy-done.6 = bf16[8,64,3,2048]{3,1,2,0:T(8,128)(2,1)S(1)} copy-done((bf16[8,64,3,2048]{3,1,2,0:T(8,128)(2,1)S(1)}, bf16[8,64,3,2048]{3,1,2,0:T(8,128)(2,1)}, u32[]{:S(2)}) %copy-start.6) | copy-done | bytes 6291480
  72.4 2.0 prep.6
  74.4 5.3 %all-to-all-done.2.z_ref = bf16[16,2,64,128]{3,2,1,0:T(8,128)(2,1)S(1)} async-done(((bf16[16,2,64,128]{3,2,1,0:T(8,128)(2,1)}), bf16[16,2,64,128]{3,2,1,0:T(8,128)(2,1)S(1)}, u32[]{:S(2)}, u32[]{:S(2)}) %all-to-all-start.2) | async-done | bytes 524320 | tf_op jit(solution)/shard_map/all_to_all | solution.py:224
  79.8 0.8 copy-done.12
  80.6 4.4 %all-to-all-start.3 = ((bf16[16,2,3,64,128]{4,3,2,1,0:T(8,128)(2,1)}), bf16[16,2,3,64,128]{4,3,2,1,0:T(8,128)(2,1)}, u32[]{:S(2)}, u32[]{:S(2)}) async-start(bf16[16,2,3,64,128]{4,3,2,1,0:T(8,128)(2,1)} %prep.6), calls=%async_computation.3 | async-start | bytes 3145728 | tf_op jit(solution)/shard_map/all_to_all | solution.py:224
  85.0 0.0 copy-start.3
  85.0 5.9 %attention.5 = bf16[16,2,64,128]{3,2,1,0:T(8,128)(2,1)S(1)} custom-call(s32[32]{0:T(128)S(1)} %copy-done.18, bf16[16,2,3,64,128]{4,3,2,1,0:T(8,128)(2,1)} %all-to-all-done.1.y_ref, f32[1,128]{1,0:T(1,128)S(1)} %bitcast.33, f32[1,128]{1,0:T(1,128)S(1)} %bitcast.37), custom_call_target="tpu_custom_call" | custom-call | flops 1073741824 | bytes 2097152 | tf_op jit(solution)/shard_map/attention/pallas_call | solution.py:141
  90.9 0.8 copy-done.14
  91.7 14.9 %all-to-all-done.3.y_ref = bf16[16,2,3,64,128]{4,3,2,1,0:T(8,128)(2,1)} async-done(((bf16[16,2,3,64,128]{4,3,2,1,0:T(8,128)(2,1)}), bf16[16,2,3,64,128]{4,3,2,1,0:T(8,128)(2,1)}, u32[]{:S(2)}, u32[]{:S(2)}) %all-to-all-start.3) | async-done | bytes 1572896 | tf_op jit(solution)/shard_map/all_to_all | solution.py:224
  106.7 4.2 %all-to-all-start.4 = ((bf16[16,2,64,128]{3,2,1,0:T(8,128)(2,1)}), bf16[16,2,64,128]{3,2,1,0:T(8,128)(2,1)}, u32[]{:S(2)}, u32[]{:S(2)}) async-start(bf16[16,2,64,128]{3,2,1,0:T(8,128)(2,1)} %copy-done.14), calls=%async_computation.4 | async-start | bytes 1048576 | tf_op jit(solution)/shard_map/all_to_all | solution.py:224
  110.9 0.0 copy-start
  111.0 4.6 %copy-done = bf16[2048,3072]{1,0:T(8,128)(2,1)S(1)} copy-done((bf16[2048,3072]{1,0:T(8,128)(2,1)S(1)}, bf16[2048,3072]{1,0:T(8,128)(2,1)}, u32[]{:S(2)}) %copy-start) | copy-done | bytes 12582936
  115.5 1.1 copy-done.8
  116.6 1.0 copy-done.13
  117.7 5.2 %project.4 = (bf16[64,3072]{1,0:T(8,128)(2,1)}, bf16[64,3072]{1,0:T(8,128)(2,1)S(1)}) custom-call(s32[32]{0:T(128)S(1)} %copy-done.18, bf16[16,2,64,128]{3,2,1,0:T(8,128)(2,1)S(1)} %copy-done.13, bf16[2048,3072]{1,0:T(8,128)(2,1)S(1)} %copy-done, f32[50,3072]{1,0:T(8,128)S(1)} %copy-done.8, bf16[8,64,3072]{2,1,0:T(8,128)(2,1)S(1)} %copy-done.3, ...), custom_call_target="tpu_custom_call" | custom-call | flops 1610612736 | bytes 14155776 | tf_op jit(solution)/shard_map/project/pallas_call | solution.py:187
  122.9 3.0 %collective-permute-start = (bf16[64,3072]{1,0:T(8,128)(2,1)}, bf16[64,3072]{1,0:T(8,128)(2,1)}, u32[]{:S(2)}, u32[]{:S(2)}) collective-permute-start(bf16[64,3072]{1,0:T(8,128)(2,1)} %get-tuple-element.22), channel_id=1, source_target_pairs={{0,64},{16,80},{32,96},{48,112},{64,0},{80,16},{96,32},{112,48},{1... | collective-permute-start | bytes 1179656 | tf_op jit(solution)/shard_map/ppermute | solution.py:236
  125.9 0.7 fusion.3
  135.4 2.8 %copy-done.7 = bf16[8,64,3,2048]{3,1,2,0:T(8,128)(2,1)S(1)} copy-done((bf16[8,64,3,2048]{3,1,2,0:T(8,128)(2,1)S(1)}, bf16[8,64,3,2048]{3,1,2,0:T(8,128)(2,1)}, u32[]{:S(2)}) %copy-start.7) | copy-done | bytes 6291480
  138.2 0.9 prep.7
  139.0 1.1 copy-done.11
  144.6 0.1 collective-permute-start.1
  144.7 7.1 %all-to-all-start.5 = ((bf16[16,2,3,64,128]{4,3,2,1,0:T(8,128)(2,1)}), bf16[16,2,3,64,128]{4,3,2,1,0:T(8,128)(2,1)}, u32[]{:S(2)}, u32[]{:S(2)}) async-start(bf16[16,2,3,64,128]{4,3,2,1,0:T(8,128)(2,1)} %copy-done.11), calls=%async_computation.5 | async-start | bytes 3145728 | tf_op jit(solution)/shard_map/all_to_all | solution.py:224
  151.9 2.0 broadcast_in_dim.27
  153.9 1.8 bitcast_dynamic-update-slice_fusion.7
  155.7 4.6 %copy-done.1 = bf16[2048,3072]{1,0:T(8,128)(2,1)S(1)} copy-done((bf16[2048,3072]{1,0:T(8,128)(2,1)S(1)}, bf16[2048,3072]{1,0:T(8,128)(2,1)}, u32[]{:S(2)}) %copy-start.1) | copy-done | bytes 12582936
  160.3 6.2 %project.5 = (bf16[64,3072]{1,0:T(8,128)(2,1)}, bf16[64,3072]{1,0:T(8,128)(2,1)}) custom-call(s32[32]{0:T(128)S(1)} %copy-done.18, bf16[16,2,64,128]{3,2,1,0:T(8,128)(2,1)} %all-to-all-done.4.z_ref, bf16[2048,3072]{1,0:T(8,128)(2,1)S(1)} %copy-done.1, f32[50,3072]{1,0:T(8,128)S(1)} %copy-done.9, bf16[8,64,3072]{2,1,0:T(8,128)(2,1)S(1)} %copy-done.3, ...), custom_call_target="tpu_custom_call" | custom-call | flops 1610612736 | bytes 14155776 | tf_op jit(solution)/shard_map/project/pallas_call | solution.py:187
  166.4 1.1 collective-permute-start.2
  167.6 1.8 bitcast_dynamic-update-slice_fusion.6
  169.3 5.8 %attention.6 = bf16[16,2,64,128]{3,2,1,0:T(8,128)(2,1)S(1)} custom-call(s32[32]{0:T(128)S(1)} %copy-done.18, bf16[16,2,3,64,128]{4,3,2,1,0:T(8,128)(2,1)} %all-to-all-done.3.y_ref, f32[1,128]{1,0:T(1,128)S(1)} %bitcast.34, f32[1,128]{1,0:T(1,128)S(1)} %bitcast.38), custom_call_target="tpu_custom_call" | custom-call | flops 1073741824 | bytes 2097152 | tf_op jit(solution)/shard_map/attention/pallas_call | solution.py:141
  175.2 0.8 copy-done.16
  175.9 1.8 collective-permute-start.3
  177.7 1.4 all-to-all-done.5.y_ref
  179.1 5.6 %all-to-all-start.6 = ((bf16[16,2,64,128]{3,2,1,0:T(8,128)(2,1)}), bf16[16,2,64,128]{3,2,1,0:T(8,128)(2,1)}, u32[]{:S(2)}, u32[]{:S(2)}) async-start(bf16[16,2,64,128]{3,2,1,0:T(8,128)(2,1)} %copy-done.16), calls=%async_computation.6 | async-start | bytes 1048576 | tf_op jit(solution)/shard_map/all_to_all | solution.py:224
  184.7 1.8 bitcast_dynamic-update-slice_fusion.5
  186.4 8.7 %all-to-all-done.6.z_ref = bf16[16,2,64,128]{3,2,1,0:T(8,128)(2,1)} async-done(((bf16[16,2,64,128]{3,2,1,0:T(8,128)(2,1)}), bf16[16,2,64,128]{3,2,1,0:T(8,128)(2,1)}, u32[]{:S(2)}, u32[]{:S(2)}) %all-to-all-start.6) | async-done | bytes 524320 | tf_op jit(solution)/shard_map/all_to_all | solution.py:224
  195.1 4.6 %copy-done.2 = bf16[2048,3072]{1,0:T(8,128)(2,1)S(1)} copy-done((bf16[2048,3072]{1,0:T(8,128)(2,1)S(1)}, bf16[2048,3072]{1,0:T(8,128)(2,1)}, u32[]{:S(2)}) %copy-start.2) | copy-done | bytes 12582936
  199.7 1.1 copy-done.10
  200.8 6.1 %project.6 = (bf16[64,3072]{1,0:T(8,128)(2,1)}, bf16[64,3072]{1,0:T(8,128)(2,1)S(1)}) custom-call(s32[32]{0:T(128)S(1)} %copy-done.18, bf16[16,2,64,128]{3,2,1,0:T(8,128)(2,1)} %all-to-all-done.6.z_ref, bf16[2048,3072]{1,0:T(8,128)(2,1)S(1)} %copy-done.2, f32[50,3072]{1,0:T(8,128)S(1)} %copy-done.10, bf16[8,64,3072]{2,1,0:T(8,128)(2,1)S(1)} %copy-done.3, ...), custom_call_target="tpu_custom_call" | custom-call | flops 1610612736 | bytes 14155776 | tf_op jit(solution)/shard_map/project/pallas_call | solution.py:187
  206.9 1.5 collective-permute-start.4
  208.4 1.8 bitcast_dynamic-update-slice_fusion.4
  210.2 5.6 %attention.7 = bf16[16,2,64,128]{3,2,1,0:T(8,128)(2,1)S(1)} custom-call(s32[32]{0:T(128)S(1)} %copy-done.18, bf16[16,2,3,64,128]{4,3,2,1,0:T(8,128)(2,1)} %all-to-all-done.5.y_ref, f32[1,128]{1,0:T(1,128)S(1)} %bitcast.35, f32[1,128]{1,0:T(1,128)S(1)} %bitcast.39), custom_call_target="tpu_custom_call" | custom-call | flops 1073741824 | bytes 2097152 | tf_op jit(solution)/shard_map/attention/pallas_call | solution.py:141
  215.8 0.8 copy-done.15
  216.6 4.2 %all-to-all-start.7 = ((bf16[16,2,64,128]{3,2,1,0:T(8,128)(2,1)}), bf16[16,2,64,128]{3,2,1,0:T(8,128)(2,1)}, u32[]{:S(2)}, u32[]{:S(2)}) async-start(bf16[16,2,64,128]{3,2,1,0:T(8,128)(2,1)} %copy-done.15), calls=%async_computation.7 | async-start | bytes 1048576 | tf_op jit(solution)/shard_map/all_to_all | solution.py:224
  220.9 0.1 collective-permute-start.5
  221.0 1.8 bitcast_dynamic-update-slice_fusion.3
  222.7 7.4 %collective-permute-done.5 = bf16[64,3072]{1,0:T(8,128)(2,1)S(1)} collective-permute-done((bf16[64,3072]{1,0:T(8,128)(2,1)S(1)}, bf16[64,3072]{1,0:T(8,128)(2,1)S(1)}, u32[]{:S(2)}, u32[]{:S(2)}) %collective-permute-start.5) | collective-permute-done | bytes 393248 | tf_op jit(solution)/shard_map/ppermute | solution.py:236
  230.1 0.8 bitcast_dynamic-update-slice_fusion.2
  230.9 0.1 all-to-all-done.7
  231.0 8.6 %project.7 = (bf16[8,64,3072]{2,1,0:T(8,128)(2,1)}, bf16[64,3072]{1,0:T(8,128)(2,1)S(1)}) fusion(bf16[8,64,3072]{2,1,0:T(8,128)(2,1)} %bitcast_dynamic-update-slice_fusion.2, s32[]{:T(128)S(6)} %select_n.30, s32[32]{0:T(128)S(1)} %copy-done.18, bf16[16,2,64,128]{3,2,1,0:T(8,128)(2,1)} %all-to-all-done.7, bf16[2048,3072]{1,0:T(8,128)(2,1)} %w_ref.6, ...), kind=kCustom, calls=%fused_computation.1 | custom fusion | flops 1610612736 | bytes 17727620 | tf_op jit(solution)/shard_map/project/pallas_call | solution.py:187
  241.7 0.8 bitcast_dynamic-update-slice_fusion
  (30 shorter events, 0.1 us)
Async XLA Ops:
  1.3 2.8 %copy-start.4 = (bf16[8,64,3,2048]{3,1,2,0:T(8,128)(2,1)S(1)}, bf16[8,64,3,2048]{3,1,2,0:T(8,128)(2,1)}, u32[]{:S(2)}) copy-start(bf16[8,64,3,2048]{3,1,2,0:T(8,128)(2,1)} %param.9) | copy-start | bytes 18874372
  4.1 0.7 copy-start.17
  6.8 32.7 %all-to-all-start = ((bf16[16,2,3,64,128]{4,3,2,1,0:T(8,128)(2,1)}), bf16[16,2,3,64,128]{4,3,2,1,0:T(8,128)(2,1)}, u32[]{:S(2)}, u32[]{:S(2)}) async-start(bf16[16,2,3,64,128]{4,3,2,1,0:T(8,128)(2,1)} %prep.4), calls=%async_computation | async-start | bytes 3145728 | tf_op jit(solution)/shard_map/all_to_all | solution.py:224
  15.0 2.8 %copy-start.5 = (bf16[8,64,3,2048]{3,1,2,0:T(8,128)(2,1)S(1)}, bf16[8,64,3,2048]{3,1,2,0:T(8,128)(2,1)}, u32[]{:S(2)}) copy-start(bf16[8,64,3,2048]{3,1,2,0:T(8,128)(2,1)} %param.9) | copy-start | bytes 18874372
  19.8 24.1 %copy-start.18 = (s32[32]{0:T(128)S(1)}, s32[32]{0:T(128)}, u32[]{:S(2)}) copy-start(s32[32]{0:T(128)} %meta.1.meta_ref) | copy-start | bytes 388
  19.8 24.1 %copy-start.19 = (f32[128]{0:T(128)S(1)}, f32[128]{0:T(128)}, u32[]{:S(2)}) copy-start(f32[128]{0:T(128)} %param.15) | copy-start | bytes 1540
  19.8 24.2 %copy-start.20 = (f32[128]{0:T(128)S(1)}, f32[128]{0:T(128)}, u32[]{:S(2)}) copy-start(f32[128]{0:T(128)} %param.16) | copy-start | bytes 1540
  39.5 26.6 %all-to-all-start.1 = ((bf16[16,2,3,64,128]{4,3,2,1,0:T(8,128)(2,1)}), bf16[16,2,3,64,128]{4,3,2,1,0:T(8,128)(2,1)}, u32[]{:S(2)}, u32[]{:S(2)}) async-start(bf16[16,2,3,64,128]{4,3,2,1,0:T(8,128)(2,1)} %prep.5), calls=%async_computation.1 | async-start | bytes 3145728 | tf_op jit(solution)/shard_map/all_to_all | solution.py:224
  66.1 13.7 %all-to-all-start.2 = ((bf16[16,2,64,128]{3,2,1,0:T(8,128)(2,1)}), bf16[16,2,64,128]{3,2,1,0:T(8,128)(2,1)S(1)}, u32[]{:S(2)}, u32[]{:S(2)}) async-start(bf16[16,2,64,128]{3,2,1,0:T(8,128)(2,1)} %attention.4), calls=%async_computation.2 | async-start | bytes 1048576 | tf_op jit(solution)/shard_map/all_to_all | solution.py:224
  69.6 2.8 %copy-start.6 = (bf16[8,64,3,2048]{3,1,2,0:T(8,128)(2,1)S(1)}, bf16[8,64,3,2048]{3,1,2,0:T(8,128)(2,1)}, u32[]{:S(2)}) copy-start(bf16[8,64,3,2048]{3,1,2,0:T(8,128)(2,1)} %param.9) | copy-start | bytes 18874372
  79.8 0.8 copy-start.12
  80.6 26.1 %all-to-all-start.3 = ((bf16[16,2,3,64,128]{4,3,2,1,0:T(8,128)(2,1)}), bf16[16,2,3,64,128]{4,3,2,1,0:T(8,128)(2,1)}, u32[]{:S(2)}, u32[]{:S(2)}) async-start(bf16[16,2,3,64,128]{4,3,2,1,0:T(8,128)(2,1)} %prep.6), calls=%async_computation.3 | async-start | bytes 3145728 | tf_op jit(solution)/shard_map/all_to_all | solution.py:224
  85.0 25.9 %copy-start.3 = (bf16[8,64,3072]{2,1,0:T(8,128)(2,1)S(1)}, bf16[8,64,3072]{2,1,0:T(8,128)(2,1)}, u32[]{:S(2)}) copy-start(bf16[8,64,3072]{2,1,0:T(8,128)(2,1)} %refs_1_.6) | copy-start | bytes 9437188
  90.9 0.8 copy-start.14
  106.7 38.0 %all-to-all-start.4 = ((bf16[16,2,64,128]{3,2,1,0:T(8,128)(2,1)}), bf16[16,2,64,128]{3,2,1,0:T(8,128)(2,1)}, u32[]{:S(2)}, u32[]{:S(2)}) async-start(bf16[16,2,64,128]{3,2,1,0:T(8,128)(2,1)} %copy-done.14), calls=%async_computation.4 | async-start | bytes 1048576 | tf_op jit(solution)/shard_map/all_to_all | solution.py:224
  110.9 4.6 %copy-start = (bf16[2048,3072]{1,0:T(8,128)(2,1)S(1)}, bf16[2048,3072]{1,0:T(8,128)(2,1)}, u32[]{:S(2)}) copy-start(bf16[2048,3072]{1,0:T(8,128)(2,1)} %w_ref.6) | copy-start | bytes 37748740
  115.5 1.1 copy-start.8
  116.6 1.0 copy-start.13
  122.9 29.0 %collective-permute-start = (bf16[64,3072]{1,0:T(8,128)(2,1)}, bf16[64,3072]{1,0:T(8,128)(2,1)}, u32[]{:S(2)}, u32[]{:S(2)}) collective-permute-start(bf16[64,3072]{1,0:T(8,128)(2,1)} %get-tuple-element.22), channel_id=1, source_target_pairs={{0,64},{16,80},{32,96},{48,112},{64,0},{80,16},{96,32},{112,48},{1... | collective-permute-start | bytes 1179656 | tf_op jit(solution)/shard_map/ppermute | solution.py:236
  135.4 2.8 %copy-start.7 = (bf16[8,64,3,2048]{3,1,2,0:T(8,128)(2,1)S(1)}, bf16[8,64,3,2048]{3,1,2,0:T(8,128)(2,1)}, u32[]{:S(2)}) copy-start(bf16[8,64,3,2048]{3,1,2,0:T(8,128)(2,1)} %param.9) | copy-start | bytes 18874372
  139.0 1.2 copy-start.11
  144.6 23.0 %collective-permute-start.1 = (bf16[64,3072]{1,0:T(8,128)(2,1)S(1)}, bf16[64,3072]{1,0:T(8,128)(2,1)}, u32[]{:S(2)}, u32[]{:S(2)}) collective-permute-start(bf16[64,3072]{1,0:T(8,128)(2,1)S(1)} %get-tuple-element.23), channel_id=1, source_target_pairs={{0,80},{16,64},{32,112},{48,96},{64,16},{80,0},{96,48},{112,32},{1... | collective-permute-start | bytes 1179656 | tf_op jit(solution)/shard_map/ppermute | solution.py:236
  144.7 34.4 %all-to-all-start.5 = ((bf16[16,2,3,64,128]{4,3,2,1,0:T(8,128)(2,1)}), bf16[16,2,3,64,128]{4,3,2,1,0:T(8,128)(2,1)}, u32[]{:S(2)}, u32[]{:S(2)}) async-start(bf16[16,2,3,64,128]{4,3,2,1,0:T(8,128)(2,1)} %copy-done.11), calls=%async_computation.5 | async-start | bytes 3145728 | tf_op jit(solution)/shard_map/all_to_all | solution.py:224
  151.9 3.8 %copy-start.9 = (f32[50,3072]{1,0:T(8,128)S(1)}, f32[50,3072]{1,0:T(8,128)}, u32[]{:S(2)}) copy-start(f32[50,3072]{1,0:T(8,128)} %gate_ref.6) | copy-start | bytes 1843204
  155.7 4.6 %copy-start.1 = (bf16[2048,3072]{1,0:T(8,128)(2,1)S(1)}, bf16[2048,3072]{1,0:T(8,128)(2,1)}, u32[]{:S(2)}) copy-start(bf16[2048,3072]{1,0:T(8,128)(2,1)} %w_ref.6) | copy-start | bytes 37748740
  166.4 18.2 %collective-permute-start.2 = (bf16[64,3072]{1,0:T(8,128)(2,1)}, bf16[64,3072]{1,0:T(8,128)(2,1)}, u32[]{:S(2)}, u32[]{:S(2)}) collective-permute-start(bf16[64,3072]{1,0:T(8,128)(2,1)} %get-tuple-element.26), channel_id=1, source_target_pairs={{0,96},{16,112},{32,64},{48,80},{64,32},{80,48},{96,0},{112,16},{1... | collective-permute-start | bytes 1179656 | tf_op jit(solution)/shard_map/ppermute | solution.py:236
  175.1 0.8 copy-start.16
  175.9 32.5 %collective-permute-start.3 = (bf16[64,3072]{1,0:T(8,128)(2,1)}, bf16[64,3072]{1,0:T(8,128)(2,1)}, u32[]{:S(2)}, u32[]{:S(2)}) collective-permute-start(bf16[64,3072]{1,0:T(8,128)(2,1)} %get-tuple-element.27), channel_id=1, source_target_pairs={{0,112},{16,96},{32,80},{48,64},{64,48},{80,32},{96,16},{112,0},{1... | collective-permute-start | bytes 1179656 | tf_op jit(solution)/shard_map/ppermute | solution.py:236
  179.1 16.0 %all-to-all-start.6 = ((bf16[16,2,64,128]{3,2,1,0:T(8,128)(2,1)}), bf16[16,2,64,128]{3,2,1,0:T(8,128)(2,1)}, u32[]{:S(2)}, u32[]{:S(2)}) async-start(bf16[16,2,64,128]{3,2,1,0:T(8,128)(2,1)} %copy-done.16), calls=%async_computation.6 | async-start | bytes 1048576 | tf_op jit(solution)/shard_map/all_to_all | solution.py:224
  195.1 4.6 %copy-start.2 = (bf16[2048,3072]{1,0:T(8,128)(2,1)S(1)}, bf16[2048,3072]{1,0:T(8,128)(2,1)}, u32[]{:S(2)}) copy-start(bf16[2048,3072]{1,0:T(8,128)(2,1)} %w_ref.6) | copy-start | bytes 37748740
  199.7 1.1 copy-start.10
  206.9 14.1 %collective-permute-start.4 = (bf16[64,3072]{1,0:T(8,128)(2,1)}, bf16[64,3072]{1,0:T(8,128)(2,1)}, u32[]{:S(2)}, u32[]{:S(2)}) collective-permute-start(bf16[64,3072]{1,0:T(8,128)(2,1)} %get-tuple-element.30), channel_id=1, source_target_pairs={{0,32},{16,48},{32,0},{48,16},{64,96},{80,112},{96,64},{112,80},{1... | collective-permute-start | bytes 1179656 | tf_op jit(solution)/shard_map/ppermute | solution.py:236
  215.8 0.8 copy-start.15
  216.6 14.4 %all-to-all-start.7 = ((bf16[16,2,64,128]{3,2,1,0:T(8,128)(2,1)}), bf16[16,2,64,128]{3,2,1,0:T(8,128)(2,1)}, u32[]{:S(2)}, u32[]{:S(2)}) async-start(bf16[16,2,64,128]{3,2,1,0:T(8,128)(2,1)} %copy-done.15), calls=%async_computation.7 | async-start | bytes 1048576 | tf_op jit(solution)/shard_map/all_to_all | solution.py:224
  220.9 9.3 %collective-permute-start.5 = (bf16[64,3072]{1,0:T(8,128)(2,1)S(1)}, bf16[64,3072]{1,0:T(8,128)(2,1)S(1)}, u32[]{:S(2)}, u32[]{:S(2)}) collective-permute-start(bf16[64,3072]{1,0:T(8,128)(2,1)S(1)} %get-tuple-element.31), channel_id=1, source_target_pairs={{0,48},{16,32},{32,16},{48,0},{64,112},{80,96},{96,80},{112,64},{1... | collective-permute-start | bytes 1179656 | tf_op jit(solution)/shard_map/ppermute | solution.py:236
  239.6 2.0 collective-permute-start.6

commit v2 on v1

v2 whole, which is shorter than its diff:
```python
import math

import jax
import jax.numpy as jnp
from jax import lax
from jax.experimental import pallas as pl
from jax.experimental.pallas import tpu as pltpu
from jax.sharding import Mesh
from jax.sharding import PartitionSpec as P

HEADS = 16
HD = 128
CG = 8
TILE = 256
SCALE = math.log2(math.e) / math.sqrt(HD)
CORES = 2
SOURCE, LENGTH, ORIGIN, SLOT, STEP = (i * CG for i in range(5))


def params(mib):
    return pltpu.CompilerParams(vmem_limit_bytes=mib * 2**20)


def cost(flops, moved):
    return pl.CostEstimate(flops=flops, bytes_accessed=moved, transcendentals=0)


def in_vmem(array):
    return pltpu.with_memory_space_constraint(array, pltpu.VMEM)


def in_hbm(array):
    return pltpu.with_memory_space_constraint(array, pltpu.HBM)


def meta_kernel(group_ref, length_ref, step_ref, slot_ref, meta_ref):
    group = group_ref[0]
    core = group & (CORES - 1)
    for i in range(CG):
        meta_ref[SOURCE + lax.shift_right_logical(slot_ref[group * CG + i], 3)] = i
        meta_ref[ORIGIN + i] = group ^ i
    for c in range(CORES):
        for i in range(CG):
            clip = ((group & ~(CORES - 1)) + c) * CG + i
            target = lax.shift_right_logical(slot_ref[clip], 3)

            @pl.when((target & (CORES - 1)) == core)
            def _(c=c, clip=clip, target=target):
                at = LENGTH + c * (CG // CORES) + lax.shift_right_logical(target, 1)
                meta_ref[at] = length_ref[clip]

    for clip in range(slot_ref.shape[0]):
        slot = slot_ref[clip]

        @pl.when(lax.shift_right_logical(slot, 3) == group)
        def _(slot=slot, clip=clip):
            k = (clip // CG) ^ group
            meta_ref[SLOT + k] = slot & 7
            meta_ref[STEP + k] = step_ref[clip]


def make_meta(group, lengths, t_index, slot_target):
    smem = pl.BlockSpec(memory_space=pltpu.SMEM)
    return pl.pallas_call(
        meta_kernel,
        out_shape=jax.ShapeDtypeStruct((5 * CG,), jnp.int32),
        in_specs=[smem] * 4,
        out_specs=smem,
        name="meta",
    )(group, lengths, t_index, slot_target)


def prep_kernel(meta_ref, x_ref, o_ref, held_ref, in_sems, out_sems):
    def arriving(d, h):
        source = x_ref.at[meta_ref[SOURCE + d], :, :, pl.ds(h * HD, HD)]
        return pltpu.make_async_copy(source, held_ref.at[d, h], in_sems.at[d, h])

    def leaving(d):
        return pltpu.make_async_copy(
            held_ref.at[d], o_ref.at[:, d % CORES, d // CORES], out_sems.at[d]
        )

    for d in range(CG):
        for h in range(HEADS):
            arriving(d, h).start()
    for d in range(CG):
        for h in range(HEADS):
            arriving(d, h).wait()
        leaving(d).start()
    for d in range(CG):
        leaving(d).wait()


def prep(meta, x):
    clips, _, rows, _ = x.shape
    anywhere = pl.BlockSpec(memory_space=pl.ANY)
    return pl.pallas_call(
        prep_kernel,
        in_specs=[pl.BlockSpec(memory_space=pltpu.SMEM), anywhere],
        out_specs=anywhere,
        out_shape=pltpu.HBM((HEADS, CORES, clips // CORES, 3, rows, HD), jnp.bfloat16),
        scratch_shapes=[
            pltpu.VMEM((clips, HEADS, 3, rows, HD), jnp.bfloat16),
            pltpu.SemaphoreType.DMA((clips, HEADS)),
            pltpu.SemaphoreType.DMA((clips,)),
        ],
        compiler_params=params(12),
        cost_estimate=cost(0, 4 * math.prod(x.shape)),
        name="prep",
    )(meta, in_hbm(x))


def spread_kernel(meta_ref, tokens_ref, *out_refs):
    for k in range(CG):

        @pl.when(pl.program_id(0) == k)
        def _(k=k):
            out_refs[k][...] = tokens_ref[0]


def spread(meta, tokens):
    rows, width = tokens.shape[1:]
    return pl.pallas_call(
        spread_kernel,
        grid_spec=pltpu.PrefetchScalarGridSpec(
            num_scalar_prefetch=1,
            grid=(CG,),
            in_specs=[
                pl.BlockSpec((1, rows, width), lambda k, m: (m[SOURCE + m[ORIGIN + k]], 0, 0))
            ],
            out_specs=[pl.BlockSpec((rows, width), lambda k, m: (0, 0))] * CG,
        ),
        out_shape=[pltpu.HBM((rows, width), tokens.dtype)] * CG,
        compiler_params=params(12),
        cost_estimate=cost(0, 4 * math.prod(tokens.shape)),
        name="spread",
    )(meta, in_hbm(tokens))


def inverse_root(wide):
    square = wide * wide
    high = square.astype(jnp.bfloat16)
    low = (square - high.astype(jnp.float32)).astype(jnp.bfloat16)
    ones = jnp.ones((2 * HD, HD), jnp.bfloat16)
    total = jnp.dot(
        jnp.concatenate([high, low], axis=1), ones, preferred_element_type=jnp.float32
    )
    return lax.rsqrt(total * (1.0 / HD) + 1e-06)


def attend(n, length, y_ref, gain, o_ref, root_ref, k_ref, v_ref):
    blocks, rows = y_ref.shape[0], y_ref.shape[4]
    per_tile = TILE // rows

    def tile(t, part):
        return y_ref[t * per_tile : (t + 1) * per_tile, 0, 0, part].reshape(TILE, HD)

    row = (n - 1) * TILE + lax.broadcasted_iota(jnp.int32, (TILE, HD), 0)
    live = row < length
    for t in range(n):
        to = slice(t * TILE, (t + 1) * TILE)
        root_ref[to] = inverse_root(tile(t, 0).astype(jnp.float32)) * SCALE
        wide = tile(t, 1).astype(jnp.float32)
        k_ref[to] = (wide * inverse_root(wide) * gain).astype(jnp.bfloat16)
        if t < n - 1:
            v_ref[to, :HD] = tile(t, 2)
            v_ref[to, HD:] = jnp.ones((TILE, HD), jnp.bfloat16)
        else:
            factor = jnp.where(live, 1.0, 0.0).astype(jnp.bfloat16)
            v_ref[to, :HD] = tile(t, 2) * factor
            v_ref[to, HD:] = factor
    for t in range(n):
        scores = lax.dot_general(
            tile(t, 0),
            k_ref[: n * TILE],
            (((1,), (1,)), ((), ())),
            preferred_element_type=jnp.float32,
        )
        root = root_ref[t * TILE : (t + 1) * TILE]
        raised = jnp.concatenate(
            [
                jnp.exp2(scores[:, i : i + HD] * root).astype(jnp.bfloat16)
                for i in range(0, n * TILE, HD)
            ],
            axis=1,
        )
        summed = jnp.dot(raised, v_ref[: n * TILE], preferred_element_type=jnp.float32)
        result = summed[:, :HD] / summed[:, HD:]
        if t == n - 1:
            result = jnp.where(live, result, 0.0)
        o_ref[0, t * per_tile : (t + 1) * per_tile, 0] = result.astype(jnp.bfloat16).reshape(
            per_tile, rows, HD
        )
    if n * per_tile < blocks:
        o_ref[0, n * per_tile :, 0] = jnp.zeros((blocks - n * per_tile, rows, HD), jnp.bfloat16)


def attention(meta, y, q_gain, k_gain):
    blocks, cores, count, parts, rows, _ = y.shape
    total = blocks * rows

    def kernel(meta_ref, y_ref, qg_ref, kg_ref, o_ref, *scratch):
        length = meta_ref[LENGTH + pl.program_id(0) * count + pl.program_id(1)]
        live_tiles = lax.div(length + (TILE - 1), TILE)
        gain = qg_ref[...] * kg_ref[...]
        for n in range(1, total // TILE + 1):

            @pl.when(live_tiles == n)
            def _(n=n):
                attend(n, length, y_ref, gain, o_ref, *scratch)

    return pl.pallas_call(
        kernel,
        grid_spec=pltpu.PrefetchScalarGridSpec(
            num_scalar_prefetch=1,
            grid=(cores, count),
            in_specs=[
                pl.BlockSpec((blocks, 1, 1, parts, rows, HD), lambda c, j, m: (0, c, j, 0, 0, 0)),
                pl.BlockSpec((1, HD), lambda c, j, m: (0, 0)),
                pl.BlockSpec((1, HD), lambda c, j, m: (0, 0)),
            ],
            out_specs=pl.BlockSpec((1, blocks, 1, rows, HD), lambda c, j, m: (j, 0, c, 0, 0)),
            scratch_shapes=[
                pltpu.VMEM((total, HD), jnp.float32),
                pltpu.VMEM((total, HD), jnp.bfloat16),
                pltpu.VMEM((total, 2 * HD), jnp.bfloat16),
            ],
        ),
        out_shape=pltpu.HBM((count, blocks, cores, rows, HD), jnp.bfloat16),
        compiler_params=params(24),
        cost_estimate=cost(
            cores * count * 4 * total * total * HD, cores * count * total * HD * 8
        ),
        name="attention",
    )(meta, in_hbm(y), q_gain, k_gain)


def project(meta, z, out_weight, gate_table, tokens):
    rows, width = tokens[0].shape
    clips, block = len(tokens), 512
    steps = width // block

    def kernel(meta_ref, z_ref, weight_ref, gate_ref, *refs):
        token_refs, (out_ref, a_ref, w_ref, sems) = refs[:clips], refs[clips:]

        def arriving(n):
            columns = pl.ds(n * block, block)
            return pltpu.make_async_copy(weight_ref.at[:, columns], w_ref.at[n], sems.at[n])

        @pl.when(pl.program_id(0) == 0)
        def _():
            for n in range(steps):
                arriving(n).start()
            for k in range(clips):
                origin = meta_ref[ORIGIN + k]
                x, core = lax.shift_right_logical(origin, 1), origin & (CORES - 1)
                for h in range(HEADS):
                    a_ref[k * rows : (k + 1) * rows, h * HD : (h + 1) * HD] = z_ref[x, h, core]

        for n in range(steps):

            @pl.when(pl.program_id(0) == n)
            def _(n=n):
                arriving(n).wait()

        projected = jnp.dot(
            a_ref[...], w_ref[pl.program_id(0)], preferred_element_type=jnp.float32
        )
        for k in range(clips):
            gate = gate_ref[pl.ds(meta_ref[STEP + k], 1), :]
            part = gate * projected[k * rows : (k + 1) * rows]
            out_ref[meta_ref[SLOT + k]] = (token_refs[k][...].astype(jnp.float32) + part).astype(
                jnp.bfloat16
            )

    return pl.pallas_call(
        kernel,
        grid_spec=pltpu.PrefetchScalarGridSpec(
            num_scalar_prefetch=1,
            grid=(steps,),
            in_specs=[
                pl.BlockSpec(memory_space=pltpu.VMEM),
                pl.BlockSpec(memory_space=pl.ANY),
                pl.BlockSpec((gate_table.shape[0], block), lambda n, m: (0, n)),
            ]
            + [pl.BlockSpec((rows, block), lambda n, m: (0, n))] * clips,
            out_specs=pl.BlockSpec((clips, rows, block), lambda n, m: (0, 0, n)),
            scratch_shapes=[
                pltpu.VMEM((clips * rows, HEADS * HD), jnp.bfloat16),
                pltpu.VMEM((steps, HEADS * HD, block), jnp.bfloat16),
                pltpu.SemaphoreType.DMA((steps,)),
            ],
        ),
        out_shape=pltpu.HBM((clips, rows, width), jnp.bfloat16),
        compiler_params=params(40),
        cost_estimate=cost(
            2 * clips * rows * HEADS * HD * width,
            2 * HEADS * HD * width + 4 * clips * rows * width,
        ),
        name="project",
    )(
        meta,
        in_vmem(z),
        in_hbm(out_weight),
        in_hbm(gate_table),
        *[in_hbm(part) for part in tokens],
    )


def per_device(qkv, tokens, lengths, t_index, slot_target, gate_table, q_gain, k_gain, out_weight):
    group = lax.axis_index(("x", "core"))
    meta = make_meta(group.reshape(1), lengths, t_index, slot_target)

    def across(part, k):
        pairs = [(g, g ^ k) for g in range(CG)]
        return lax.ppermute(part, ("x", "core"), pairs) if k else part

    def exchange(array, axes, kept):
        sent = array.reshape(-1, *array.shape[kept:])
        arrived = lax.all_to_all(sent, axes, split_axis=0, concat_axis=0, tiled=True)
        return arrived.reshape(array.shape)

    y = exchange(prep(meta, jnp.swapaxes(qkv, 1, 2)), ("z", "y", "core"), 2)
    resid = [across(part, k) for k, part in enumerate(spread(meta, tokens))]
    y, *resid = lax.optimization_barrier((y, *resid))
    attended = attention(meta, y, q_gain.reshape(1, HD), k_gain.reshape(1, HD))
    z = exchange(attended, ("x", "z", "y"), 2)
    return project(meta, z, out_weight, gate_table, resid)


def solution(mesh):
    apart = Mesh(mesh.devices.reshape(CG // CORES, CORES, 4, 4), ("x", "core", "z", "y"))
    clips, tokens = ("x", "core"), ("z", "y")
    return jax.shard_map(
        per_device,
        mesh=apart,
        in_specs=(
            P(clips, tokens, None, None),
            P(clips, tokens, None),
            P(),
            P(),
            P(),
            P(),
            P(),
            P(),
            P(),
        ),
        out_specs=P(clips, tokens, None),
        check_vma=False,
    )
```

time: 246 us -> 159 us (0.65); the launches traced: 242 us -> 159 us
  local copies, waits for them, and re-layouts: 46.3 us -> 0.65 us
  blocking collectives: 0 us -> 39 us
  starting transfers between devices: 49.4 us -> 17.9 us
  between operations: 15.5 us -> 0.11 us
  waiting for transfers between devices: 73.2 us -> 61.9 us
  Pallas kernels: 49.4 us -> 39.2 us
  other arithmetic: 8.61 us -> 0 us
    all_to_all x0 -> x1, blocking collectives: none -> 39 us  [exchange(): lax.all_to_all(sent, axes, split_axis=0, concat_axis=0, tiled=True)]
    all_to_all x8 -> x1, waiting for transfers between devices: 65.9 us -> 28.6 us  [exchange(): lax.all_to_all(sent, axes, split_axis=0, concat_axis=0, tiled=True)]
    all_to_all x8 -> x1, starting transfers between devices: 41.8 us -> 8.54 us  [exchange(): lax.all_to_all(sent, axes, split_axis=0, concat_axis=0, tiled=True)]
    unnamed x42 -> x22, local copies, waits for them, and re-layouts: 33.2 us -> 0.65 us
    ppermute x7, waiting for transfers between devices: 7.39 us -> 33.3 us  [across(): return lax.ppermute(part, ('x', 'core'), pairs) if k else part]
    dynamic_update_slice x7 -> x0, local copies, waits for them, and re-layouts: 10.4 us -> none  [finish(): out = lax.dynamic_update_slice(out, result[None], (meta[3 * CG + k], 0, 0))]
    pallas_call x12 -> x5, Pallas kernels: 49.4 us -> 39.2 us  [the longest x1 12.9 us: project(): pl.pallas_call(kernel, grid_spec=pltpu.PrefetchScalarGridSpec(num_scalar_...]
    pallas_call x1 -> x0, other arithmetic: 8.61 us -> none  [project(): pl.pallas_call(functools.partial(project_kernel, first, count), grid_spec...]
  transfers between devices with their start and end apart: 15 -> 8, of which waited for: 8 -> 6; matrix products, arithmetic and copies ran while one was open for 5% -> 0% of each run, Pallas kernels for 19% -> 4%
where the time goes in v2:
time: 159 us
  waiting for transfers between devices  61.9 us (39%)
  Pallas kernels  39.2 us (25%)
  blocking collectives  39 us (25%)
  starting transfers between devices  17.9 us (11%)
    all_to_all x1, blocking collectives, exchange(): lax.all_to_all(sent, axes, split_axis=0, concat_axis=0, tiled=True)  39 us
    ppermute x7, waiting for transfers between devices, across(): return lax.ppermute(part, ('x', 'core'), pairs) if k else part  33.3 us
    all_to_all x1, waiting for transfers between devices, exchange(): lax.all_to_all(sent, axes, split_axis=0, concat_axis=0, tiled=True)  28.6 us
    pallas_call x1, Pallas kernels, project(): pl.pallas_call(kernel, grid_spec=pltpu.PrefetchScalarGridSpec(num_scalar_...  12.9 us
    pallas_call x1, Pallas kernels, attention(): pl.pallas_call(kernel, grid_spec=pltpu.PrefetchScalarGridSpec(num_scalar_...  11.1 us
    ppermute x7, starting transfers between devices, across(): return lax.ppermute(part, ('x', 'core'), pairs) if k else part  9.31 us
    all_to_all x1, starting transfers between devices, exchange(): lax.all_to_all(sent, axes, split_axis=0, concat_axis=0, tiled=True)  8.54 us
    pallas_call x1, Pallas kernels, prep(): pl.pallas_call(prep_kernel, in_specs=[pl.BlockSpec(memory_space=pltpu.SME...  7.1 us
  transfers between devices with their start and end apart: 8, of which 6 were waited for; matrix products, arithmetic and copies ran while one was open for 0% of the time, Pallas kernels for 4%

profile of v2, /device:TPU:0, one launch (start us, length us, event | category | flops | bytes accessed | tf_op | source)
XLA Modules:
  0.0 158.7 jit_solution(8531519885355833742)
XLA Ops:
  0.0 1.4 meta.1.meta_ref
  1.4 0.0 copy-start
  1.4 0.6 copy-done
  2.0 7.1 %prep.1 = bf16[16,2,4,3,64,128]{5,4,3,2,1,0:T(8,128)(2,1)} custom-call(s32[40]{0:T(128)S(1)} %copy-done, bf16[8,3,64,2048]{3,2,1,0:T(8,128)(2,1)} %bitcast.12), custom_call_target="tpu_custom_call" | custom-call | bytes 12582912 | tf_op jit(solution)/shard_map/prep/pallas_call | solution.py:97
  9.1 0.0 copy-start.1
  9.1 0.0 copy-start.2
  9.2 0.0 copy-start.3
  9.2 8.5 %all-to-all-start = ((bf16[32,4,3,64,128]{4,3,2,1,0:T(8,128)(2,1)}), bf16[32,4,3,64,128]{4,3,2,1,0:T(8,128)(2,1)}, u32[]{:S(2)}, u32[]{:S(2)}) async-start(bf16[32,4,3,64,128]{4,3,2,1,0:T(8,128)(2,1)} %bitcast.11), calls=%async_computation | async-start | bytes 12582912 | tf_op jit(solution)/shard_map/all_to_all | solution.py:320
  17.7 0.0 copy-done.1
  17.7 6.7 %spread.1 = (bf16[64,3072]{1,0:T(8,128)(2,1)}, bf16[64,3072]{1,0:T(8,128)(2,1)}, bf16[64,3072]{1,0:T(8,128)(2,1)}, bf16[64,3072]{1,0:T(8,128)(2,1)}, bf16[64,307...) custom-call(s32[40]{0:T(128)S(1)} %copy-done.1, ...), custom_call_target="tpu_custom_call" | custom-call | bytes 6291456 | tf_op jit(solution)/shard_map/spread/pallas_call | solution.py:123
  24.4 0.2 collective-permute-start
  24.6 1.5 collective-permute-start.1
  26.1 0.2 collective-permute-start.2
  26.3 3.0 %collective-permute-start.3 = (bf16[64,3072]{1,0:T(8,128)(2,1)}, bf16[64,3072]{1,0:T(8,128)(2,1)S(1)}, u32[]{:S(2)}, u32[]{:S(2)}) collective-permute-start(bf16[64,3072]{1,0:T(8,128)(2,1)} %get-tuple-element.26), channel_id=1, source_target_pairs={{0,64},{16,80},{32,96},{48,112},{64,0},{80,16},{96,32},{112,48},{1... | collective-permute-start | bytes 1179656 | tf_op jit(solution)/shard_map/ppermute | solution.py:316
  29.3 0.3 collective-permute-start.4
  29.6 0.0 collective-permute-done.refs_1_
  29.6 0.0 copy-start.4
  29.6 2.8 %collective-permute-start.5 = (bf16[64,3072]{1,0:T(8,128)(2,1)}, bf16[64,3072]{1,0:T(8,128)(2,1)S(1)}, u32[]{:S(2)}, u32[]{:S(2)}) collective-permute-start(bf16[64,3072]{1,0:T(8,128)(2,1)} %get-tuple-element.28), channel_id=1, source_target_pairs={{0,96},{16,112},{32,64},{48,80},{64,32},{80,48},{96,0},{112,16},{1... | collective-permute-start | bytes 1179656 | tf_op jit(solution)/shard_map/ppermute | solution.py:316
  32.4 4.4 %collective-permute-done.1.refs_2_ = bf16[64,3072]{1,0:T(8,128)(2,1)S(1)} collective-permute-done((bf16[64,3072]{1,0:T(8,128)(2,1)}, bf16[64,3072]{1,0:T(8,128)(2,1)S(1)}, u32[]{:S(2)}, u32[]{:S(2)}) %collective-permute-start.1) | collective-permute-done | bytes 393248 | tf_op jit(solution)/shard_map/ppermute | solution.py:316
  36.7 0.0 copy-start.5
  36.7 1.3 collective-permute-start.6
  38.1 6.2 %collective-permute-done.2.refs_3_ = bf16[64,3072]{1,0:T(8,128)(2,1)S(1)} collective-permute-done((bf16[64,3072]{1,0:T(8,128)(2,1)}, bf16[64,3072]{1,0:T(8,128)(2,1)S(1)}, u32[]{:S(2)}, u32[]{:S(2)}) %collective-permute-start.2) | collective-permute-done | bytes 393248 | tf_op jit(solution)/shard_map/ppermute | solution.py:316
  44.3 0.0 copy-start.6
  44.3 11.6 %collective-permute-done.3.refs_4_ = bf16[64,3072]{1,0:T(8,128)(2,1)S(1)} collective-permute-done((bf16[64,3072]{1,0:T(8,128)(2,1)}, bf16[64,3072]{1,0:T(8,128)(2,1)S(1)}, u32[]{:S(2)}, u32[]{:S(2)}) %collective-permute-start.3) | collective-permute-done | bytes 393248 | tf_op jit(solution)/shard_map/ppermute | solution.py:316
  55.9 0.0 copy-start.7
  55.9 7.2 %collective-permute-done.4.refs_5_ = bf16[64,3072]{1,0:T(8,128)(2,1)S(1)} collective-permute-done((bf16[64,3072]{1,0:T(8,128)(2,1)}, bf16[64,3072]{1,0:T(8,128)(2,1)S(1)}, u32[]{:S(2)}, u32[]{:S(2)}) %collective-permute-start.4) | collective-permute-done | bytes 393248 | tf_op jit(solution)/shard_map/ppermute | solution.py:316
  63.1 0.0 copy-start.8
  63.1 0.0 collective-permute-done.5.refs_6_
  63.1 0.0 copy-start.9
  63.1 3.9 %collective-permute-done.6.refs_7_ = bf16[64,3072]{1,0:T(8,128)(2,1)S(1)} collective-permute-done((bf16[64,3072]{1,0:T(8,128)(2,1)}, bf16[64,3072]{1,0:T(8,128)(2,1)S(1)}, u32[]{:S(2)}, u32[]{:S(2)}) %collective-permute-start.6) | collective-permute-done | bytes 393248 | tf_op jit(solution)/shard_map/ppermute | solution.py:316
  67.0 0.0 copy-start.10
  67.0 28.6 %all-to-all-done = bf16[32,4,3,64,128]{4,3,2,1,0:T(8,128)(2,1)} async-done(((bf16[32,4,3,64,128]{4,3,2,1,0:T(8,128)(2,1)}), bf16[32,4,3,64,128]{4,3,2,1,0:T(8,128)(2,1)}, u32[]{:S(2)}, u32[]{:S(2)}) %all-to-all-start) | async-done | bytes 6291488 | tf_op jit(solution)/shard_map/all_to_all | solution.py:320
  95.6 0.0 copy-done.2
  95.6 0.0 copy-done.3
  95.6 11.1 %attention.1 = bf16[4,16,2,64,128]{4,3,2,1,0:T(8,128)(2,1)} custom-call(s32[40]{0:T(128)S(1)} %copy-done.1, bf16[16,2,4,3,64,128]{5,4,3,2,1,0:T(8,128)(2,1)} %bitcast.3.y_ref, f32[1,128]{1,0:T(1,128)S(1)} %bitcast.9, f32[1,128]{1,0:T(1,128)S(1)} %bitcast.10), custom_call_target="tpu_custom_call" | custom-call | flops 4294967296 | bytes 8388608 | tf_op jit(solution)/shard_map/attention/pallas_call | solution.py:212
  106.7 0.0 copy-done.4
  106.7 0.0 copy-done.5
  106.7 0.0 copy-done.6
  106.7 0.0 copy-done.7
  106.8 0.0 copy-done.8
  106.8 0.0 copy-done.9
  106.8 0.0 copy-done.10
  106.8 39.0 %all_to_all.10 = bf16[64,2,64,128]{3,2,1,0:T(8,128)(2,1)S(1)} all-to-all(bf16[64,2,64,128]{3,2,1,0:T(8,128)(2,1)} %bitcast.13), channel_id=1, replica_groups=mesh['x'=4,'core'=2,'z'=4,'y'=4] {'x','z','y'}, dimensions={0} | all-to-all | bytes 4194304 | tf_op jit(solution)/shard_map/all_to_all | solution.py:320
  145.8 12.9 %project.1 = bf16[8,64,3072]{2,1,0:T(8,128)(2,1)} custom-call(s32[40]{0:T(128)S(1)} %copy-done.1, bf16[4,16,2,64,128]{4,3,2,1,0:T(8,128)(2,1)S(1)} %bitcast.8, bf16[2048,3072]{1,0:T(8,128)(2,1)} %weight_ref.1, f32[50,3072]{1,0:T(8,128)} %gate_ref.1, bf16[64,3072]{1,0:T(8,128)(2,1)} %get-tuple-element.31.refs_0_, bf16[64,3072]{1,0:T(8,128)(2,1)} %copy-done.4, ...), custom_call_target="tpu_custom_call" | custom-call | flops 6442450944 | bytes 18874368 | tf_op jit(solution)/shard_map/project/pallas_call | solution.py:276
Async XLA Ops:
  1.4 0.6 copy-start
  9.1 8.6 %copy-start.1 = (s32[40]{0:T(128)S(1)}, s32[40]{0:T(128)}, u32[]{:S(2)}) copy-start(s32[40]{0:T(128)} %meta.1.meta_ref) | copy-start | bytes 484
  9.1 86.5 %copy-start.2 = (f32[128]{0:T(128)S(1)}, f32[128]{0:T(128)}, u32[]{:S(2)}) copy-start(f32[128]{0:T(128)} %param.15) | copy-start | bytes 1540
  9.2 86.4 %copy-start.3 = (f32[128]{0:T(128)S(1)}, f32[128]{0:T(128)}, u32[]{:S(2)}) copy-start(f32[128]{0:T(128)} %param.16) | copy-start | bytes 1540
  9.2 86.4 %all-to-all-start = ((bf16[32,4,3,64,128]{4,3,2,1,0:T(8,128)(2,1)}), bf16[32,4,3,64,128]{4,3,2,1,0:T(8,128)(2,1)}, u32[]{:S(2)}, u32[]{:S(2)}) async-start(bf16[32,4,3,64,128]{4,3,2,1,0:T(8,128)(2,1)} %bitcast.11), calls=%async_computation | async-start | bytes 12582912 | tf_op jit(solution)/shard_map/all_to_all | solution.py:320
  24.4 5.2 %collective-permute-start = (bf16[64,3072]{1,0:T(8,128)(2,1)}, bf16[64,3072]{1,0:T(8,128)(2,1)S(1)}, u32[]{:S(2)}, u32[]{:S(2)}) collective-permute-start(bf16[64,3072]{1,0:T(8,128)(2,1)} %get-tuple-element.23), channel_id=1, source_target_pairs={{0,16},{16,0},{32,48},{48,32},{64,80},{80,64},{96,112},{112,96},{1... | collective-permute-start | bytes 1179656 | tf_op jit(solution)/shard_map/ppermute | solution.py:316
  24.6 12.1 %collective-permute-start.1 = (bf16[64,3072]{1,0:T(8,128)(2,1)}, bf16[64,3072]{1,0:T(8,128)(2,1)S(1)}, u32[]{:S(2)}, u32[]{:S(2)}) collective-permute-start(bf16[64,3072]{1,0:T(8,128)(2,1)} %get-tuple-element.24), channel_id=1, source_target_pairs={{0,32},{16,48},{32,0},{48,16},{64,96},{80,112},{96,64},{112,80},{1... | collective-permute-start | bytes 1179656 | tf_op jit(solution)/shard_map/ppermute | solution.py:316
  26.1 18.2 %collective-permute-start.2 = (bf16[64,3072]{1,0:T(8,128)(2,1)}, bf16[64,3072]{1,0:T(8,128)(2,1)S(1)}, u32[]{:S(2)}, u32[]{:S(2)}) collective-permute-start(bf16[64,3072]{1,0:T(8,128)(2,1)} %get-tuple-element.25), channel_id=1, source_target_pairs={{0,48},{16,32},{32,16},{48,0},{64,112},{80,96},{96,80},{112,64},{1... | collective-permute-start | bytes 1179656 | tf_op jit(solution)/shard_map/ppermute | solution.py:316
  26.3 29.6 %collective-permute-start.3 = (bf16[64,3072]{1,0:T(8,128)(2,1)}, bf16[64,3072]{1,0:T(8,128)(2,1)S(1)}, u32[]{:S(2)}, u32[]{:S(2)}) collective-permute-start(bf16[64,3072]{1,0:T(8,128)(2,1)} %get-tuple-element.26), channel_id=1, source_target_pairs={{0,64},{16,80},{32,96},{48,112},{64,0},{80,16},{96,32},{112,48},{1... | collective-permute-start | bytes 1179656 | tf_op jit(solution)/shard_map/ppermute | solution.py:316
  29.3 33.8 %collective-permute-start.4 = (bf16[64,3072]{1,0:T(8,128)(2,1)}, bf16[64,3072]{1,0:T(8,128)(2,1)S(1)}, u32[]{:S(2)}, u32[]{:S(2)}) collective-permute-start(bf16[64,3072]{1,0:T(8,128)(2,1)} %get-tuple-element.27), channel_id=1, source_target_pairs={{0,80},{16,64},{32,112},{48,96},{64,16},{80,0},{96,48},{112,32},{1... | collective-permute-start | bytes 1179656 | tf_op jit(solution)/shard_map/ppermute | solution.py:316
  29.6 77.1 %copy-start.4 = (bf16[64,3072]{1,0:T(8,128)(2,1)}, bf16[64,3072]{1,0:T(8,128)(2,1)S(1)}, u32[]{:S(2)}) copy-start(bf16[64,3072]{1,0:T(8,128)(2,1)S(1)} %collective-permute-done.refs_1_) | copy-start | bytes 1179652
  29.6 33.5 %collective-permute-start.5 = (bf16[64,3072]{1,0:T(8,128)(2,1)}, bf16[64,3072]{1,0:T(8,128)(2,1)S(1)}, u32[]{:S(2)}, u32[]{:S(2)}) collective-permute-start(bf16[64,3072]{1,0:T(8,128)(2,1)} %get-tuple-element.28), channel_id=1, source_target_pairs={{0,96},{16,112},{32,64},{48,80},{64,32},{80,48},{96,0},{112,16},{1... | collective-permute-start | bytes 1179656 | tf_op jit(solution)/shard_map/ppermute | solution.py:316
  36.7 70.0 %copy-start.5 = (bf16[64,3072]{1,0:T(8,128)(2,1)}, bf16[64,3072]{1,0:T(8,128)(2,1)S(1)}, u32[]{:S(2)}) copy-start(bf16[64,3072]{1,0:T(8,128)(2,1)S(1)} %collective-permute-done.1.refs_2_) | copy-start | bytes 1179652
  36.7 30.3 %collective-permute-start.6 = (bf16[64,3072]{1,0:T(8,128)(2,1)}, bf16[64,3072]{1,0:T(8,128)(2,1)S(1)}, u32[]{:S(2)}, u32[]{:S(2)}) collective-permute-start(bf16[64,3072]{1,0:T(8,128)(2,1)} %get-tuple-element.29), channel_id=1, source_target_pairs={{0,112},{16,96},{32,80},{48,64},{64,48},{80,32},{96,16},{112,0},{1... | collective-permute-start | bytes 1179656 | tf_op jit(solution)/shard_map/ppermute | solution.py:316
  44.3 62.4 %copy-start.6 = (bf16[64,3072]{1,0:T(8,128)(2,1)}, bf16[64,3072]{1,0:T(8,128)(2,1)S(1)}, u32[]{:S(2)}) copy-start(bf16[64,3072]{1,0:T(8,128)(2,1)S(1)} %collective-permute-done.2.refs_3_) | copy-start | bytes 1179652
  55.9 50.8 %copy-start.7 = (bf16[64,3072]{1,0:T(8,128)(2,1)}, bf16[64,3072]{1,0:T(8,128)(2,1)S(1)}, u32[]{:S(2)}) copy-start(bf16[64,3072]{1,0:T(8,128)(2,1)S(1)} %collective-permute-done.3.refs_4_) | copy-start | bytes 1179652
  63.1 43.7 %copy-start.8 = (bf16[64,3072]{1,0:T(8,128)(2,1)}, bf16[64,3072]{1,0:T(8,128)(2,1)S(1)}, u32[]{:S(2)}) copy-start(bf16[64,3072]{1,0:T(8,128)(2,1)S(1)} %collective-permute-done.4.refs_5_) | copy-start | bytes 1179652
  63.1 43.7 %copy-start.9 = (bf16[64,3072]{1,0:T(8,128)(2,1)}, bf16[64,3072]{1,0:T(8,128)(2,1)S(1)}, u32[]{:S(2)}) copy-start(bf16[64,3072]{1,0:T(8,128)(2,1)S(1)} %collective-permute-done.5.refs_6_) | copy-start | bytes 1179652
  67.0 39.8 %copy-start.10 = (bf16[64,3072]{1,0:T(8,128)(2,1)}, bf16[64,3072]{1,0:T(8,128)(2,1)S(1)}, u32[]{:S(2)}) copy-start(bf16[64,3072]{1,0:T(8,128)(2,1)S(1)} %collective-permute-done.6.refs_7_) | copy-start | bytes 1179652

commit v3 on v2

v3 whole, which is shorter than its diff:
```python
import math

import jax
import jax.numpy as jnp
from jax import lax
from jax.experimental import pallas as pl
from jax.experimental.pallas import tpu as pltpu
from jax.sharding import Mesh
from jax.sharding import PartitionSpec as P

HEADS = 16
HD = 128
CG = 8
TILE = 256
SCALE = math.log2(math.e) / math.sqrt(HD)
CORES = 2
GROUPS = CG // CORES
SOURCE, LENGTH, ORIGIN, SLOT, STEP = (i * CG for i in range(5))


def params(mib):
    return pltpu.CompilerParams(vmem_limit_bytes=mib * 2**20)


def cost(flops, moved):
    return pl.CostEstimate(flops=flops, bytes_accessed=moved, transcendentals=0)


def in_vmem(array):
    return pltpu.with_memory_space_constraint(array, pltpu.VMEM)


def in_hbm(array):
    return pltpu.with_memory_space_constraint(array, pltpu.HBM)


def meta_kernel(group_ref, length_ref, step_ref, slot_ref, meta_ref):
    group = group_ref[0]
    core = group & (CORES - 1)
    for i in range(CG):
        meta_ref[SOURCE + lax.shift_right_logical(slot_ref[group * CG + i], 3)] = i
        meta_ref[ORIGIN + i] = group ^ i
    for c in range(CORES):
        for i in range(CG):
            clip = ((group & ~(CORES - 1)) + c) * CG + i
            target = lax.shift_right_logical(slot_ref[clip], 3)

            @pl.when((target & (CORES - 1)) == core)
            def _(c=c, clip=clip, target=target):
                at = LENGTH + c * (CG // CORES) + lax.shift_right_logical(target, 1)
                meta_ref[at] = length_ref[clip]

    for clip in range(slot_ref.shape[0]):
        slot = slot_ref[clip]

        @pl.when(lax.shift_right_logical(slot, 3) == group)
        def _(slot=slot, clip=clip):
            k = (clip // CG) ^ group
            meta_ref[SLOT + k] = slot & 7
            meta_ref[STEP + k] = step_ref[clip]


def make_meta(group, lengths, t_index, slot_target):
    smem = pl.BlockSpec(memory_space=pltpu.SMEM)
    return pl.pallas_call(
        meta_kernel,
        out_shape=jax.ShapeDtypeStruct((5 * CG,), jnp.int32),
        in_specs=[smem] * 4,
        out_specs=smem,
        name="meta",
    )(group, lengths, t_index, slot_target)


def prep(group, slot_target, x):
    clips, _, rows, _ = x.shape
    targets = range(clips)
    ahead = 3

    def kernel(group_ref, slot_ref, x_ref, o_ref, held_ref, in_sems, out_sems):
        base = group_ref[0] * clips
        own = [lax.shift_right_logical(slot_ref[base + i], 3) for i in range(clips)]

        def source(target):
            return sum(jnp.where(own[i] == target, i, 0) for i in range(1, clips))

        sources = [source(target) for target in targets]

        def arriving(n, h):
            columns = x_ref.at[sources[n], :, :, pl.ds(h * HD, HD)]
            return pltpu.make_async_copy(columns, held_ref.at[n, h], in_sems.at[n])

        def all_of(n):
            return pltpu.make_async_copy(held_ref.at[n], held_ref.at[n], in_sems.at[n])

        def leaving(n):
            to = o_ref.at[:, n % CORES, n // CORES]
            return pltpu.make_async_copy(held_ref.at[n], to, out_sems.at[n])

        for n in range(len(targets) + ahead):
            if n < len(targets):
                for h in range(HEADS):
                    arriving(n, h).start()
            if n >= ahead:
                all_of(n - ahead).wait()
                leaving(n - ahead).start()
        for n in range(len(targets)):
            leaving(n).wait()

    smem = pl.BlockSpec(memory_space=pltpu.SMEM)
    anywhere = pl.BlockSpec(memory_space=pl.ANY)
    return pl.pallas_call(
        kernel,
        in_specs=[smem, smem, anywhere],
        out_specs=anywhere,
        out_shape=pltpu.HBM((HEADS, CORES, GROUPS, 3, rows, HD), jnp.bfloat16),
        scratch_shapes=[
            pltpu.VMEM((len(targets), HEADS, 3, rows, HD), jnp.bfloat16),
            pltpu.SemaphoreType.DMA((len(targets),)),
            pltpu.SemaphoreType.DMA((len(targets),)),
        ],
        compiler_params=params(12),
        cost_estimate=cost(0, len(targets) * 12 * rows * HEADS * HD),
        name="prep",
    )(group, slot_target, in_hbm(x))


def spread_kernel(meta_ref, tokens_ref, *out_refs):
    for k in range(CG):

        @pl.when(pl.program_id(0) == k)
        def _(k=k):
            out_refs[k][...] = tokens_ref[0]


def spread(meta, tokens):
    rows, width = tokens.shape[1:]
    return pl.pallas_call(
        spread_kernel,
        grid_spec=pltpu.PrefetchScalarGridSpec(
            num_scalar_prefetch=1,
            grid=(CG,),
            in_specs=[
                pl.BlockSpec((1, rows, width), lambda k, m: (m[SOURCE + m[ORIGIN + k]], 0, 0))
            ],
            out_specs=[pl.BlockSpec((rows, width), lambda k, m: (0, 0))] * CG,
        ),
        out_shape=[pltpu.HBM((rows, width), tokens.dtype)] * CG,
        compiler_params=params(12),
        cost_estimate=cost(0, 4 * math.prod(tokens.shape)),
        name="spread",
    )(meta, in_hbm(tokens))


def inverse_root(wide):
    return lax.rsqrt(jnp.mean(wide * wide, axis=-1, keepdims=True) + 1e-06)


def attend(n, length, tile, store, gain, root_ref, k_ref, v_ref):
    row = (n - 1) * TILE + lax.broadcasted_iota(jnp.int32, (TILE, HD), 0)
    live = row < length
    for t in range(n):
        to = slice(t * TILE, (t + 1) * TILE)
        root = inverse_root(tile(t, 0).astype(jnp.float32)) * SCALE
        root_ref[to] = jnp.broadcast_to(root, (TILE, HD))
        wide = tile(t, 1).astype(jnp.float32)
        k_ref[to] = (wide * inverse_root(wide) * gain).astype(jnp.bfloat16)
        if t < n - 1:
            v_ref[to, :HD] = tile(t, 2)
            v_ref[to, HD:] = jnp.ones((TILE, HD), jnp.bfloat16)
        else:
            factor = jnp.where(live, 1.0, 0.0).astype(jnp.bfloat16)
            v_ref[to, :HD] = tile(t, 2) * factor
            v_ref[to, HD:] = factor
    for t in range(n):
        scores = lax.dot_general(
            tile(t, 0),
            k_ref[: n * TILE],
            (((1,), (1,)), ((), ())),
            preferred_element_type=jnp.float32,
        )
        root = root_ref[t * TILE : (t + 1) * TILE]
        raised = jnp.concatenate(
            [
                jnp.exp2(scores[:, i : i + HD] * root).astype(jnp.bfloat16)
                for i in range(0, n * TILE, HD)
            ],
            axis=1,
        )
        summed = jnp.dot(raised, v_ref[: n * TILE], preferred_element_type=jnp.float32)
        result = summed[:, :HD] / summed[:, HD:]
        if t == n - 1:
            result = jnp.where(live, result, 0.0)
        store(t, result.astype(jnp.bfloat16))


def attention(meta, y, q_gain, k_gain):
    blocks, cores, groups, parts, rows, _ = y.shape
    total = blocks * rows
    per_tile, tiles = TILE // rows, total // TILE

    clips = cores * groups

    def kernel(meta_ref, y_ref, qg_ref, kg_ref, o_ref, held_ref, sems, *scratch):
        gain = qg_ref[...] * kg_ref[...]

        def arriving(i):
            clip = y_ref.at[:, lax.div(i, groups), lax.rem(i, groups)]
            return pltpu.make_async_copy(clip, held_ref.at[i], sems.at[i])

        for i in range(clips):
            arriving(i).start()

        def one_clip(i, carry):
            arriving(i).wait()
            c, x = lax.div(i, groups), lax.rem(i, groups)
            length = meta_ref[LENGTH + i]
            live_tiles = lax.div(length + (TILE - 1), TILE)

            def tile(t, part):
                at = slice(t * per_tile, (t + 1) * per_tile)
                return held_ref[i, at, part].reshape(TILE, HD)

            def store(t, result):
                at = slice(t * per_tile, (t + 1) * per_tile)
                o_ref[x, at, c] = result.reshape(per_tile, rows, HD)

            for n in range(1, tiles + 1):

                @pl.when(live_tiles == n)
                def _(n=n):
                    attend(n, length, tile, store, gain, *scratch)
                    for t in range(n, tiles):
                        store(t, jnp.zeros((TILE, HD), jnp.bfloat16))

            return carry

        lax.fori_loop(0, clips, one_clip, 0)

    vmem = pl.BlockSpec(memory_space=pltpu.VMEM)
    return pl.pallas_call(
        kernel,
        in_specs=[
            pl.BlockSpec(memory_space=pltpu.SMEM),
            pl.BlockSpec(memory_space=pl.ANY),
            vmem,
            vmem,
        ],
        out_specs=vmem,
        out_shape=pltpu.VMEM((groups, blocks, cores, rows, HD), jnp.bfloat16),
        scratch_shapes=[
            pltpu.VMEM((clips, blocks, parts, rows, HD), jnp.bfloat16),
            pltpu.SemaphoreType.DMA((clips,)),
            pltpu.VMEM((total, HD), jnp.float32),
            pltpu.VMEM((total, HD), jnp.bfloat16),
            pltpu.VMEM((total, 2 * HD), jnp.bfloat16),
        ],
        compiler_params=params(24),
        cost_estimate=cost(clips * 4 * total * total * HD, clips * total * HD * 8),
        name="attention",
    )(meta, in_hbm(y), q_gain, k_gain)


def load(weight):
    def kernel(from_ref, to_ref, sem):
        copy = pltpu.make_async_copy(from_ref, to_ref, sem)
        copy.start()
        copy.wait()

    return pl.pallas_call(
        kernel,
        in_specs=[pl.BlockSpec(memory_space=pl.ANY)],
        out_specs=pl.BlockSpec(memory_space=pltpu.VMEM),
        out_shape=pltpu.VMEM(weight.shape, weight.dtype),
        scratch_shapes=[pltpu.SemaphoreType.DMA],
        compiler_params=params(16),
        cost_estimate=cost(0, 4 * math.prod(weight.shape)),
        name="load",
    )(in_hbm(weight))


def project(meta, z, out_weight, gate_table, tokens):
    rows, width = tokens[0].shape
    clips, block = len(tokens), 512
    steps = width // block

    def kernel(meta_ref, z_ref, w_ref, gate_ref, *refs):
        token_refs, (out_ref, a_ref) = refs[:clips], refs[clips:]

        @pl.when(pl.program_id(0) == 0)
        def _():
            for k in range(clips):
                origin = meta_ref[ORIGIN + k]
                x, core = lax.shift_right_logical(origin, 1), origin & (CORES - 1)
                for h in range(HEADS):
                    a_ref[k * rows : (k + 1) * rows, h * HD : (h + 1) * HD] = z_ref[x, h, core]

        columns = pl.ds(pl.multiple_of(pl.program_id(0) * block, block), block)
        projected = jnp.dot(a_ref[...], w_ref[:, columns], preferred_element_type=jnp.float32)
        for k in range(clips):
            gate = gate_ref[pl.ds(meta_ref[STEP + k], 1), :]
            part = gate * projected[k * rows : (k + 1) * rows]
            out_ref[meta_ref[SLOT + k]] = (token_refs[k][...].astype(jnp.float32) + part).astype(
                jnp.bfloat16
            )

    return pl.pallas_call(
        kernel,
        grid_spec=pltpu.PrefetchScalarGridSpec(
            num_scalar_prefetch=1,
            grid=(steps,),
            in_specs=[
                pl.BlockSpec(memory_space=pltpu.VMEM),
                pl.BlockSpec(memory_space=pltpu.VMEM),
                pl.BlockSpec((gate_table.shape[0], block), lambda n, m: (0, n)),
            ]
            + [pl.BlockSpec((rows, block), lambda n, m: (0, n))] * clips,
            out_specs=pl.BlockSpec((clips, rows, block), lambda n, m: (0, 0, n)),
            scratch_shapes=[pltpu.VMEM((clips * rows, HEADS * HD), jnp.bfloat16)],
        ),
        out_shape=pltpu.HBM((clips, rows, width), jnp.bfloat16),
        compiler_params=params(24),
        cost_estimate=cost(
            2 * clips * rows * HEADS * HD * width,
            2 * HEADS * HD * width + 4 * clips * rows * width,
        ),
        name="project",
    )(
        meta,
        in_vmem(z),
        in_vmem(out_weight),
        in_hbm(gate_table),
        *[in_hbm(part) for part in tokens],
    )


def per_device(qkv, tokens, lengths, t_index, slot_target, gate_table, q_gain, k_gain, out_weight):
    group = lax.axis_index(("x", "core"))
    group = group.reshape(1)
    meta = make_meta(group, lengths, t_index, slot_target)

    def across(part, k):
        pairs = [(g, g ^ k) for g in range(CG)]
        return lax.ppermute(part, ("x", "core"), pairs) if k else part

    def exchange(array, axes, kept):
        sent = array.reshape(-1, *array.shape[kept:])
        arrived = lax.all_to_all(sent, axes, split_axis=0, concat_axis=0, tiled=True)
        return arrived.reshape(array.shape)

    resid = [across(part, k) for k, part in enumerate(spread(meta, tokens))]
    weight = load(out_weight)
    y = exchange(prep(group, slot_target, jnp.swapaxes(qkv, 1, 2)), ("z", "y", "core"), 2)
    y, weight, *resid = lax.optimization_barrier((y, weight, *resid))
    attended = attention(meta, y, q_gain.reshape(1, HD), k_gain.reshape(1, HD))
    z = exchange(attended, ("x", "z", "y"), 2)
    return project(meta, z, weight, gate_table, resid)


def solution(mesh):
    apart = Mesh(mesh.devices.reshape(GROUPS, CORES, 4, 4), ("x", "core", "z", "y"))
    clips, tokens = ("x", "core"), ("z", "y")
    return jax.shard_map(
        per_device,
        mesh=apart,
        in_specs=(
            P(clips, tokens, None, None),
            P(clips, tokens, None),
            P(),
            P(),
            P(),
            P(),
            P(),
            P(),
            P(),
        ),
        out_specs=P(clips, tokens, None),
        check_vma=False,
    )
```

time: 159 us -> 152 us (0.956); the launches traced: 159 us -> 149 us
  waiting for transfers between devices: 61.9 us -> 50.6 us
  local copies, waits for them, and re-layouts: 0.65 us -> 5.84 us
  blocking collectives: 39 us -> 35.3 us
    ppermute x7, waiting for transfers between devices: 33.3 us -> 24.1 us  [across(): return lax.ppermute(part, ('x', 'core'), pairs) if k else part]
    unnamed x22 -> x28, local copies, waits for them, and re-layouts: 0.65 us -> 5.84 us
    all_to_all x1, blocking collectives: 39 us -> 35.3 us  [exchange(): lax.all_to_all(sent, axes, split_axis=0, concat_axis=0, tiled=True)]
    pallas_call x2 -> x3, Pallas kernels: 18.2 us -> 20.7 us  [the longest x1 10.1 us: attention(): pl.pallas_call(kernel, in_specs=[pl.BlockSpec(memory_space=pltpu.SMEM), p...]
    pallas_call x1, Pallas kernels: 12.9 us -> 10.7 us  [project(): pl.pallas_call(kernel, grid_spec=pltpu.PrefetchScalarGridSpec(num_scalar_...]
    all_to_all x1, waiting for transfers between devices: 28.6 us -> 26.5 us  [exchange(): lax.all_to_all(sent, axes, split_axis=0, concat_axis=0, tiled=True)]
  transfers between devices with their start and end apart: 8 -> 8, of which waited for: 6 -> 5; matrix products, arithmetic and copies ran while one was open for 0% -> 0% of each run, Pallas kernels for 4% -> 8%
where the time goes in v3:
time: 152 us; the launch traced here: 149 us
  waiting for transfers between devices  50.6 us (33%)
  Pallas kernels  39.5 us (26%)
  blocking collectives  35.3 us (23%)
  starting transfers between devices  17.9 us (12%)
  local copies, waits for them, and re-layouts  5.84 us (4%)
    all_to_all x1, blocking collectives, exchange(): lax.all_to_all(sent, axes, split_axis=0, concat_axis=0, tiled=True)  35.3 us
    all_to_all x1, waiting for transfers between devices, exchange(): lax.all_to_all(sent, axes, split_axis=0, concat_axis=0, tiled=True)  26.5 us
    ppermute x7, waiting for transfers between devices, across(): return lax.ppermute(part, ('x', 'core'), pairs) if k else part  24.1 us
    pallas_call x1, Pallas kernels, project(): pl.pallas_call(kernel, grid_spec=pltpu.PrefetchScalarGridSpec(num_scalar_...  10.7 us
    pallas_call x1, Pallas kernels, attention(): pl.pallas_call(kernel, in_specs=[pl.BlockSpec(memory_space=pltpu.SMEM), p...  10.1 us
    ppermute x7, starting transfers between devices, across(): return lax.ppermute(part, ('x', 'core'), pairs) if k else part  9.39 us
    all_to_all x1, starting transfers between devices, exchange(): lax.all_to_all(sent, axes, split_axis=0, concat_axis=0, tiled=True)  8.54 us
    pallas_call x1, Pallas kernels, spread(): pl.pallas_call(spread_kernel, grid_spec=pltpu.PrefetchScalarGridSpec(num_...  6.68 us
  transfers between devices with their start and end apart: 8, of which 5 were waited for; matrix products, arithmetic and copies ran while one was open for 0% of the time, Pallas kernels for 8%

profile of v3, /device:TPU:0, one launch (start us, length us, event | category | flops | bytes accessed | tf_op | source)
XLA Modules:
  0.0 149.4 jit_solution(8031343822666899202)
XLA Ops:
  0.0 0.0 copy-start.2
  0.0 0.7 copy-done.2
  0.7 6.1 %prep.1 = bf16[16,2,4,3,64,128]{5,4,3,2,1,0:T(8,128)(2,1)} custom-call(s32[1]{0:T(128)} %bitcast.group_ref, s32[64]{0:T(128)S(1)} %copy-done.2, bf16[8,3,64,2048]{3,2,1,0:T(8,128)(2,1)} %bitcast.13), custom_call_target="tpu_custom_call" | custom-call | bytes 12582912 | tf_op jit(solution)/shard_map/prep/pallas_call | solution.py:111
  6.7 8.5 %all-to-all-start = ((bf16[32,4,3,64,128]{4,3,2,1,0:T(8,128)(2,1)}), bf16[32,4,3,64,128]{4,3,2,1,0:T(8,128)(2,1)}, u32[]{:S(2)}, u32[]{:S(2)}) async-start(bf16[32,4,3,64,128]{4,3,2,1,0:T(8,128)(2,1)} %bitcast.12), calls=%async_computation | async-start | bytes 12582912 | tf_op jit(solution)/shard_map/all_to_all | solution.py:347
  15.3 1.4 meta.1.meta_ref
  16.7 0.0 copy-start.3
  16.7 0.6 copy-done.3
  17.3 6.7 %spread.1 = (bf16[64,3072]{1,0:T(8,128)(2,1)}, bf16[64,3072]{1,0:T(8,128)(2,1)}, bf16[64,3072]{1,0:T(8,128)(2,1)}, bf16[64,3072]{1,0:T(8,128)(2,1)}, bf16[64,307...) custom-call(s32[40]{0:T(128)S(1)} %copy-done.3, ...), custom_call_target="tpu_custom_call" | custom-call | bytes 6291456 | tf_op jit(solution)/shard_map/spread/pallas_call | solution.py:137
  24.0 0.2 collective-permute-start
  24.2 1.5 collective-permute-start.1
  25.7 0.2 collective-permute-start.2
  25.9 3.0 %collective-permute-start.3 = (bf16[64,3072]{1,0:T(8,128)(2,1)}, bf16[64,3072]{1,0:T(8,128)(2,1)S(1)}, u32[]{:S(2)}, u32[]{:S(2)}) collective-permute-start(bf16[64,3072]{1,0:T(8,128)(2,1)} %get-tuple-element.27), channel_id=1, source_target_pairs={{0,64},{16,80},{32,96},{48,112},{64,0},{80,16},{96,32},{112,48},{1... | collective-permute-start | bytes 1179656 | tf_op jit(solution)/shard_map/ppermute | solution.py:343
  28.9 0.3 collective-permute-start.4
  29.2 0.0 collective-permute-done.refs_1_
  29.2 0.0 copy-start.7
  29.2 2.8 %collective-permute-start.5 = (bf16[64,3072]{1,0:T(8,128)(2,1)}, bf16[64,3072]{1,0:T(8,128)(2,1)S(1)}, u32[]{:S(2)}, u32[]{:S(2)}) collective-permute-start(bf16[64,3072]{1,0:T(8,128)(2,1)} %get-tuple-element.29), channel_id=1, source_target_pairs={{0,96},{16,112},{32,64},{48,80},{64,32},{80,48},{96,0},{112,16},{1... | collective-permute-start | bytes 1179656 | tf_op jit(solution)/shard_map/ppermute | solution.py:343
  32.0 4.4 %collective-permute-done.1.refs_2_ = bf16[64,3072]{1,0:T(8,128)(2,1)S(1)} collective-permute-done((bf16[64,3072]{1,0:T(8,128)(2,1)}, bf16[64,3072]{1,0:T(8,128)(2,1)S(1)}, u32[]{:S(2)}, u32[]{:S(2)}) %collective-permute-start.1) | collective-permute-done | bytes 393248 | tf_op jit(solution)/shard_map/ppermute | solution.py:343
  36.4 0.0 copy-start.8
  36.4 0.0 copy-start.4
  36.4 0.0 copy-start.5
  36.4 0.0 copy-start.6
  36.4 1.4 collective-permute-start.6
  37.8 4.6 %load.1.w_ref = bf16[2048,3072]{1,0:T(8,128)(2,1)S(1)} custom-call(bf16[2048,3072]{1,0:T(8,128)(2,1)} %from_ref.1), custom_call_target="tpu_custom_call" | custom-call | bytes 25165824 | tf_op jit(solution)/shard_map/load/pallas_call | solution.py:269
  42.4 0.0 copy-done.7
  42.4 0.0 copy-done.8
  42.4 0.0 copy-start
  42.4 4.5 %copy-done = bf16[2048,3072]{1,0:T(8,128)(2,1)} copy-done((bf16[2048,3072]{1,0:T(8,128)(2,1)}, bf16[2048,3072]{1,0:T(8,128)(2,1)S(1)}, u32[]{:S(2)}) %copy-start) | copy-done | bytes 12582936
  46.9 0.0 collective-permute-done.2.refs_3_
  47.0 0.0 copy-start.9
  47.0 8.6 %collective-permute-done.3.refs_4_ = bf16[64,3072]{1,0:T(8,128)(2,1)S(1)} collective-permute-done((bf16[64,3072]{1,0:T(8,128)(2,1)}, bf16[64,3072]{1,0:T(8,128)(2,1)S(1)}, u32[]{:S(2)}, u32[]{:S(2)}) %collective-permute-start.3) | collective-permute-done | bytes 393248 | tf_op jit(solution)/shard_map/ppermute | solution.py:343
  55.5 0.0 copy-start.10
  55.5 7.2 %collective-permute-done.4.refs_5_ = bf16[64,3072]{1,0:T(8,128)(2,1)S(1)} collective-permute-done((bf16[64,3072]{1,0:T(8,128)(2,1)}, bf16[64,3072]{1,0:T(8,128)(2,1)S(1)}, u32[]{:S(2)}, u32[]{:S(2)}) %collective-permute-start.4) | collective-permute-done | bytes 393248 | tf_op jit(solution)/shard_map/ppermute | solution.py:343
  62.7 0.0 copy-start.11
  62.7 0.0 collective-permute-done.5.refs_6_
  62.7 0.0 copy-start.12
  62.7 3.9 %collective-permute-done.6.refs_7_ = bf16[64,3072]{1,0:T(8,128)(2,1)S(1)} collective-permute-done((bf16[64,3072]{1,0:T(8,128)(2,1)}, bf16[64,3072]{1,0:T(8,128)(2,1)S(1)}, u32[]{:S(2)}, u32[]{:S(2)}) %collective-permute-start.6) | collective-permute-done | bytes 393248 | tf_op jit(solution)/shard_map/ppermute | solution.py:343
  66.6 0.0 copy-start.13
  66.6 26.5 %all-to-all-done = bf16[32,4,3,64,128]{4,3,2,1,0:T(8,128)(2,1)} async-done(((bf16[32,4,3,64,128]{4,3,2,1,0:T(8,128)(2,1)}), bf16[32,4,3,64,128]{4,3,2,1,0:T(8,128)(2,1)}, u32[]{:S(2)}, u32[]{:S(2)}) %all-to-all-start) | async-done | bytes 6291488 | tf_op jit(solution)/shard_map/all_to_all | solution.py:347
  93.2 0.0 copy-done.4
  93.2 0.0 copy-done.5
  93.2 0.0 copy-done.6
  93.2 0.0 copy-start.1
  93.2 10.1 %attention.1 = bf16[4,16,2,64,128]{4,3,2,1,0:T(8,128)(2,1)S(1)} custom-call(s32[40]{0:T(128)S(1)} %copy-done.4, bf16[16,2,4,3,64,128]{5,4,3,2,1,0:T(8,128)(2,1)} %bitcast.3.y_ref, f32[1,128]{1,0:T(1,128)S(1)} %bitcast.10, f32[1,128]{1,0:T(1,128)S(1)} %bitcast.11), custom_call_target="tpu_custom_call" | custom-call | flops 4294967296 | bytes 8388608 | tf_op jit(solution)/shard_map/attention/pallas_call | solution.py:240
  103.3 0.0 copy-done.9
  103.3 0.0 copy-done.10
  103.3 0.0 copy-done.11
  103.3 0.0 copy-done.12
  103.3 0.0 copy-done.13
  103.3 35.3 %all_to_all.10 = bf16[64,2,64,128]{3,2,1,0:T(8,128)(2,1)S(1)} all-to-all(bf16[64,2,64,128]{3,2,1,0:T(8,128)(2,1)S(1)} %bitcast.9), channel_id=1, replica_groups=mesh['x'=4,'core'=2,'z'=4,'y'=4] {'x','z','y'}, dimensions={0} | all-to-all | bytes 4194304 | tf_op jit(solution)/shard_map/all_to_all | solution.py:347
  138.7 0.0 copy-done.1
  138.7 10.7 %project.1 = bf16[8,64,3072]{2,1,0:T(8,128)(2,1)} custom-call(s32[40]{0:T(128)S(1)} %copy-done.4, bf16[4,16,2,64,128]{4,3,2,1,0:T(8,128)(2,1)S(1)} %bitcast.8, bf16[2048,3072]{1,0:T(8,128)(2,1)S(1)} %copy-done.1, f32[50,3072]{1,0:T(8,128)} %gate_ref.1, bf16[64,3072]{1,0:T(8,128)(2,1)} %get-tuple-element.33.refs_0_, bf16[64,3072]{1,0:T(8,128)(2,1)} %copy-done.7, ...), custom_call_target="tpu_custom_call" | custom-call | flops 6442450944 | bytes 18874368 | tf_op jit(solution)/shard_map/project/pallas_call | solution.py:306
Async XLA Ops:
  0.0 0.7 copy-start.2
  6.7 86.4 %all-to-all-start = ((bf16[32,4,3,64,128]{4,3,2,1,0:T(8,128)(2,1)}), bf16[32,4,3,64,128]{4,3,2,1,0:T(8,128)(2,1)}, u32[]{:S(2)}, u32[]{:S(2)}) async-start(bf16[32,4,3,64,128]{4,3,2,1,0:T(8,128)(2,1)} %bitcast.12), calls=%async_computation | async-start | bytes 12582912 | tf_op jit(solution)/shard_map/all_to_all | solution.py:347
  16.7 0.6 copy-start.3
  24.0 5.2 %collective-permute-start = (bf16[64,3072]{1,0:T(8,128)(2,1)}, bf16[64,3072]{1,0:T(8,128)(2,1)S(1)}, u32[]{:S(2)}, u32[]{:S(2)}) collective-permute-start(bf16[64,3072]{1,0:T(8,128)(2,1)} %get-tuple-element.24), channel_id=1, source_target_pairs={{0,16},{16,0},{32,48},{48,32},{64,80},{80,64},{96,112},{112,96},{1... | collective-permute-start | bytes 1179656 | tf_op jit(solution)/shard_map/ppermute | solution.py:343
  24.2 12.1 %collective-permute-start.1 = (bf16[64,3072]{1,0:T(8,128)(2,1)}, bf16[64,3072]{1,0:T(8,128)(2,1)S(1)}, u32[]{:S(2)}, u32[]{:S(2)}) collective-permute-start(bf16[64,3072]{1,0:T(8,128)(2,1)} %get-tuple-element.25), channel_id=1, source_target_pairs={{0,32},{16,48},{32,0},{48,16},{64,96},{80,112},{96,64},{112,80},{1... | collective-permute-start | bytes 1179656 | tf_op jit(solution)/shard_map/ppermute | solution.py:343
  25.7 21.2 %collective-permute-start.2 = (bf16[64,3072]{1,0:T(8,128)(2,1)}, bf16[64,3072]{1,0:T(8,128)(2,1)S(1)}, u32[]{:S(2)}, u32[]{:S(2)}) collective-permute-start(bf16[64,3072]{1,0:T(8,128)(2,1)} %get-tuple-element.26), channel_id=1, source_target_pairs={{0,48},{16,32},{32,16},{48,0},{64,112},{80,96},{96,80},{112,64},{1... | collective-permute-start | bytes 1179656 | tf_op jit(solution)/shard_map/ppermute | solution.py:343
  25.9 29.6 %collective-permute-start.3 = (bf16[64,3072]{1,0:T(8,128)(2,1)}, bf16[64,3072]{1,0:T(8,128)(2,1)S(1)}, u32[]{:S(2)}, u32[]{:S(2)}) collective-permute-start(bf16[64,3072]{1,0:T(8,128)(2,1)} %get-tuple-element.27), channel_id=1, source_target_pairs={{0,64},{16,80},{32,96},{48,112},{64,0},{80,16},{96,32},{112,48},{1... | collective-permute-start | bytes 1179656 | tf_op jit(solution)/shard_map/ppermute | solution.py:343
  28.9 33.8 %collective-permute-start.4 = (bf16[64,3072]{1,0:T(8,128)(2,1)}, bf16[64,3072]{1,0:T(8,128)(2,1)S(1)}, u32[]{:S(2)}, u32[]{:S(2)}) collective-permute-start(bf16[64,3072]{1,0:T(8,128)(2,1)} %get-tuple-element.28), channel_id=1, source_target_pairs={{0,80},{16,64},{32,112},{48,96},{64,16},{80,0},{96,48},{112,32},{1... | collective-permute-start | bytes 1179656 | tf_op jit(solution)/shard_map/ppermute | solution.py:343
  29.2 13.2 %copy-start.7 = (bf16[64,3072]{1,0:T(8,128)(2,1)}, bf16[64,3072]{1,0:T(8,128)(2,1)S(1)}, u32[]{:S(2)}) copy-start(bf16[64,3072]{1,0:T(8,128)(2,1)S(1)} %collective-permute-done.refs_1_) | copy-start | bytes 1179652
  29.2 33.5 %collective-permute-start.5 = (bf16[64,3072]{1,0:T(8,128)(2,1)}, bf16[64,3072]{1,0:T(8,128)(2,1)S(1)}, u32[]{:S(2)}, u32[]{:S(2)}) collective-permute-start(bf16[64,3072]{1,0:T(8,128)(2,1)} %get-tuple-element.29), channel_id=1, source_target_pairs={{0,96},{16,112},{32,64},{48,80},{64,32},{80,48},{96,0},{112,16},{1... | collective-permute-start | bytes 1179656 | tf_op jit(solution)/shard_map/ppermute | solution.py:343
  36.4 6.0 %copy-start.8 = (bf16[64,3072]{1,0:T(8,128)(2,1)}, bf16[64,3072]{1,0:T(8,128)(2,1)S(1)}, u32[]{:S(2)}) copy-start(bf16[64,3072]{1,0:T(8,128)(2,1)S(1)} %collective-permute-done.1.refs_2_) | copy-start | bytes 1179652
  36.4 56.8 %copy-start.4 = (s32[40]{0:T(128)S(1)}, s32[40]{0:T(128)}, u32[]{:S(2)}) copy-start(s32[40]{0:T(128)} %meta.1.meta_ref) | copy-start | bytes 484
  36.4 56.8 %copy-start.5 = (f32[128]{0:T(128)S(1)}, f32[128]{0:T(128)}, u32[]{:S(2)}) copy-start(f32[128]{0:T(128)} %param.15) | copy-start | bytes 1540
  36.4 56.8 %copy-start.6 = (f32[128]{0:T(128)S(1)}, f32[128]{0:T(128)}, u32[]{:S(2)}) copy-start(f32[128]{0:T(128)} %param.16) | copy-start | bytes 1540
  36.4 30.2 %collective-permute-start.6 = (bf16[64,3072]{1,0:T(8,128)(2,1)}, bf16[64,3072]{1,0:T(8,128)(2,1)S(1)}, u32[]{:S(2)}, u32[]{:S(2)}) collective-permute-start(bf16[64,3072]{1,0:T(8,128)(2,1)} %get-tuple-element.30), channel_id=1, source_target_pairs={{0,112},{16,96},{32,80},{48,64},{64,48},{80,32},{96,16},{112,0},{1... | collective-permute-start | bytes 1179656 | tf_op jit(solution)/shard_map/ppermute | solution.py:343
  42.4 4.5 %copy-start = (bf16[2048,3072]{1,0:T(8,128)(2,1)}, bf16[2048,3072]{1,0:T(8,128)(2,1)S(1)}, u32[]{:S(2)}) copy-start(bf16[2048,3072]{1,0:T(8,128)(2,1)S(1)} %load.1.w_ref) | copy-start | bytes 37748740
  47.0 56.3 %copy-start.9 = (bf16[64,3072]{1,0:T(8,128)(2,1)}, bf16[64,3072]{1,0:T(8,128)(2,1)S(1)}, u32[]{:S(2)}) copy-start(bf16[64,3072]{1,0:T(8,128)(2,1)S(1)} %collective-permute-done.2.refs_3_) | copy-start | bytes 1179652
  55.5 47.8 %copy-start.10 = (bf16[64,3072]{1,0:T(8,128)(2,1)}, bf16[64,3072]{1,0:T(8,128)(2,1)S(1)}, u32[]{:S(2)}) copy-start(bf16[64,3072]{1,0:T(8,128)(2,1)S(1)} %collective-permute-done.3.refs_4_) | copy-start | bytes 1179652
  62.7 40.6 %copy-start.11 = (bf16[64,3072]{1,0:T(8,128)(2,1)}, bf16[64,3072]{1,0:T(8,128)(2,1)S(1)}, u32[]{:S(2)}) copy-start(bf16[64,3072]{1,0:T(8,128)(2,1)S(1)} %collective-permute-done.4.refs_5_) | copy-start | bytes 1179652
  62.7 40.6 %copy-start.12 = (bf16[64,3072]{1,0:T(8,128)(2,1)}, bf16[64,3072]{1,0:T(8,128)(2,1)S(1)}, u32[]{:S(2)}) copy-start(bf16[64,3072]{1,0:T(8,128)(2,1)S(1)} %collective-permute-done.5.refs_6_) | copy-start | bytes 1179652
  66.6 36.7 %copy-start.13 = (bf16[64,3072]{1,0:T(8,128)(2,1)}, bf16[64,3072]{1,0:T(8,128)(2,1)S(1)}, u32[]{:S(2)}) copy-start(bf16[64,3072]{1,0:T(8,128)(2,1)S(1)} %collective-permute-done.6.refs_7_) | copy-start | bytes 1179652
  93.2 45.5 %copy-start.1 = (bf16[2048,3072]{1,0:T(8,128)(2,1)S(1)}, bf16[2048,3072]{1,0:T(8,128)(2,1)}, u32[]{:S(2)}) copy-start(bf16[2048,3072]{1,0:T(8,128)(2,1)} %copy-done) | copy-start | bytes 37748740

commit v4 on v3

--- a/solution.py
+++ b/solution.py
@@ -121,7 +121,7 @@
         compiler_params=params(12),
         cost_estimate=cost(0, len(targets) * 12 * rows * HEADS * HD),
         name="prep",
-    )(group, slot_target, in_hbm(x))
+    )(in_hbm(group), in_hbm(slot_target), in_hbm(x))
 
 
 def spread_kernel(meta_ref, tokens_ref, *out_refs):
@@ -171,13 +171,20 @@
             factor = jnp.where(live, 1.0, 0.0).astype(jnp.bfloat16)
             v_ref[to, :HD] = tile(t, 2) * factor
             v_ref[to, HD:] = factor
-    for t in range(n):
-        scores = lax.dot_general(
+
+    def scores_of(t):
+        return lax.dot_general(
             tile(t, 0),
             k_ref[: n * TILE],
             (((1,), (1,)), ((), ())),
             preferred_element_type=jnp.float32,
         )
+
+    ahead = [scores_of(t) for t in range(min(2, n))]
+    for t in range(n):
+        scores = ahead.pop(0)
+        if t + 2 < n:
+            ahead.append(scores_of(t + 2))
         root = root_ref[t * TILE : (t + 1) * TILE]
         raised = jnp.concatenate(
             [
@@ -222,7 +229,7 @@
 
             def store(t, result):
                 at = slice(t * per_tile, (t + 1) * per_tile)
-                o_ref[x, at, c] = result.reshape(per_tile, rows, HD)
+                o_ref[at, x, c] = result.reshape(per_tile, rows, HD)
 
             for n in range(1, tiles + 1):
 
@@ -246,7 +253,7 @@
             vmem,
         ],
         out_specs=vmem,
-        out_shape=pltpu.VMEM((groups, blocks, cores, rows, HD), jnp.bfloat16),
+        out_shape=pltpu.VMEM((blocks, groups, cores, rows, HD), jnp.bfloat16),
         scratch_shapes=[
             pltpu.VMEM((clips, blocks, parts, rows, HD), jnp.bfloat16),
             pltpu.SemaphoreType.DMA((clips,)),
@@ -278,46 +285,61 @@
     )(in_hbm(weight))
 
 
-def project(meta, z, out_weight, gate_table, tokens):
+def project(meta, z, weight, gate_table, tokens):
     rows, width = tokens[0].shape
     clips, block = len(tokens), 512
     steps = width // block
 
     def kernel(meta_ref, z_ref, w_ref, gate_ref, *refs):
-        token_refs, (out_ref, a_ref) = refs[:clips], refs[clips:]
-
-        @pl.when(pl.program_id(0) == 0)
-        def _():
+        token_refs = refs[:clips]
+        out_ref, a_ref, rate_ref, resid_ref, held_ref, in_sems, out_sems = refs[clips:]
+        arriving = [
+            pltpu.make_async_copy(token_refs[k], resid_ref.at[k], in_sems.at[k])
+            for k in range(clips)
+        ] + [pltpu.make_async_copy(gate_ref, rate_ref, in_sems.at[clips])]
+        for copy in arriving:
+            copy.start()
+        for k in range(clips):
+            origin = meta_ref[ORIGIN + k]
+            x, core = lax.shift_right_logical(origin, 1), origin & (CORES - 1)
+            for h in range(HEADS):
+                a_ref[k * rows : (k + 1) * rows, h * HD : (h + 1) * HD] = z_ref[h, x, core]
+        for copy in arriving:
+            copy.wait()
+
+        def leaving(n, columns):
+            return pltpu.make_async_copy(
+                held_ref.at[n], out_ref.at[:, :, columns], out_sems.at[n]
+            )
+
+        for n in range(steps):
+            columns = pl.ds(n * block, block)
+            projected = jnp.dot(a_ref[...], w_ref[:, columns], preferred_element_type=jnp.float32)
             for k in range(clips):
-                origin = meta_ref[ORIGIN + k]
-                x, core = lax.shift_right_logical(origin, 1), origin & (CORES - 1)
-                for h in range(HEADS):
-                    a_ref[k * rows : (k + 1) * rows, h * HD : (h + 1) * HD] = z_ref[x, h, core]
-
-        columns = pl.ds(pl.multiple_of(pl.program_id(0) * block, block), block)
-        projected = jnp.dot(a_ref[...], w_ref[:, columns], preferred_element_type=jnp.float32)
-        for k in range(clips):
-            gate = gate_ref[pl.ds(meta_ref[STEP + k], 1), :]
-            part = gate * projected[k * rows : (k + 1) * rows]
-            out_ref[meta_ref[SLOT + k]] = (token_refs[k][...].astype(jnp.float32) + part).astype(
-                jnp.bfloat16
-            )
-
+                gate = rate_ref[pl.ds(meta_ref[STEP + k], 1), columns]
+                part = gate * projected[k * rows : (k + 1) * rows]
+                total = resid_ref[k, :, columns].astype(jnp.float32) + part
+                held_ref[n, meta_ref[SLOT + k]] = total.astype(jnp.bfloat16)
+            leaving(n, columns).start()
+        for n in range(steps):
+            leaving(n, pl.ds(n * block, block)).wait()
+
+    smem, vmem, anywhere = (
+        pl.BlockSpec(memory_space=space) for space in (pltpu.SMEM, pltpu.VMEM, pl.ANY)
+    )
     return pl.pallas_call(
         kernel,
-        grid_spec=pltpu.PrefetchScalarGridSpec(
-            num_scalar_prefetch=1,
-            grid=(steps,),
-            in_specs=[
-                pl.BlockSpec(memory_space=pltpu.VMEM),
-                pl.BlockSpec(memory_space=pltpu.VMEM),
-                pl.BlockSpec((gate_table.shape[0], block), lambda n, m: (0, n)),
-            ]
-            + [pl.BlockSpec((rows, block), lambda n, m: (0, n))] * clips,
-            out_specs=pl.BlockSpec((clips, rows, block), lambda n, m: (0, 0, n)),
-            scratch_shapes=[pltpu.VMEM((clips * rows, HEADS * HD), jnp.bfloat16)],
-        ),
+        in_specs=[smem, vmem, vmem, anywhere] + [anywhere] * clips,
+        out_specs=anywhere,
         out_shape=pltpu.HBM((clips, rows, width), jnp.bfloat16),
+        scratch_shapes=[
+            pltpu.VMEM((clips * rows, HEADS * HD), jnp.bfloat16),
+            pltpu.VMEM(gate_table.shape, jnp.float32),
+            pltpu.VMEM((clips, rows, width), jnp.bfloat16),
+            pltpu.VMEM((steps, clips, rows, block), jnp.bfloat16),
+            pltpu.SemaphoreType.DMA((clips + 1,)),
+            pltpu.SemaphoreType.DMA((steps,)),
+        ],
         compiler_params=params(24),
         cost_estimate=cost(
             2 * clips * rows * HEADS * HD * width,
@@ -327,7 +349,7 @@
     )(
         meta,
         in_vmem(z),
-        in_vmem(out_weight),
+        in_vmem(weight),
         in_hbm(gate_table),
         *[in_hbm(part) for part in tokens],
     )
@@ -352,7 +374,7 @@
     y = exchange(prep(group, slot_target, jnp.swapaxes(qkv, 1, 2)), ("z", "y", "core"), 2)
     y, weight, *resid = lax.optimization_barrier((y, weight, *resid))
     attended = attention(meta, y, q_gain.reshape(1, HD), k_gain.reshape(1, HD))
-    z = exchange(attended, ("x", "z", "y"), 2)
+    z = exchange(attended, ("z", "y", "x"), 2)
     return project(meta, z, weight, gate_table, resid)
 
 

time: 152 us -> 153 us (level)
  blocking collectives: 35.3 us -> 39.7 us
  Pallas kernels: 39.5 us -> 37.5 us
    all_to_all x1, blocking collectives: 35.3 us -> 39.7 us  [exchange(): lax.all_to_all(sent, axes, split_axis=0, concat_axis=0, tiled=True)]
    pallas_call x1, Pallas kernels: 10.1 us -> 8.46 us  [attention(): pl.pallas_call(kernel, in_specs=[pl.BlockSpec(memory_space=pltpu.SMEM), p...]
    unnamed x28 -> x26, local copies, waits for them, and re-layouts: 5.84 us -> 5.18 us
where the time goes in v4:
time: 153 us; the launch traced here: 151 us
  waiting for transfers between devices  50.6 us (33%)
  blocking collectives  39.7 us (26%)
  Pallas kernels  37.5 us (25%)
  starting transfers between devices  17.9 us (12%)
  local copies, waits for them, and re-layouts  5.18 us (3%)
    all_to_all x1, blocking collectives, exchange(): lax.all_to_all(sent, axes, split_axis=0, concat_axis=0, tiled=True)  39.7 us
    all_to_all x1, waiting for transfers between devices, exchange(): lax.all_to_all(sent, axes, split_axis=0, concat_axis=0, tiled=True)  26.5 us
    ppermute x7, waiting for transfers between devices, across(): return lax.ppermute(part, ('x', 'core'), pairs) if k else part  24.1 us
    pallas_call x1, Pallas kernels, project(): pl.pallas_call(kernel, in_specs=[smem, vmem, vmem, anywhere] + [anywhere]...  10.2 us
    ppermute x7, starting transfers between devices, across(): return lax.ppermute(part, ('x', 'core'), pairs) if k else part  9.39 us
    all_to_all x1, starting transfers between devices, exchange(): lax.all_to_all(sent, axes, split_axis=0, concat_axis=0, tiled=True)  8.54 us
    pallas_call x1, Pallas kernels, attention(): pl.pallas_call(kernel, in_specs=[pl.BlockSpec(memory_space=pltpu.SMEM), p...  8.46 us
    pallas_call x1, Pallas kernels, spread(): pl.pallas_call(spread_kernel, grid_spec=pltpu.PrefetchScalarGridSpec(num_...  6.69 us
  transfers between devices with their start and end apart: 8, of which 5 were waited for; matrix products, arithmetic and copies ran while one was open for 0% of the time, Pallas kernels for 8%

profile of v4, /device:TPU:0, one launch (start us, length us, event | category | flops | bytes accessed | tf_op | source)
XLA Modules:
  0.0 151.1 jit_solution(17106732757972181505)
XLA Ops:
  0.0 6.2 %prep.1 = bf16[16,2,4,3,64,128]{5,4,3,2,1,0:T(8,128)(2,1)} custom-call(s32[1]{0:T(128)} %bitcast.group_ref, s32[64]{0:T(128)} %slot_ref.3, bf16[8,3,64,2048]{3,2,1,0:T(8,128)(2,1)} %bitcast.13), custom_call_target="tpu_custom_call" | custom-call | bytes 12582912 | tf_op jit(solution)/shard_map/prep/pallas_call | solution.py:111
  6.2 8.5 %all-to-all-start = ((bf16[32,4,3,64,128]{4,3,2,1,0:T(8,128)(2,1)}), bf16[32,4,3,64,128]{4,3,2,1,0:T(8,128)(2,1)}, u32[]{:S(2)}, u32[]{:S(2)}) async-start(bf16[32,4,3,64,128]{4,3,2,1,0:T(8,128)(2,1)} %bitcast.12), calls=%async_computation | async-start | bytes 12582912 | tf_op jit(solution)/shard_map/all_to_all | solution.py:369
  14.7 1.4 meta.1.meta_ref
  16.1 0.0 copy-start.2
  16.1 0.6 copy-done.2
  16.8 6.7 %spread.1 = (bf16[64,3072]{1,0:T(8,128)(2,1)}, bf16[64,3072]{1,0:T(8,128)(2,1)}, bf16[64,3072]{1,0:T(8,128)(2,1)}, bf16[64,3072]{1,0:T(8,128)(2,1)}, bf16[64,307...) custom-call(s32[40]{0:T(128)S(1)} %copy-done.2, ...), custom_call_target="tpu_custom_call" | custom-call | bytes 6291456 | tf_op jit(solution)/shard_map/spread/pallas_call | solution.py:137
  23.5 0.2 collective-permute-start
  23.7 1.5 collective-permute-start.1
  25.2 0.2 collective-permute-start.2
  25.3 3.0 %collective-permute-start.3 = (bf16[64,3072]{1,0:T(8,128)(2,1)}, bf16[64,3072]{1,0:T(8,128)(2,1)S(1)}, u32[]{:S(2)}, u32[]{:S(2)}) collective-permute-start(bf16[64,3072]{1,0:T(8,128)(2,1)} %get-tuple-element.27), channel_id=1, source_target_pairs={{0,64},{16,80},{32,96},{48,112},{64,0},{80,16},{96,32},{112,48},{1... | collective-permute-start | bytes 1179656 | tf_op jit(solution)/shard_map/ppermute | solution.py:365
  28.3 0.3 collective-permute-start.4
  28.7 0.0 collective-permute-done.refs_1_
  28.7 0.0 copy-start.6
  28.7 2.8 %collective-permute-start.5 = (bf16[64,3072]{1,0:T(8,128)(2,1)}, bf16[64,3072]{1,0:T(8,128)(2,1)S(1)}, u32[]{:S(2)}, u32[]{:S(2)}) collective-permute-start(bf16[64,3072]{1,0:T(8,128)(2,1)} %get-tuple-element.29), channel_id=1, source_target_pairs={{0,96},{16,112},{32,64},{48,80},{64,32},{80,48},{96,0},{112,16},{1... | collective-permute-start | bytes 1179656 | tf_op jit(solution)/shard_map/ppermute | solution.py:365
  31.4 4.4 %collective-permute-done.1.refs_2_ = bf16[64,3072]{1,0:T(8,128)(2,1)S(1)} collective-permute-done((bf16[64,3072]{1,0:T(8,128)(2,1)}, bf16[64,3072]{1,0:T(8,128)(2,1)S(1)}, u32[]{:S(2)}, u32[]{:S(2)}) %collective-permute-start.1) | collective-permute-done | bytes 393248 | tf_op jit(solution)/shard_map/ppermute | solution.py:365
  35.8 0.0 copy-start.7
  35.8 0.0 copy-start.3
  35.8 0.0 copy-start.4
  35.8 0.0 copy-start.5
  35.8 1.4 collective-permute-start.6
  37.2 4.6 %load.1.w_ref = bf16[2048,3072]{1,0:T(8,128)(2,1)S(1)} custom-call(bf16[2048,3072]{1,0:T(8,128)(2,1)} %from_ref.1), custom_call_target="tpu_custom_call" | custom-call | bytes 25165824 | tf_op jit(solution)/shard_map/load/pallas_call | solution.py:276
  41.8 0.0 copy-done.6
  41.9 0.0 copy-done.7
  41.9 0.0 copy-start
  41.9 4.5 %copy-done = bf16[2048,3072]{1,0:T(8,128)(2,1)} copy-done((bf16[2048,3072]{1,0:T(8,128)(2,1)}, bf16[2048,3072]{1,0:T(8,128)(2,1)S(1)}, u32[]{:S(2)}) %copy-start) | copy-done | bytes 12582936
  46.4 0.0 collective-permute-done.2.refs_3_
  46.4 0.0 copy-start.8
  46.4 8.6 %collective-permute-done.3.refs_4_ = bf16[64,3072]{1,0:T(8,128)(2,1)S(1)} collective-permute-done((bf16[64,3072]{1,0:T(8,128)(2,1)}, bf16[64,3072]{1,0:T(8,128)(2,1)S(1)}, u32[]{:S(2)}, u32[]{:S(2)}) %collective-permute-start.3) | collective-permute-done | bytes 393248 | tf_op jit(solution)/shard_map/ppermute | solution.py:365
  55.0 0.0 copy-start.9
  55.0 7.2 %collective-permute-done.4.refs_5_ = bf16[64,3072]{1,0:T(8,128)(2,1)S(1)} collective-permute-done((bf16[64,3072]{1,0:T(8,128)(2,1)}, bf16[64,3072]{1,0:T(8,128)(2,1)S(1)}, u32[]{:S(2)}, u32[]{:S(2)}) %collective-permute-start.4) | collective-permute-done | bytes 393248 | tf_op jit(solution)/shard_map/ppermute | solution.py:365
  62.2 0.0 copy-start.10
  62.2 0.0 collective-permute-done.5.refs_6_
  62.2 0.0 copy-start.11
  62.2 3.9 %collective-permute-done.6.refs_7_ = bf16[64,3072]{1,0:T(8,128)(2,1)S(1)} collective-permute-done((bf16[64,3072]{1,0:T(8,128)(2,1)}, bf16[64,3072]{1,0:T(8,128)(2,1)S(1)}, u32[]{:S(2)}, u32[]{:S(2)}) %collective-permute-start.6) | collective-permute-done | bytes 393248 | tf_op jit(solution)/shard_map/ppermute | solution.py:365
  66.1 0.0 copy-start.12
  66.1 26.5 %all-to-all-done = bf16[32,4,3,64,128]{4,3,2,1,0:T(8,128)(2,1)} async-done(((bf16[32,4,3,64,128]{4,3,2,1,0:T(8,128)(2,1)}), bf16[32,4,3,64,128]{4,3,2,1,0:T(8,128)(2,1)}, u32[]{:S(2)}, u32[]{:S(2)}) %all-to-all-start) | async-done | bytes 6291488 | tf_op jit(solution)/shard_map/all_to_all | solution.py:369
  92.6 0.0 copy-done.3
  92.6 0.0 copy-done.4
  92.6 0.0 copy-done.5
  92.6 0.0 copy-start.1
  92.6 8.5 %attention.1 = bf16[16,4,2,64,128]{4,3,2,1,0:T(8,128)(2,1)S(1)} custom-call(s32[40]{0:T(128)S(1)} %copy-done.3, bf16[16,2,4,3,64,128]{5,4,3,2,1,0:T(8,128)(2,1)} %bitcast.3.y_ref, f32[1,128]{1,0:T(1,128)S(1)} %bitcast.10, f32[1,128]{1,0:T(1,128)S(1)} %bitcast.11), custom_call_target="tpu_custom_call" | custom-call | flops 4294967296 | bytes 8388608 | tf_op jit(solution)/shard_map/attention/pallas_call | solution.py:247
  101.1 0.0 copy-done.8
  101.1 0.0 copy-done.9
  101.1 0.0 copy-done.10
  101.1 0.0 copy-done.11
  101.1 0.0 copy-done.12
  101.1 39.7 %all_to_all.10 = bf16[64,2,64,128]{3,2,1,0:T(8,128)(2,1)S(1)} all-to-all(bf16[64,2,64,128]{3,2,1,0:T(8,128)(2,1)S(1)} %bitcast.9), channel_id=1, replica_groups=mesh['x'=4,'core'=2,'z'=4,'y'=4] {'z','y','x'}, dimensions={0} | all-to-all | bytes 4194304 | tf_op jit(solution)/shard_map/all_to_all | solution.py:369
  140.8 0.0 copy-done.1
  140.8 10.2 %project.1 = bf16[8,64,3072]{2,1,0:T(8,128)(2,1)} custom-call(s32[40]{0:T(128)S(1)} %copy-done.3, bf16[16,4,2,64,128]{4,3,2,1,0:T(8,128)(2,1)S(1)} %bitcast.8, bf16[2048,3072]{1,0:T(8,128)(2,1)S(1)} %copy-done.1, f32[50,3072]{1,0:T(8,128)} %gate_ref.1, bf16[64,3072]{1,0:T(8,128)(2,1)} %get-tuple-element.33.refs_0_, bf16[64,3072]{1,0:T(8,128)(2,1)} %copy-done.6, ...), custom_call_target="tpu_custom_call" | custom-call | flops 6442450944 | bytes 18874368 | tf_op jit(solution)/shard_map/project/pallas_call | solution.py:330
Async XLA Ops:
  6.2 86.4 %all-to-all-start = ((bf16[32,4,3,64,128]{4,3,2,1,0:T(8,128)(2,1)}), bf16[32,4,3,64,128]{4,3,2,1,0:T(8,128)(2,1)}, u32[]{:S(2)}, u32[]{:S(2)}) async-start(bf16[32,4,3,64,128]{4,3,2,1,0:T(8,128)(2,1)} %bitcast.12), calls=%async_computation | async-start | bytes 12582912 | tf_op jit(solution)/shard_map/all_to_all | solution.py:369
  16.1 0.6 copy-start.2
  23.5 5.2 %collective-permute-start = (bf16[64,3072]{1,0:T(8,128)(2,1)}, bf16[64,3072]{1,0:T(8,128)(2,1)S(1)}, u32[]{:S(2)}, u32[]{:S(2)}) collective-permute-start(bf16[64,3072]{1,0:T(8,128)(2,1)} %get-tuple-element.24), channel_id=1, source_target_pairs={{0,16},{16,0},{32,48},{48,32},{64,80},{80,64},{96,112},{112,96},{1... | collective-permute-start | bytes 1179656 | tf_op jit(solution)/shard_map/ppermute | solution.py:365
  23.7 12.1 %collective-permute-start.1 = (bf16[64,3072]{1,0:T(8,128)(2,1)}, bf16[64,3072]{1,0:T(8,128)(2,1)S(1)}, u32[]{:S(2)}, u32[]{:S(2)}) collective-permute-start(bf16[64,3072]{1,0:T(8,128)(2,1)} %get-tuple-element.25), channel_id=1, source_target_pairs={{0,32},{16,48},{32,0},{48,16},{64,96},{80,112},{96,64},{112,80},{1... | collective-permute-start | bytes 1179656 | tf_op jit(solution)/shard_map/ppermute | solution.py:365
  25.2 21.2 %collective-permute-start.2 = (bf16[64,3072]{1,0:T(8,128)(2,1)}, bf16[64,3072]{1,0:T(8,128)(2,1)S(1)}, u32[]{:S(2)}, u32[]{:S(2)}) collective-permute-start(bf16[64,3072]{1,0:T(8,128)(2,1)} %get-tuple-element.26), channel_id=1, source_target_pairs={{0,48},{16,32},{32,16},{48,0},{64,112},{80,96},{96,80},{112,64},{1... | collective-permute-start | bytes 1179656 | tf_op jit(solution)/shard_map/ppermute | solution.py:365
  25.3 29.6 %collective-permute-start.3 = (bf16[64,3072]{1,0:T(8,128)(2,1)}, bf16[64,3072]{1,0:T(8,128)(2,1)S(1)}, u32[]{:S(2)}, u32[]{:S(2)}) collective-permute-start(bf16[64,3072]{1,0:T(8,128)(2,1)} %get-tuple-element.27), channel_id=1, source_target_pairs={{0,64},{16,80},{32,96},{48,112},{64,0},{80,16},{96,32},{112,48},{1... | collective-permute-start | bytes 1179656 | tf_op jit(solution)/shard_map/ppermute | solution.py:365
  28.3 33.8 %collective-permute-start.4 = (bf16[64,3072]{1,0:T(8,128)(2,1)}, bf16[64,3072]{1,0:T(8,128)(2,1)S(1)}, u32[]{:S(2)}, u32[]{:S(2)}) collective-permute-start(bf16[64,3072]{1,0:T(8,128)(2,1)} %get-tuple-element.28), channel_id=1, source_target_pairs={{0,80},{16,64},{32,112},{48,96},{64,16},{80,0},{96,48},{112,32},{1... | collective-permute-start | bytes 1179656 | tf_op jit(solution)/shard_map/ppermute | solution.py:365
  28.7 13.2 %copy-start.6 = (bf16[64,3072]{1,0:T(8,128)(2,1)}, bf16[64,3072]{1,0:T(8,128)(2,1)S(1)}, u32[]{:S(2)}) copy-start(bf16[64,3072]{1,0:T(8,128)(2,1)S(1)} %collective-permute-done.refs_1_) | copy-start | bytes 1179652
  28.7 33.5 %collective-permute-start.5 = (bf16[64,3072]{1,0:T(8,128)(2,1)}, bf16[64,3072]{1,0:T(8,128)(2,1)S(1)}, u32[]{:S(2)}, u32[]{:S(2)}) collective-permute-start(bf16[64,3072]{1,0:T(8,128)(2,1)} %get-tuple-element.29), channel_id=1, source_target_pairs={{0,96},{16,112},{32,64},{48,80},{64,32},{80,48},{96,0},{112,16},{1... | collective-permute-start | bytes 1179656 | tf_op jit(solution)/shard_map/ppermute | solution.py:365
  35.8 6.0 %copy-start.7 = (bf16[64,3072]{1,0:T(8,128)(2,1)}, bf16[64,3072]{1,0:T(8,128)(2,1)S(1)}, u32[]{:S(2)}) copy-start(bf16[64,3072]{1,0:T(8,128)(2,1)S(1)} %collective-permute-done.1.refs_2_) | copy-start | bytes 1179652
  35.8 56.8 %copy-start.3 = (s32[40]{0:T(128)S(1)}, s32[40]{0:T(128)}, u32[]{:S(2)}) copy-start(s32[40]{0:T(128)} %meta.1.meta_ref) | copy-start | bytes 484
  35.8 56.8 %copy-start.4 = (f32[128]{0:T(128)S(1)}, f32[128]{0:T(128)}, u32[]{:S(2)}) copy-start(f32[128]{0:T(128)} %param.15) | copy-start | bytes 1540
  35.8 56.8 %copy-start.5 = (f32[128]{0:T(128)S(1)}, f32[128]{0:T(128)}, u32[]{:S(2)}) copy-start(f32[128]{0:T(128)} %param.16) | copy-start | bytes 1540
  35.8 30.2 %collective-permute-start.6 = (bf16[64,3072]{1,0:T(8,128)(2,1)}, bf16[64,3072]{1,0:T(8,128)(2,1)S(1)}, u32[]{:S(2)}, u32[]{:S(2)}) collective-permute-start(bf16[64,3072]{1,0:T(8,128)(2,1)} %get-tuple-element.30), channel_id=1, source_target_pairs={{0,112},{16,96},{32,80},{48,64},{64,48},{80,32},{96,16},{112,0},{1... | collective-permute-start | bytes 1179656 | tf_op jit(solution)/shard_map/ppermute | solution.py:365
  41.9 4.5 %copy-start = (bf16[2048,3072]{1,0:T(8,128)(2,1)}, bf16[2048,3072]{1,0:T(8,128)(2,1)S(1)}, u32[]{:S(2)}) copy-start(bf16[2048,3072]{1,0:T(8,128)(2,1)S(1)} %load.1.w_ref) | copy-start | bytes 37748740
  46.4 54.7 %copy-start.8 = (bf16[64,3072]{1,0:T(8,128)(2,1)}, bf16[64,3072]{1,0:T(8,128)(2,1)S(1)}, u32[]{:S(2)}) copy-start(bf16[64,3072]{1,0:T(8,128)(2,1)S(1)} %collective-permute-done.2.refs_3_) | copy-start | bytes 1179652
  55.0 46.1 %copy-start.9 = (bf16[64,3072]{1,0:T(8,128)(2,1)}, bf16[64,3072]{1,0:T(8,128)(2,1)S(1)}, u32[]{:S(2)}) copy-start(bf16[64,3072]{1,0:T(8,128)(2,1)S(1)} %collective-permute-done.3.refs_4_) | copy-start | bytes 1179652
  62.2 39.0 %copy-start.10 = (bf16[64,3072]{1,0:T(8,128)(2,1)}, bf16[64,3072]{1,0:T(8,128)(2,1)S(1)}, u32[]{:S(2)}) copy-start(bf16[64,3072]{1,0:T(8,128)(2,1)S(1)} %collective-permute-done.4.refs_5_) | copy-start | bytes 1179652
  62.2 39.0 %copy-start.11 = (bf16[64,3072]{1,0:T(8,128)(2,1)}, bf16[64,3072]{1,0:T(8,128)(2,1)S(1)}, u32[]{:S(2)}) copy-start(bf16[64,3072]{1,0:T(8,128)(2,1)S(1)} %collective-permute-done.5.refs_6_) | copy-start | bytes 1179652
  66.1 35.1 %copy-start.12 = (bf16[64,3072]{1,0:T(8,128)(2,1)}, bf16[64,3072]{1,0:T(8,128)(2,1)S(1)}, u32[]{:S(2)}) copy-start(bf16[64,3072]{1,0:T(8,128)(2,1)S(1)} %collective-permute-done.6.refs_7_) | copy-start | bytes 1179652
  92.6 48.2 %copy-start.1 = (bf16[2048,3072]{1,0:T(8,128)(2,1)S(1)}, bf16[2048,3072]{1,0:T(8,128)(2,1)}, u32[]{:S(2)}) copy-start(bf16[2048,3072]{1,0:T(8,128)(2,1)} %copy-done) | copy-start | bytes 37748740

commit v5 on v4

--- a/solution.py
+++ b/solution.py
@@ -151,30 +151,30 @@
     )(meta, in_hbm(tokens))
 
 
-def inverse_root(wide):
-    return lax.rsqrt(jnp.mean(wide * wide, axis=-1, keepdims=True) + 1e-06)
-
-
-def attend(n, length, tile, store, gain, root_ref, k_ref, v_ref):
+def rms(part, gain):
+    wide = part.astype(jnp.float32)
+    mean = jnp.mean(wide * wide, axis=-1, keepdims=True)
+    return (wide * lax.rsqrt(mean + 1e-06) * gain).astype(jnp.bfloat16)
+
+
+def ready(length, tile, tiles, q_gain, k_gain, q_ref, k_ref, v_ref):
+    for t in range(tiles):
+        to = slice(t * TILE, (t + 1) * TILE)
+        q_ref[to] = rms(tile(t, 0), q_gain)
+        k_ref[to] = rms(tile(t, 1), k_gain)
+        row = t * TILE + lax.broadcasted_iota(jnp.int32, (TILE, HD), 0)
+        factor = jnp.where(row < length, 1.0, 0.0).astype(jnp.bfloat16)
+        v_ref[to, :HD] = tile(t, 2) * factor
+        v_ref[to, HD:] = factor
+
+
+def attend(n, length, store, q_ref, k_ref, v_ref):
     row = (n - 1) * TILE + lax.broadcasted_iota(jnp.int32, (TILE, HD), 0)
     live = row < length
-    for t in range(n):
-        to = slice(t * TILE, (t + 1) * TILE)
-        root = inverse_root(tile(t, 0).astype(jnp.float32)) * SCALE
-        root_ref[to] = jnp.broadcast_to(root, (TILE, HD))
-        wide = tile(t, 1).astype(jnp.float32)
-        k_ref[to] = (wide * inverse_root(wide) * gain).astype(jnp.bfloat16)
-        if t < n - 1:
-            v_ref[to, :HD] = tile(t, 2)
-            v_ref[to, HD:] = jnp.ones((TILE, HD), jnp.bfloat16)
-        else:
-            factor = jnp.where(live, 1.0, 0.0).astype(jnp.bfloat16)
-            v_ref[to, :HD] = tile(t, 2) * factor
-            v_ref[to, HD:] = factor
 
     def scores_of(t):
         return lax.dot_general(
-            tile(t, 0),
+            q_ref[t * TILE : (t + 1) * TILE],
             k_ref[: n * TILE],
             (((1,), (1,)), ((), ())),
             preferred_element_type=jnp.float32,
@@ -185,14 +185,7 @@
         scores = ahead.pop(0)
         if t + 2 < n:
             ahead.append(scores_of(t + 2))
-        root = root_ref[t * TILE : (t + 1) * TILE]
-        raised = jnp.concatenate(
-            [
-                jnp.exp2(scores[:, i : i + HD] * root).astype(jnp.bfloat16)
-                for i in range(0, n * TILE, HD)
-            ],
-            axis=1,
-        )
+        raised = jnp.exp2(scores * SCALE).astype(jnp.bfloat16)
         summed = jnp.dot(raised, v_ref[: n * TILE], preferred_element_type=jnp.float32)
         result = summed[:, :HD] / summed[:, HD:]
         if t == n - 1:
@@ -208,7 +201,8 @@
     clips = cores * groups
 
     def kernel(meta_ref, y_ref, qg_ref, kg_ref, o_ref, held_ref, sems, *scratch):
-        gain = qg_ref[...] * kg_ref[...]
+        gains = qg_ref[...], kg_ref[...]
+        sets = scratch[:3], scratch[3:]
 
         def arriving(i):
             clip = y_ref.at[:, lax.div(i, groups), lax.rem(i, groups)]
@@ -217,16 +211,21 @@
         for i in range(clips):
             arriving(i).start()
 
-        def one_clip(i, carry):
-            arriving(i).wait()
+        def tile_of(i):
+            def tile(t, part):
+                at = slice(t * per_tile, (t + 1) * per_tile)
+                return held_ref[i, at, part].reshape(TILE, HD)
+
+            return tile
+
+        def make_ready(i, refs):
+            ready(meta_ref[LENGTH + i], tile_of(i), tiles, *gains, *refs)
+
+        def one_clip(i, following, own, other):
             c, x = lax.div(i, groups), lax.rem(i, groups)
             length = meta_ref[LENGTH + i]
             live_tiles = lax.div(length + (TILE - 1), TILE)
 
-            def tile(t, part):
-                at = slice(t * per_tile, (t + 1) * per_tile)
-                return held_ref[i, at, part].reshape(TILE, HD)
-
             def store(t, result):
                 at = slice(t * per_tile, (t + 1) * per_tile)
                 o_ref[at, x, c] = result.reshape(per_tile, rows, HD)
@@ -235,13 +234,27 @@
 
                 @pl.when(live_tiles == n)
                 def _(n=n):
-                    attend(n, length, tile, store, gain, *scratch)
+                    make_ready(following, other)
+                    attend(n, length, store, *own)
                     for t in range(n, tiles):
                         store(t, jnp.zeros((TILE, HD), jnp.bfloat16))
 
+        arriving(0).wait()
+        make_ready(0, sets[0])
+
+        def two_clips(pair, carry):
+            i = 2 * pair
+            arriving(i + 1).wait()
+            one_clip(i, i + 1, *sets)
+
+            @pl.when(i + 2 < clips)
+            def _():
+                arriving(i + 2).wait()
+
+            one_clip(i + 1, jnp.minimum(i + 2, clips - 1), *sets[::-1])
             return carry
 
-        lax.fori_loop(0, clips, one_clip, 0)
+        lax.fori_loop(0, clips // 2, two_clips, 0)
 
     vmem = pl.BlockSpec(memory_space=pltpu.VMEM)
     return pl.pallas_call(
@@ -257,10 +270,13 @@
         scratch_shapes=[
             pltpu.VMEM((clips, blocks, parts, rows, HD), jnp.bfloat16),
             pltpu.SemaphoreType.DMA((clips,)),
-            pltpu.VMEM((total, HD), jnp.float32),
+        ]
+        + [
+            pltpu.VMEM((total, HD), jnp.bfloat16),
             pltpu.VMEM((total, HD), jnp.bfloat16),
             pltpu.VMEM((total, 2 * HD), jnp.bfloat16),
-        ],
+        ]
+        * 2,
         compiler_params=params(24),
         cost_estimate=cost(clips * 4 * total * total * HD, clips * total * HD * 8),
         name="attention",

time: 153 us -> 151 us (0.987); the launches traced: 151 us -> 151 us
  blocking collectives: 39.7 us -> 37.6 us
  Pallas kernels: 37.5 us -> 39.1 us
    all_to_all x1, blocking collectives: 39.7 us -> 37.6 us  [exchange(): lax.all_to_all(sent, axes, split_axis=0, concat_axis=0, tiled=True)]
    pallas_call x1, Pallas kernels: 8.46 us -> 10 us  [attention(): pl.pallas_call(kernel, in_specs=[pl.BlockSpec(memory_space=pltpu.SMEM), p...]
where the time goes in v5:
time: 151 us
  waiting for transfers between devices  50.6 us (34%)
  Pallas kernels  39.1 us (26%)
  blocking collectives  37.6 us (25%)
  starting transfers between devices  17.9 us (12%)
  local copies, waits for them, and re-layouts  5.18 us (3%)
    all_to_all x1, blocking collectives, exchange(): lax.all_to_all(sent, axes, split_axis=0, concat_axis=0, tiled=True)  37.6 us
    all_to_all x1, waiting for transfers between devices, exchange(): lax.all_to_all(sent, axes, split_axis=0, concat_axis=0, tiled=True)  26.5 us
    ppermute x7, waiting for transfers between devices, across(): return lax.ppermute(part, ('x', 'core'), pairs) if k else part  24.1 us
    pallas_call x1, Pallas kernels, project(): pl.pallas_call(kernel, in_specs=[smem, vmem, vmem, anywhere] + [anywhere]...  10.2 us
    pallas_call x1, Pallas kernels, attention(): pl.pallas_call(kernel, in_specs=[pl.BlockSpec(memory_space=pltpu.SMEM), p...  10 us
    ppermute x7, starting transfers between devices, across(): return lax.ppermute(part, ('x', 'core'), pairs) if k else part  9.39 us
    all_to_all x1, starting transfers between devices, exchange(): lax.all_to_all(sent, axes, split_axis=0, concat_axis=0, tiled=True)  8.54 us
    pallas_call x1, Pallas kernels, spread(): pl.pallas_call(spread_kernel, grid_spec=pltpu.PrefetchScalarGridSpec(num_...  6.69 us
  transfers between devices with their start and end apart: 8, of which 5 were waited for; matrix products, arithmetic and copies ran while one was open for 0% of the time, Pallas kernels for 8%

profile of v5, /device:TPU:0, one launch (start us, length us, event | category | flops | bytes accessed | tf_op | source)
XLA Modules:
  0.0 150.7 jit_solution(3534961120362724805)
XLA Ops:
  0.0 6.2 %prep.1 = bf16[16,2,4,3,64,128]{5,4,3,2,1,0:T(8,128)(2,1)} custom-call(s32[1]{0:T(128)} %bitcast.group_ref, s32[64]{0:T(128)} %slot_ref.3, bf16[8,3,64,2048]{3,2,1,0:T(8,128)(2,1)} %bitcast.13), custom_call_target="tpu_custom_call" | custom-call | bytes 12582912 | tf_op jit(solution)/shard_map/prep/pallas_call | solution.py:111
  6.2 8.5 %all-to-all-start = ((bf16[32,4,3,64,128]{4,3,2,1,0:T(8,128)(2,1)}), bf16[32,4,3,64,128]{4,3,2,1,0:T(8,128)(2,1)}, u32[]{:S(2)}, u32[]{:S(2)}) async-start(bf16[32,4,3,64,128]{4,3,2,1,0:T(8,128)(2,1)} %bitcast.12), calls=%async_computation | async-start | bytes 12582912 | tf_op jit(solution)/shard_map/all_to_all | solution.py:385
  14.7 1.4 meta.1.meta_ref
  16.1 0.0 copy-start.2
  16.1 0.6 copy-done.2
  16.8 6.7 %spread.1 = (bf16[64,3072]{1,0:T(8,128)(2,1)}, bf16[64,3072]{1,0:T(8,128)(2,1)}, bf16[64,3072]{1,0:T(8,128)(2,1)}, bf16[64,3072]{1,0:T(8,128)(2,1)}, bf16[64,307...) custom-call(s32[40]{0:T(128)S(1)} %copy-done.2, ...), custom_call_target="tpu_custom_call" | custom-call | bytes 6291456 | tf_op jit(solution)/shard_map/spread/pallas_call | solution.py:137
  23.5 0.2 collective-permute-start
  23.7 1.5 collective-permute-start.1
  25.2 0.2 collective-permute-start.2
  25.3 3.0 %collective-permute-start.3 = (bf16[64,3072]{1,0:T(8,128)(2,1)}, bf16[64,3072]{1,0:T(8,128)(2,1)S(1)}, u32[]{:S(2)}, u32[]{:S(2)}) collective-permute-start(bf16[64,3072]{1,0:T(8,128)(2,1)} %get-tuple-element.27), channel_id=1, source_target_pairs={{0,64},{16,80},{32,96},{48,112},{64,0},{80,16},{96,32},{112,48},{1... | collective-permute-start | bytes 1179656 | tf_op jit(solution)/shard_map/ppermute | solution.py:381
  28.3 0.3 collective-permute-start.4
  28.7 0.0 collective-permute-done.refs_1_
  28.7 0.0 copy-start.6
  28.7 2.8 %collective-permute-start.5 = (bf16[64,3072]{1,0:T(8,128)(2,1)}, bf16[64,3072]{1,0:T(8,128)(2,1)S(1)}, u32[]{:S(2)}, u32[]{:S(2)}) collective-permute-start(bf16[64,3072]{1,0:T(8,128)(2,1)} %get-tuple-element.29), channel_id=1, source_target_pairs={{0,96},{16,112},{32,64},{48,80},{64,32},{80,48},{96,0},{112,16},{1... | collective-permute-start | bytes 1179656 | tf_op jit(solution)/shard_map/ppermute | solution.py:381
  31.4 4.4 %collective-permute-done.1.refs_2_ = bf16[64,3072]{1,0:T(8,128)(2,1)S(1)} collective-permute-done((bf16[64,3072]{1,0:T(8,128)(2,1)}, bf16[64,3072]{1,0:T(8,128)(2,1)S(1)}, u32[]{:S(2)}, u32[]{:S(2)}) %collective-permute-start.1) | collective-permute-done | bytes 393248 | tf_op jit(solution)/shard_map/ppermute | solution.py:381
  35.8 0.0 copy-start.7
  35.8 0.0 copy-start.3
  35.8 0.0 copy-start.4
  35.8 0.0 copy-start.5
  35.8 1.4 collective-permute-start.6
  37.2 4.6 %load.1.w_ref = bf16[2048,3072]{1,0:T(8,128)(2,1)S(1)} custom-call(bf16[2048,3072]{1,0:T(8,128)(2,1)} %from_ref.1), custom_call_target="tpu_custom_call" | custom-call | bytes 25165824 | tf_op jit(solution)/shard_map/load/pallas_call | solution.py:292
  41.8 0.0 copy-done.6
  41.9 0.0 copy-done.7
  41.9 0.0 copy-start
  41.9 4.5 %copy-done = bf16[2048,3072]{1,0:T(8,128)(2,1)} copy-done((bf16[2048,3072]{1,0:T(8,128)(2,1)}, bf16[2048,3072]{1,0:T(8,128)(2,1)S(1)}, u32[]{:S(2)}) %copy-start) | copy-done | bytes 12582936
  46.4 0.0 collective-permute-done.2.refs_3_
  46.4 0.0 copy-start.8
  46.4 8.6 %collective-permute-done.3.refs_4_ = bf16[64,3072]{1,0:T(8,128)(2,1)S(1)} collective-permute-done((bf16[64,3072]{1,0:T(8,128)(2,1)}, bf16[64,3072]{1,0:T(8,128)(2,1)S(1)}, u32[]{:S(2)}, u32[]{:S(2)}) %collective-permute-start.3) | collective-permute-done | bytes 393248 | tf_op jit(solution)/shard_map/ppermute | solution.py:381
  55.0 0.0 copy-start.9
  55.0 7.2 %collective-permute-done.4.refs_5_ = bf16[64,3072]{1,0:T(8,128)(2,1)S(1)} collective-permute-done((bf16[64,3072]{1,0:T(8,128)(2,1)}, bf16[64,3072]{1,0:T(8,128)(2,1)S(1)}, u32[]{:S(2)}, u32[]{:S(2)}) %collective-permute-start.4) | collective-permute-done | bytes 393248 | tf_op jit(solution)/shard_map/ppermute | solution.py:381
  62.2 0.0 copy-start.10
  62.2 0.0 collective-permute-done.5.refs_6_
  62.2 0.0 copy-start.11
  62.2 3.9 %collective-permute-done.6.refs_7_ = bf16[64,3072]{1,0:T(8,128)(2,1)S(1)} collective-permute-done((bf16[64,3072]{1,0:T(8,128)(2,1)}, bf16[64,3072]{1,0:T(8,128)(2,1)S(1)}, u32[]{:S(2)}, u32[]{:S(2)}) %collective-permute-start.6) | collective-permute-done | bytes 393248 | tf_op jit(solution)/shard_map/ppermute | solution.py:381
  66.1 0.0 copy-start.12
  66.1 26.5 %all-to-all-done = bf16[32,4,3,64,128]{4,3,2,1,0:T(8,128)(2,1)} async-done(((bf16[32,4,3,64,128]{4,3,2,1,0:T(8,128)(2,1)}), bf16[32,4,3,64,128]{4,3,2,1,0:T(8,128)(2,1)}, u32[]{:S(2)}, u32[]{:S(2)}) %all-to-all-start) | async-done | bytes 6291488 | tf_op jit(solution)/shard_map/all_to_all | solution.py:385
  92.6 0.0 copy-done.3
  92.6 0.0 copy-done.4
  92.6 0.0 copy-done.5
  92.6 0.0 copy-start.1
  92.6 10.0 %attention.1 = bf16[16,4,2,64,128]{4,3,2,1,0:T(8,128)(2,1)S(1)} custom-call(s32[40]{0:T(128)S(1)} %copy-done.3, bf16[16,2,4,3,64,128]{5,4,3,2,1,0:T(8,128)(2,1)} %bitcast.3.y_ref, f32[1,128]{1,0:T(1,128)S(1)} %bitcast.10, f32[1,128]{1,0:T(1,128)S(1)} %bitcast.11), custom_call_target="tpu_custom_call" | custom-call | flops 4294967296 | bytes 8388608 | tf_op jit(solution)/shard_map/attention/pallas_call | solution.py:260
  102.7 0.0 copy-done.8
  102.7 0.0 copy-done.9
  102.7 0.0 copy-done.10
  102.7 0.0 copy-done.11
  102.7 0.0 copy-done.12
  102.7 37.6 %all_to_all.10 = bf16[64,2,64,128]{3,2,1,0:T(8,128)(2,1)S(1)} all-to-all(bf16[64,2,64,128]{3,2,1,0:T(8,128)(2,1)S(1)} %bitcast.9), channel_id=1, replica_groups=mesh['x'=4,'core'=2,'z'=4,'y'=4] {'z','y','x'}, dimensions={0} | all-to-all | bytes 4194304 | tf_op jit(solution)/shard_map/all_to_all | solution.py:385
  140.4 0.0 copy-done.1
  140.4 10.2 %project.1 = bf16[8,64,3072]{2,1,0:T(8,128)(2,1)} custom-call(s32[40]{0:T(128)S(1)} %copy-done.3, bf16[16,4,2,64,128]{4,3,2,1,0:T(8,128)(2,1)S(1)} %bitcast.8, bf16[2048,3072]{1,0:T(8,128)(2,1)S(1)} %copy-done.1, f32[50,3072]{1,0:T(8,128)} %gate_ref.1, bf16[64,3072]{1,0:T(8,128)(2,1)} %get-tuple-element.33.refs_0_, bf16[64,3072]{1,0:T(8,128)(2,1)} %copy-done.6, ...), custom_call_target="tpu_custom_call" | custom-call | flops 6442450944 | bytes 18874368 | tf_op jit(solution)/shard_map/project/pallas_call | solution.py:346
Async XLA Ops:
  6.2 86.4 %all-to-all-start = ((bf16[32,4,3,64,128]{4,3,2,1,0:T(8,128)(2,1)}), bf16[32,4,3,64,128]{4,3,2,1,0:T(8,128)(2,1)}, u32[]{:S(2)}, u32[]{:S(2)}) async-start(bf16[32,4,3,64,128]{4,3,2,1,0:T(8,128)(2,1)} %bitcast.12), calls=%async_computation | async-start | bytes 12582912 | tf_op jit(solution)/shard_map/all_to_all | solution.py:385
  16.1 0.6 copy-start.2
  23.5 5.2 %collective-permute-start = (bf16[64,3072]{1,0:T(8,128)(2,1)}, bf16[64,3072]{1,0:T(8,128)(2,1)S(1)}, u32[]{:S(2)}, u32[]{:S(2)}) collective-permute-start(bf16[64,3072]{1,0:T(8,128)(2,1)} %get-tuple-element.24), channel_id=1, source_target_pairs={{0,16},{16,0},{32,48},{48,32},{64,80},{80,64},{96,112},{112,96},{1... | collective-permute-start | bytes 1179656 | tf_op jit(solution)/shard_map/ppermute | solution.py:381
  23.7 12.1 %collective-permute-start.1 = (bf16[64,3072]{1,0:T(8,128)(2,1)}, bf16[64,3072]{1,0:T(8,128)(2,1)S(1)}, u32[]{:S(2)}, u32[]{:S(2)}) collective-permute-start(bf16[64,3072]{1,0:T(8,128)(2,1)} %get-tuple-element.25), channel_id=1, source_target_pairs={{0,32},{16,48},{32,0},{48,16},{64,96},{80,112},{96,64},{112,80},{1... | collective-permute-start | bytes 1179656 | tf_op jit(solution)/shard_map/ppermute | solution.py:381
  25.2 21.2 %collective-permute-start.2 = (bf16[64,3072]{1,0:T(8,128)(2,1)}, bf16[64,3072]{1,0:T(8,128)(2,1)S(1)}, u32[]{:S(2)}, u32[]{:S(2)}) collective-permute-start(bf16[64,3072]{1,0:T(8,128)(2,1)} %get-tuple-element.26), channel_id=1, source_target_pairs={{0,48},{16,32},{32,16},{48,0},{64,112},{80,96},{96,80},{112,64},{1... | collective-permute-start | bytes 1179656 | tf_op jit(solution)/shard_map/ppermute | solution.py:381
  25.3 29.6 %collective-permute-start.3 = (bf16[64,3072]{1,0:T(8,128)(2,1)}, bf16[64,3072]{1,0:T(8,128)(2,1)S(1)}, u32[]{:S(2)}, u32[]{:S(2)}) collective-permute-start(bf16[64,3072]{1,0:T(8,128)(2,1)} %get-tuple-element.27), channel_id=1, source_target_pairs={{0,64},{16,80},{32,96},{48,112},{64,0},{80,16},{96,32},{112,48},{1... | collective-permute-start | bytes 1179656 | tf_op jit(solution)/shard_map/ppermute | solution.py:381
  28.3 33.8 %collective-permute-start.4 = (bf16[64,3072]{1,0:T(8,128)(2,1)}, bf16[64,3072]{1,0:T(8,128)(2,1)S(1)}, u32[]{:S(2)}, u32[]{:S(2)}) collective-permute-start(bf16[64,3072]{1,0:T(8,128)(2,1)} %get-tuple-element.28), channel_id=1, source_target_pairs={{0,80},{16,64},{32,112},{48,96},{64,16},{80,0},{96,48},{112,32},{1... | collective-permute-start | bytes 1179656 | tf_op jit(solution)/shard_map/ppermute | solution.py:381
  28.7 13.2 %copy-start.6 = (bf16[64,3072]{1,0:T(8,128)(2,1)}, bf16[64,3072]{1,0:T(8,128)(2,1)S(1)}, u32[]{:S(2)}) copy-start(bf16[64,3072]{1,0:T(8,128)(2,1)S(1)} %collective-permute-done.refs_1_) | copy-start | bytes 1179652
  28.7 33.5 %collective-permute-start.5 = (bf16[64,3072]{1,0:T(8,128)(2,1)}, bf16[64,3072]{1,0:T(8,128)(2,1)S(1)}, u32[]{:S(2)}, u32[]{:S(2)}) collective-permute-start(bf16[64,3072]{1,0:T(8,128)(2,1)} %get-tuple-element.29), channel_id=1, source_target_pairs={{0,96},{16,112},{32,64},{48,80},{64,32},{80,48},{96,0},{112,16},{1... | collective-permute-start | bytes 1179656 | tf_op jit(solution)/shard_map/ppermute | solution.py:381
  35.8 6.0 %copy-start.7 = (bf16[64,3072]{1,0:T(8,128)(2,1)}, bf16[64,3072]{1,0:T(8,128)(2,1)S(1)}, u32[]{:S(2)}) copy-start(bf16[64,3072]{1,0:T(8,128)(2,1)S(1)} %collective-permute-done.1.refs_2_) | copy-start | bytes 1179652
  35.8 56.8 %copy-start.3 = (s32[40]{0:T(128)S(1)}, s32[40]{0:T(128)}, u32[]{:S(2)}) copy-start(s32[40]{0:T(128)} %meta.1.meta_ref) | copy-start | bytes 484
  35.8 56.8 %copy-start.4 = (f32[128]{0:T(128)S(1)}, f32[128]{0:T(128)}, u32[]{:S(2)}) copy-start(f32[128]{0:T(128)} %param.15) | copy-start | bytes 1540
  35.8 56.8 %copy-start.5 = (f32[128]{0:T(128)S(1)}, f32[128]{0:T(128)}, u32[]{:S(2)}) copy-start(f32[128]{0:T(128)} %param.16) | copy-start | bytes 1540
  35.8 30.2 %collective-permute-start.6 = (bf16[64,3072]{1,0:T(8,128)(2,1)}, bf16[64,3072]{1,0:T(8,128)(2,1)S(1)}, u32[]{:S(2)}, u32[]{:S(2)}) collective-permute-start(bf16[64,3072]{1,0:T(8,128)(2,1)} %get-tuple-element.30), channel_id=1, source_target_pairs={{0,112},{16,96},{32,80},{48,64},{64,48},{80,32},{96,16},{112,0},{1... | collective-permute-start | bytes 1179656 | tf_op jit(solution)/shard_map/ppermute | solution.py:381
  41.9 4.5 %copy-start = (bf16[2048,3072]{1,0:T(8,128)(2,1)}, bf16[2048,3072]{1,0:T(8,128)(2,1)S(1)}, u32[]{:S(2)}) copy-start(bf16[2048,3072]{1,0:T(8,128)(2,1)S(1)} %load.1.w_ref) | copy-start | bytes 37748740
  46.4 56.3 %copy-start.8 = (bf16[64,3072]{1,0:T(8,128)(2,1)}, bf16[64,3072]{1,0:T(8,128)(2,1)S(1)}, u32[]{:S(2)}) copy-start(bf16[64,3072]{1,0:T(8,128)(2,1)S(1)} %collective-permute-done.2.refs_3_) | copy-start | bytes 1179652
  55.0 47.7 %copy-start.9 = (bf16[64,3072]{1,0:T(8,128)(2,1)}, bf16[64,3072]{1,0:T(8,128)(2,1)S(1)}, u32[]{:S(2)}) copy-start(bf16[64,3072]{1,0:T(8,128)(2,1)S(1)} %collective-permute-done.3.refs_4_) | copy-start | bytes 1179652
  62.2 40.5 %copy-start.10 = (bf16[64,3072]{1,0:T(8,128)(2,1)}, bf16[64,3072]{1,0:T(8,128)(2,1)S(1)}, u32[]{:S(2)}) copy-start(bf16[64,3072]{1,0:T(8,128)(2,1)S(1)} %collective-permute-done.4.refs_5_) | copy-start | bytes 1179652
  62.2 40.5 %copy-start.11 = (bf16[64,3072]{1,0:T(8,128)(2,1)}, bf16[64,3072]{1,0:T(8,128)(2,1)S(1)}, u32[]{:S(2)}) copy-start(bf16[64,3072]{1,0:T(8,128)(2,1)S(1)} %collective-permute-done.5.refs_6_) | copy-start | bytes 1179652
  66.1 36.6 %copy-start.12 = (bf16[64,3072]{1,0:T(8,128)(2,1)}, bf16[64,3072]{1,0:T(8,128)(2,1)S(1)}, u32[]{:S(2)}) copy-start(bf16[64,3072]{1,0:T(8,128)(2,1)S(1)} %collective-permute-done.6.refs_7_) | copy-start | bytes 1179652
  92.6 47.7 %copy-start.1 = (bf16[2048,3072]{1,0:T(8,128)(2,1)S(1)}, bf16[2048,3072]{1,0:T(8,128)(2,1)}, u32[]{:S(2)}) copy-start(bf16[2048,3072]{1,0:T(8,128)(2,1)} %copy-done) | copy-start | bytes 37748740
